TPU v7x, 256 devices: a whole 4x4x8 slice. The times are simulated.
256 devices in a mesh: tile: 32 (over x, z), pair: 8 (over y, core).
Axes of the slice: x: 4, y: 4, z: 8, core: 2. Of those that a mesh axis runs over, the one named last changes fastest.
Arguments:
- amplitudes: float32 [512, 32768], P('pair', 'tile'), may hold values from -6 to 6
- driver: float32 [512, 32768], P('pair', 'tile'), may hold values from -6 to 6
- integrals: float32 [2048, 128, 128], P('tile'), may hold values from -0.25 to 0.25
- tile_rows: int32 [2048], P('tile'), may hold values from 0 to 255, as said below
- tile_cols: int32 [2048], P('tile'), may hold values from 0 to 255, as said below
- tile_count: int32 [32], P('tile'), may hold values from 16 to 64, as said below
- pair_energy: float32 [512], P('pair'), may hold values from -3 to -0.5
- virt_energy: float32 [32768], P('tile'), may hold values from 0.5 to 4
Outputs:
- new_amps: float32 [512, 32768], P('pair', 'tile')
Inputs may be any that keep to these rules, and one draw needn't show every extreme that they name: The first tile_count[o] slots of owner o are live; at least one owner has all 64 live. `tile_rows`: with tile_cols, names the row tile of each slot; a slot's row and column tiles lie in one symmetry sector; sector s (s = 0 to 7) is the tiles 4*s*s to 4*(s+1)*(s+1)-1; no (row tile, column tile) pair is named by two slots. `tile_cols`: the column tile of each slot, in the sector of its row tile.
All inputs are finite; a program needn't handle non-finite values.
Results may differ from a plain program's by a relative error of at most 0.0003.
Values sent between devices are 32-bit elements; how exact they have to be, the bound alone decides.
No kernel may reach another device: no remote copies, remote signals or barrier semaphores. Data moves between devices by JAX's collectives and lax.ppermute only.
A program may use at most 128 MiB of HBM per device.

v0:
```python
import jax
import jax.numpy as jnp
from jax import lax
from jax.sharding import PartitionSpec as P


def contract(blocks, stored, row_list, col_list, live_count):
    tile_width = stored.shape[1]
    group_size = 8
    slot_total = stored.shape[0]
    rows_here = blocks.shape[0]
    groups = (live_count + group_size - 1) // group_size

    def group_step(group, totals):
        index_list = group * group_size + jnp.arange(group_size, dtype=jnp.int32)
        safe_index = jnp.minimum(index_list, slot_total - 1)
        pieces = jnp.take(stored, safe_index, axis=0)
        row_ids = jnp.take(row_list, safe_index, axis=0)
        col_ids = jnp.take(col_list, safe_index, axis=0)
        active = (index_list < live_count).astype(jnp.float32)
        inputs = jnp.take(blocks, row_ids, axis=1)
        product = jnp.einsum("pgk,gkn->pgn", inputs, pieces, precision=lax.Precision.HIGHEST)
        product = product * active[None, :, None]
        return totals.at[:, col_ids, :].add(product)

    start_totals = jnp.zeros((rows_here, blocks.shape[1], tile_width), jnp.float32)
    return lax.fori_loop(0, groups, group_step, start_totals)


def shards(
    amplitudes, driver, integrals, tile_rows, tile_cols, tile_count, pair_energy, virt_energy
):
    tile_width = integrals.shape[1]
    rows_here = amplitudes.shape[0]
    columns_all = amplitudes.shape[1] * lax.axis_size("tile")
    tiles_total = columns_all // tile_width
    live_count = tile_count[0]
    gathered = lax.all_gather(amplitudes, "tile", axis=1, tiled=True)
    blocks = gathered.reshape(rows_here, tiles_total, tile_width)
    partial_value = contract(blocks, integrals, tile_rows, tile_cols, live_count)
    partial_value = partial_value.reshape(rows_here, columns_all)
    ladder = lax.psum_scatter(partial_value, "tile", scatter_dimension=1, tiled=True)
    denominator = virt_energy[None, :] - pair_energy[:, None]
    return (driver + ladder) / denominator


def solution(mesh):
    return jax.shard_map(
        shards,
        mesh=mesh,
        in_specs=(
            P("pair", "tile"),
            P("pair", "tile"),
            P("tile", None, None),
            P("tile"),
            P("tile"),
            P("tile"),
            P("pair"),
            P("tile"),
        ),
        out_specs=P("pair", "tile"),
        check_vma=False,
    )
```

profile of v0, /device:TPU:6, one launch (start us, length us, event | category | flops | bytes accessed | tf_op | source)
XLA Modules:
  0.0 456.8 jit_solution(8476548188149778402)
XLA Ops:
  6.5 0.0 all-gather.2.cloned.1.call-start
  6.5 0.7 all-gather.2.cloned.1.call-update
  7.3 0.0 reduce-scatter.2.cloned.1.call-start
  8.0 101.4 %all-gather.2.cloned.1.call-done = f32[64,32768]{1,0:T(8,128)} async-done(((f32[64,1024]{1,0:T(8,128)}), f32[64,32768]{1,0:T(8,128)}) %all-gather.2.cloned.1.call-update) | async-done | bytes 8388624 | tf_op jit(solution)/shard_map/all_gather | solution.py:38
  109.3 7.8 %copy_bitcast_fusion.1 = f32[64,256,128]{2,0,1:T(8,128)} fusion(f32[64,32768]{1,0:T(8,128)} %all-gather.2.cloned.1.call-done), kind=kLoop, calls=%fused_computation.28 | loop fusion | bytes 16777216 | tf_op jit(solution)/shard_map/while | solution.py:27
  117.1 0.0 copy-start
  117.1 4.3 broadcast_in_dim.34
  121.5 0.0 copy-done
  121.5 0.0 copy-done.1
  121.5 46.9 %while.10 = (s32[]{:T(128)}, f32[64,256,128]{2,0,1:T(8,128)}, s32[]{:T(128)}, s32[64]{0:T(128)S(1)}, f32[64,128,128]{2,1,0:T(8,128)}, /*index=5*/s32[64]{0:T(128...) while((s32[]{:T(128)}, f32[64,256,128]{2,0,1:T(8,128)}, s32[]{:T(128)}, s32[64]{0:T(128)S(1)}, ...), condition=%wide.region_2.4_spmd, body=%wide.region_0.3_spmd.sunk | while | flops 100994424 | bytes 3420969 | solution.py:27
  121.5 0.7 compare_and_fusion.5
  122.2 0.6 gather_fusion.2
  122.8 0.6 gather_fusion
  123.5 3.9 gather_fusion.3
  127.5 2.8 gather_fusion.1
  130.2 0.7 fusion.19
  130.9 2.3 scatter_fusion
  133.2 0.7 compare_and_fusion.5
  133.9 0.6 gather_fusion.2
  134.5 0.6 gather_fusion
  135.2 3.9 gather_fusion.3
  139.2 2.8 gather_fusion.1
  141.9 0.7 fusion.19
  142.6 2.3 scatter_fusion
  144.9 0.7 compare_and_fusion.5
  145.6 0.6 gather_fusion.2
  146.3 0.6 gather_fusion
  147.0 3.9 gather_fusion.3
  150.9 2.8 gather_fusion.1
  153.7 0.7 fusion.19
  154.4 2.3 scatter_fusion
  156.7 0.7 compare_and_fusion.5
  157.4 0.6 gather_fusion.2
  158.0 0.6 gather_fusion
  158.7 3.9 gather_fusion.3
  162.7 2.8 gather_fusion.1
  165.4 0.7 fusion.19
  166.1 2.3 scatter_fusion
  168.4 7.2 %copy_bitcast_fusion = f32[64,32768]{1,0:T(8,128)} fusion(f32[64,256,128]{2,0,1:T(8,128)} %get-tuple-element.49), kind=kLoop, calls=%fused_computation.27 | loop fusion | bytes 16777216 | tf_op jit(solution)/shard_map/reshape | solution.py:41
  175.5 0.0 copy-start.2
  175.5 0.0 copy-start.3
  175.5 0.0 copy-start.4
  175.5 0.0 reduce-scatter.2.cloned.1.call-update
  175.6 272.6 %reduce-scatter.2.cloned.1.call-done = f32[64,1024]{1,0:T(8,128)} async-done(((f32[64,32768]{1,0:T(8,128)}), f32[64,1024]{1,0:T(8,128)}) %reduce-scatter.2.cloned.1.call-update) | async-done | bytes 262160 | tf_op jit(solution)/shard_map/reduce_scatter | solution.py:42
  448.1 0.0 copy-done.2
  448.1 0.0 copy-done.3
  448.2 0.0 copy-done.4
  448.2 1.8 subtract_divide_fusion
  (29 shorter events, 0.2 us)
Async XLA Ops:
  6.5 102.8 %all-gather.2.cloned.1.call-start = ((), (), s32[]{:S(2)}) async-start(), calls=%async_computation.1 | async-start | bytes 8650752 | tf_op jit(solution)/shard_map/all_gather | solution.py:38
  7.3 440.9 %reduce-scatter.2.cloned.1.call-start = ((), (), s32[]{:S(2)}) async-start(), calls=%async_computation.2 | async-start | bytes 8650752 | tf_op jit(solution)/shard_map/reduce_scatter | solution.py:42
  117.1 4.3 copy-start
  117.1 4.3 copy-start.1
  175.5 272.6 %copy-start.2 = (f32[64,1024]{1,0:T(8,128)S(1)}, f32[64,1024]{1,0:T(8,128)}, u32[]{:S(2)}) copy-start(f32[64,1024]{1,0:T(8,128)} %param.13) | copy-start | bytes 786436
  175.5 272.6 %copy-start.3 = (f32[1024]{0:T(1024)S(1)}, f32[1024]{0:T(1024)}, u32[]{:S(2)}) copy-start(f32[1024]{0:T(1024)} %param.19) | copy-start | bytes 12292
  175.5 272.6 %copy-start.4 = (f32[64]{0:T(128)S(1)}, f32[64]{0:T(128)}, u32[]{:S(2)}) copy-start(f32[64]{0:T(128)} %param.18) | copy-start | bytes 772
Sparse Core Ops, SparseCore 0:
  9.9 99.3 all-gather.1
  175.7 272.4 reduce-scatter.1
where the time goes:
time: 459 us; the launch traced here: 457 us
  waiting for transfers between devices  375 us (82%)
  local copies, waits for them, and re-layouts  51.3 us (11%)
  between operations  14.1 us (3%)
  other arithmetic  13.7 us (3%)
    reduce_scatter x1, waiting for transfers between devices, shards(): lax.psum_scatter(partial_value, 'tile', scatter_dimension=1, tiled=True)  273 us
    all_gather x1, waiting for transfers between devices, shards(): gathered = lax.all_gather(amplitudes, 'tile', axis=1, tiled=True)  101 us
    gather x4, local copies, waits for them, and re-layouts, group_step(): inputs = jnp.take(blocks, row_ids, axis=1)  15.8 us
    gather x4, local copies, waits for them, and re-layouts, group_step(): pieces = jnp.take(stored, safe_index, axis=0)  11.1 us
  transfers between devices with their start and end apart: 2, of which 2 were waited for; matrix products, arithmetic and copies ran while one was open for 0% of the time, Pallas kernels for 0%

commit v1 on v0

--- a/solution.py
+++ b/solution.py
@@ -1,7 +1,37 @@
 import jax
 import jax.numpy as jnp
 from jax import lax
+from jax.experimental import pallas as pl
+from jax.experimental.pallas import tpu as pltpu
 from jax.sharding import PartitionSpec as P
+
+XS = 4
+ZS = 8
+YS = 4
+CAP = 32
+TOTAL_CAP = 80
+GROUP = 4
+EXTRA = 16
+HERE = 64
+PIECE = 16
+WIDTH = 128
+
+Z_GROUPS = [[x * ZS + z for z in range(ZS)] for x in range(XS)]
+
+
+def x_shift(step):
+    return [(x * ZS + z, ((x + step) % XS) * ZS + z) for x in range(XS) for z in range(ZS)]
+
+
+def z_shift(step):
+    return [(x * ZS + z, x * ZS + (z + step) % ZS) for x in range(XS) for z in range(ZS)]
+
+
+def y_shift(step):
+    return [(y * 2 + core, ((y + step) % YS) * 2 + core) for y in range(YS) for core in range(2)]
+
+
+CORE_SWAP = [(y * 2 + core, y * 2 + 1 - core) for y in range(YS) for core in range(2)]
 
 
 def contract(blocks, stored, row_list, col_list, live_count):
@@ -27,21 +57,255 @@
     return lax.fori_loop(0, groups, group_step, start_totals)
 
 
+def dense_ladder(amplitudes, integrals, tile_rows, tile_cols, tile_count):
+    rows_here = amplitudes.shape[0]
+    columns_all = amplitudes.shape[1] * lax.axis_size("tile")
+    gathered = lax.all_gather(amplitudes, "tile", axis=1, tiled=True)
+    blocks = gathered.reshape(rows_here, columns_all // WIDTH, WIDTH)
+    partial_value = contract(blocks, integrals, tile_rows, tile_cols, tile_count[0])
+    partial_value = partial_value.reshape(rows_here, columns_all)
+    return lax.psum_scatter(partial_value, "tile", scatter_dimension=1, tiled=True)
+
+
+def home(row, col):
+    return jnp.minimum(row, col) // HERE
+
+
+def pack_kernel(place, rows, cols, count, stored, *refs):
+    outs, packed = refs[:XS], refs[XS]
+    mine = place[0]
+
+    def step(slot, counts):
+        target = lax.rem(home(rows[slot], cols[slot]) - mine + XS, XS)
+        position = counts[0]
+        for j in range(1, XS):
+            position = jnp.where(target == j, counts[j], position)
+
+        @pl.when(position < CAP)
+        def _():
+            packed[target * CAP + position] = stored[slot]
+
+        return tuple(counts[j] + (target == j).astype(jnp.int32) for j in range(XS))
+
+    lax.fori_loop(0, count[0], step, (jnp.int32(0),) * XS)
+    for j in range(XS):
+        outs[j][...] = packed[j * CAP:(j + 1) * CAP]
+
+
+def pack(place, rows, cols, count, integrals):
+    slots = integrals.shape[0]
+    spec = pltpu.PrefetchScalarGridSpec(
+        num_scalar_prefetch=4,
+        grid=(1,),
+        in_specs=[pl.BlockSpec((slots, PIECE, WIDTH), lambda i, place, *_: (0, place[1], 0))],
+        out_specs=[pl.BlockSpec((CAP, PIECE, WIDTH), lambda i, *_: (0, 0, 0))] * XS,
+        scratch_shapes=[pltpu.VMEM((XS * CAP, PIECE, WIDTH), jnp.float32)],
+    )
+    return pl.pallas_call(
+        pack_kernel,
+        grid_spec=spec,
+        out_shape=[jax.ShapeDtypeStruct((CAP, PIECE, WIDTH), jnp.float32)] * XS,
+        compiler_params=pltpu.CompilerParams(vmem_limit_bytes=16 * 2**20),
+        name="pack",
+    )(place, rows, cols, count, integrals)
+
+
+def plan_kernel(place, *refs):
+    metas, (row_at, col_at, info) = refs[:XS], refs[XS:]
+    mine = place[0]
+    low = mine * HERE
+    total = jnp.int32(0)
+    over = jnp.int32(0)
+    for j in range(XS):
+        meta = metas[j]
+        base = total
+
+        def step(slot, found):
+            row, col = meta[0, slot], meta[1, slot]
+            wanted = home(row, col) == mine
+
+            @pl.when(wanted & (base + found < TOTAL_CAP))
+            def _():
+                row_at[base + found] = row - low
+                col_at[base + found] = col - low
+
+            return found + wanted.astype(jnp.int32)
+
+        found = lax.fori_loop(0, meta[2, 0], step, jnp.int32(0))
+        over = jnp.maximum(over, (found > CAP).astype(jnp.int32))
+        info[j] = jnp.minimum(found, CAP)
+        total = total + found
+    over = jnp.maximum(over, (total > TOTAL_CAP).astype(jnp.int32))
+    info[XS] = jnp.minimum(total, TOTAL_CAP)
+    info[XS + 1] = over
+    for extra in range(GROUP):
+        row_at[info[XS] + extra] = 0
+        col_at[info[XS] + extra] = HERE + EXTRA
+    for rest in range(XS + 2, 8):
+        info[rest] = 0
+
+
+def plan(place, metas):
+    smem = pl.BlockSpec(memory_space=pltpu.SMEM)
+    return pl.pallas_call(
+        plan_kernel,
+        in_specs=[smem] * (1 + XS),
+        out_specs=[smem] * 3,
+        out_shape=[
+            jax.ShapeDtypeStruct((TOTAL_CAP + GROUP,), jnp.int32),
+            jax.ShapeDtypeStruct((TOTAL_CAP + GROUP,), jnp.int32),
+            jax.ShapeDtypeStruct((8,), jnp.int32),
+        ],
+        name="plan",
+    )(place, *metas)
+
+
+def compact_kernel(info, *refs):
+    sources, out = refs[:XS], refs[XS]
+    base = jnp.int32(0)
+    for j in range(XS):
+        source = sources[j]
+
+        def step(item, _):
+            @pl.when(base + item < TOTAL_CAP)
+            def _():
+                out[base + item] = source[item]
+
+            return 0
+
+        lax.fori_loop(0, info[j], step, 0)
+        base = base + info[j]
+
+
+def compact(info, sources):
+    vmem = pl.BlockSpec(memory_space=pltpu.VMEM)
+    return pl.pallas_call(
+        compact_kernel,
+        in_specs=[pl.BlockSpec(memory_space=pltpu.SMEM)] + [vmem] * XS,
+        out_specs=vmem,
+        out_shape=jax.ShapeDtypeStruct((TOTAL_CAP, PIECE, WIDTH), jnp.float32),
+        compiler_params=pltpu.CompilerParams(vmem_limit_bytes=16 * 2**20),
+        name="compact",
+    )(info, *sources)
+
+
+def ladder_kernel(place, row_at, col_at, info, near, extra, *refs):
+    pieces = refs[:2 * YS]
+    out, out_extra, split, tile, sums = refs[2 * YS:]
+    rows_here = near.shape[1]
+    for block in range(ZS + 2):
+        for part in range(ZS):
+            source = near if block < ZS else extra
+            at = block if block < ZS else block - ZS
+            value = source[at, :, part * WIDTH:(part + 1) * WIDTH]
+            high = value.astype(jnp.bfloat16)
+            split[block * ZS + part, :, :WIDTH] = high
+            split[block * ZS + part, :, WIDTH:] = (value - high.astype(jnp.float32)).astype(jnp.bfloat16)
+    sums[...] = jnp.zeros_like(sums)
+    my_y = lax.div(place[1], 2)
+    my_core = lax.rem(place[1], 2)
+    blank = jnp.zeros((WIDTH, WIDTH), jnp.bfloat16)
+
+    def step(group, _):
+        products = []
+        for member in range(GROUP):
+            item = group * GROUP + member
+            safe = jnp.minimum(item, TOTAL_CAP - 1)
+            for shift in range(YS):
+                for swapped in range(2):
+                    core = my_core if swapped == 0 else 1 - my_core
+                    origin = lax.rem(my_y - shift + YS, YS) * 2 + core
+                    at = pl.multiple_of(origin * PIECE, PIECE)
+                    tile[member, pl.ds(at, PIECE), :] = pieces[shift * 2 + swapped][safe]
+            value = tile[member]
+            high = value.astype(jnp.bfloat16)
+            low = (value - high.astype(jnp.float32)).astype(jnp.bfloat16)
+            right = jnp.concatenate(
+                [jnp.concatenate([high, low], axis=1), jnp.concatenate([high, blank], axis=1)], axis=0
+            )
+            product = jnp.dot(split[row_at[item]], right, preferred_element_type=jnp.float32)
+            products.append(product[:, :WIDTH] + product[:, WIDTH:])
+        for member in range(GROUP):
+            item = group * GROUP + member
+            sums[col_at[item]] += products[member]
+        return 0
+
+    groups = lax.div(info[XS] + GROUP - 1, GROUP)
+    lax.fori_loop(0, groups, step, 0)
+    for block in range(ZS):
+        for part in range(ZS):
+            out[block, :, part * WIDTH:(part + 1) * WIDTH] = sums[block * ZS + part]
+    for block in range(2):
+        for part in range(ZS):
+            out_extra[block, :, part * WIDTH:(part + 1) * WIDTH] = sums[HERE + block * ZS + part]
+
+
+def ladder_of(place, row_at, col_at, info, near, extra, pieces):
+    rows_here = near.shape[1]
+    wide = near.shape[2]
+    vmem = pl.BlockSpec(memory_space=pltpu.VMEM)
+    smem = pl.BlockSpec(memory_space=pltpu.SMEM)
+    return pl.pallas_call(
+        ladder_kernel,
+        in_specs=[smem] * 4 + [vmem] * (2 + 2 * YS),
+        out_specs=[vmem, vmem],
+        out_shape=[
+            jax.ShapeDtypeStruct((ZS, rows_here, wide), jnp.float32),
+            jax.ShapeDtypeStruct((2, rows_here, wide), jnp.float32),
+        ],
+        scratch_shapes=[
+            pltpu.VMEM((HERE + EXTRA, rows_here, 2 * WIDTH), jnp.bfloat16),
+            pltpu.VMEM((GROUP, WIDTH, WIDTH), jnp.float32),
+            pltpu.VMEM((HERE + EXTRA + 1, rows_here, WIDTH), jnp.float32),
+        ],
+        compiler_params=pltpu.CompilerParams(vmem_limit_bytes=40 * 2**20),
+        name="ladder",
+    )(place, row_at, col_at, info, near, extra, *pieces)
+
+
 def shards(
     amplitudes, driver, integrals, tile_rows, tile_cols, tile_count, pair_energy, virt_energy
 ):
-    tile_width = integrals.shape[1]
-    rows_here = amplitudes.shape[0]
-    columns_all = amplitudes.shape[1] * lax.axis_size("tile")
-    tiles_total = columns_all // tile_width
-    live_count = tile_count[0]
-    gathered = lax.all_gather(amplitudes, "tile", axis=1, tiled=True)
-    blocks = gathered.reshape(rows_here, tiles_total, tile_width)
-    partial_value = contract(blocks, integrals, tile_rows, tile_cols, live_count)
-    partial_value = partial_value.reshape(rows_here, columns_all)
-    ladder = lax.psum_scatter(partial_value, "tile", scatter_dimension=1, tiled=True)
+    my_tile = lax.axis_index("tile")
+    my_x = my_tile // ZS
+    my_pair = lax.axis_index("pair")
+    place = jnp.stack([my_x, my_pair]).astype(jnp.int32)
+
+    near = lax.all_gather(amplitudes, "tile", axis=0, axis_index_groups=Z_GROUPS)
+    extra = lax.ppermute(near[:2], "tile", x_shift(-1))
+
+    meta = jnp.stack([tile_rows, tile_cols, jnp.broadcast_to(tile_count, tile_rows.shape)])
+    metas = [meta] + [lax.ppermute(meta, "tile", x_shift(step)) for step in range(1, XS)]
+    row_at, col_at, info = plan(place, metas)
+
+    packed = pack(place, tile_rows, tile_cols, tile_count, integrals)
+    moved = [packed[0]] + [lax.ppermute(packed[step], "tile", x_shift(step)) for step in range(1, XS)]
+    mine = compact(info, moved)
+    along_y = [mine] + [lax.ppermute(mine, "pair", y_shift(step)) for step in range(1, YS)]
+    pieces = []
+    for piece in along_y:
+        pieces += [piece, lax.ppermute(piece, "pair", CORE_SWAP)]
+
+    out, out_extra = ladder_of(place, row_at, col_at, info, near, extra, pieces)
+    from_left = lax.ppermute(out_extra, "tile", x_shift(1))
+    from_left = jnp.where(my_x > 0, from_left, 0.0)
+    out = jnp.concatenate([out[:2] + from_left, out[2:]], axis=0)
+    quick = lax.psum_scatter(out, "tile", scatter_dimension=0, axis_index_groups=Z_GROUPS, tiled=True)[0]
+
+    over = info[XS + 1:XS + 2].astype(jnp.float32)
+    for step in (1, 2):
+        over = jnp.maximum(over, lax.ppermute(over, "tile", x_shift(step)))
+    for step in (1, 2, 4):
+        over = jnp.maximum(over, lax.ppermute(over, "tile", z_shift(step)))
+
     denominator = virt_energy[None, :] - pair_energy[:, None]
-    return (driver + ladder) / denominator
+    result = (driver + quick) / denominator
+
+    def slow():
+        ladder = dense_ladder(amplitudes, integrals, tile_rows, tile_cols, tile_count)
+        return (driver + ladder) / denominator
+
+    return lax.cond(over[0] > 0.5, slow, lambda: result)
 
 
 def solution(mesh):

time: 459 us -> 169 us (0.37)
  waiting for transfers between devices: 375 us -> 90.5 us
  local copies, waits for them, and re-layouts: 51.3 us -> 12.8 us
  starting transfers between devices: 0.04 us -> 30.1 us
  Pallas kernels: 0 us -> 13.5 us
  other arithmetic: 13.7 us -> 3.48 us
    reduce_scatter x1, waiting for transfers between devices: 273 us -> 8.9 us  [shards(): lax.psum_scatter(out, 'tile', scatter_dimension=0, axis_index_groups=Z_GR...]
    all_gather x1, waiting for transfers between devices: 101 us -> 0.01 us  [shards(): lax.all_gather(amplitudes, 'tile', axis=0, axis_index_groups=Z_GROUPS)]
    ppermute x0 -> x20, waiting for transfers between devices: none -> 80.8 us  [the longest x3 29.1 us: shards(): lax.ppermute(mine, 'pair', y_shift(step))]
    gather x16 -> x0, local copies, waits for them, and re-layouts: 32 us -> none  [the longest x4 15.8 us: group_step(): inputs = jnp.take(blocks, row_ids, axis=1)]
    ppermute x0 -> x20, starting transfers between devices: none -> 30 us  [the longest x3 9.97 us: shards(): over = jnp.maximum(over, lax.ppermute(over, 'tile', z_shift(step)))]
    pallas_call x0 -> x4, Pallas kernels: none -> 13.5 us  [the longest x1 6.43 us: ladder_of(): pl.pallas_call(ladder_kernel, in_specs=[smem] * 4 + [vmem] * (2 + 2 * YS)...]
    unnamed x10 -> x48, local copies, waits for them, and re-layouts: 0.02 us -> 11 us
    scatter-add x4 -> x0, other arithmetic: 9.13 us -> none  [group_step(): return totals.at[:, col_ids, :].add(product)]
  transfers between devices with their start and end apart: 2 -> 22, of which waited for: 2 -> 12; matrix products, arithmetic and copies ran while one was open for 0% -> 2% of each run, Pallas kernels for 0% -> 4%
where the time goes in v1:
time: 169 us
  waiting for transfers between devices  90.5 us (54%)
  starting transfers between devices  30.1 us (18%)
  between operations  18.3 us (11%)
  Pallas kernels  13.5 us (8%)
  local copies, waits for them, and re-layouts  12.8 us (8%)
  other arithmetic  3.48 us (2%)
    ppermute x3, waiting for transfers between devices, shards(): lax.ppermute(mine, 'pair', y_shift(step))  29.1 us
    ppermute x1, waiting for transfers between devices, shards(): extra = lax.ppermute(near[:2], 'tile', x_shift(-1))  14.5 us
    ppermute x1, waiting for transfers between devices, shards(): from_left = lax.ppermute(out_extra, 'tile', x_shift(1))  13.7 us
    unnamed x48, local copies, waits for them, and re-layouts  11 us
    ppermute x3, waiting for transfers between devices, shards(): over = jnp.maximum(over, lax.ppermute(over, 'tile', z_shift(step)))  10.8 us
    ppermute x3, starting transfers between devices, shards(): over = jnp.maximum(over, lax.ppermute(over, 'tile', z_shift(step)))  9.97 us
    ppermute x3, waiting for transfers between devices, shards(): lax.ppermute(meta, 'tile', x_shift(step))  9.19 us
    reduce_scatter x1, waiting for transfers between devices, shards(): lax.psum_scatter(out, 'tile', scatter_dimension=0, axis_index_groups=Z_GR...  8.9 us
  transfers between devices with their start and end apart: 22, of which 12 were waited for; matrix products, arithmetic and copies ran while one was open for 2% of the time, Pallas kernels for 4%

profile of v1, /device:TPU:6, one launch (start us, length us, event | category | flops | bytes accessed | tf_op | source)
XLA Modules:
  0.0 168.6 jit_solution(14172447404587604714)
XLA Ops:
  6.5 0.7 all-gather.6.cloned.1.call-update
  8.0 2.0 %pack.1 = (f32[32,16,128]{2,1,0:T(8,128)S(1)}, f32[32,16,128]{2,1,0:T(8,128)S(1)}, f32[32,16,128]{2,1,0:T(8,128)S(1)}, f32[32,16,128]{2,1,0:T(8,128)S(1)}) custom-call(s32[2]{0:T(128)S(1)} %pad_add_fusion.place, s32[64]{0:T(128)} %rows.1, s32[64]{0:T(128)} %cols.1, s32[1]{0:T(128)S(6)} %copy.30.count, f32[64,128,128]{2,1,0:T(8,128)} %stored.1), custom_call_target="tpu_custom_call" | custom-call | tf_op jit(solution)/shard_map/pack/pallas_call | solution.py:104
  10.1 2.6 %collective-permute-start.9 = (f32[32,16,128]{2,1,0:T(8,128)S(1)}, f32[32,16,128]{2,1,0:T(8,128)S(1)}, u32[]{:S(2)}, u32[]{:S(2)}) collective-permute-start(f32[32,16,128]{2,1,0:T(8,128)S(1)} %get-tuple-element.99), channel_id=1, source_target_pairs={{0,64},{8,72},{16,80},{24,88},{32,96},{40,104},{48,112},{56,120},{... | collective-permute-start | bytes 786440 | tf_op jit(solution)/shard_map/ppermute | solution.py:282
  12.7 1.4 collective-permute-start.10
  14.3 0.7 add_add_fusion.refs_0_
  15.0 2.1 %collective-permute-start.2 = (s32[3,64]{1,0:T(4,128)S(1)}, s32[3,64]{1,0:T(4,128)S(1)}, u32[]{:S(2)}, u32[]{:S(2)}) collective-permute-start(s32[3,64]{1,0:T(4,128)S(1)} %add_add_fusion.refs_0_), channel_id=1, source_target_pairs={{0,192},{8,200},{16,208},{24,216},{32,224},{40,232},{48,240},{56,2... | collective-permute-start | bytes 2312 | tf_op jit(solution)/shard_map/ppermute | solution.py:278
  17.1 2.6 %collective-permute-start.1 = (s32[3,64]{1,0:T(4,128)S(1)}, s32[3,64]{1,0:T(4,128)S(1)}, u32[]{:S(2)}, u32[]{:S(2)}) collective-permute-start(s32[3,64]{1,0:T(4,128)S(1)} %add_add_fusion.refs_0_), channel_id=1, source_target_pairs={{0,128},{8,136},{16,144},{24,152},{32,160},{40,168},{48,176},{56,1... | collective-permute-start | bytes 2312 | tf_op jit(solution)/shard_map/ppermute | solution.py:278
  19.7 6.2 %collective-permute-done.2.refs_3_ = s32[3,64]{1,0:T(4,128)S(1)} collective-permute-done((s32[3,64]{1,0:T(4,128)S(1)}, s32[3,64]{1,0:T(4,128)S(1)}, u32[]{:S(2)}, u32[]{:S(2)}) %collective-permute-start.2) | collective-permute-done | bytes 800 | tf_op jit(solution)/shard_map/ppermute | solution.py:278
  25.8 0.6 collective-permute-start
  26.4 3.0 %collective-permute-done.refs_1_ = s32[3,64]{1,0:T(4,128)S(1)} collective-permute-done((s32[3,64]{1,0:T(4,128)S(1)}, s32[3,64]{1,0:T(4,128)S(1)}, u32[]{:S(2)}, u32[]{:S(2)}) %collective-permute-start) | collective-permute-done | bytes 800 | tf_op jit(solution)/shard_map/ppermute | solution.py:278
  29.5 0.6 copy-done.24
  30.0 3.9 %plan.1 = (s32[84]{0:T(128)}, s32[84]{0:T(128)}, s32[8]{0:T(128)}) custom-call(s32[2]{0:T(128)} %copy-done.7, s32[3,64]{1,0:T(4,128)} %copy-done.20, s32[3,64]{1,0:T(4,128)} %copy-done.24, s32[3,64]{1,0:T(4,128)} %copy-done.23, s32[3,64]{1,0:T(4,128)} %copy-done.22), custom_call_target="tpu_custom_call" | custom-call | tf_op jit(solution)/shard_map/plan/pallas_call | solution.py:150
  34.6 1.1 compact.1.refs_0_
  35.7 3.2 %collective-permute-start.17 = (f32[80,16,128]{2,1,0:T(8,128)S(1)}, f32[80,16,128]{2,1,0:T(8,128)S(1)}, u32[]{:S(2)}, u32[]{:S(2)}) collective-permute-start(f32[80,16,128]{2,1,0:T(8,128)S(1)} %compact.1.refs_0_), channel_id=1, source_target_pairs={{0,6},{1,7},{2,0},{3,1},{4,2},{5,3},{6,4},{7,5},{8,14},{9,15},{10,... | collective-permute-start | bytes 1966088 | tf_op jit(solution)/shard_map/ppermute | solution.py:284
  38.9 0.6 collective-permute-start.15
  39.5 1.0 collective-permute-start.13
  40.5 25.9 %collective-permute-done.17.refs_6_ = f32[80,16,128]{2,1,0:T(8,128)S(1)} collective-permute-done((f32[80,16,128]{2,1,0:T(8,128)S(1)}, f32[80,16,128]{2,1,0:T(8,128)S(1)}, u32[]{:S(2)}, u32[]{:S(2)}) %collective-permute-start.17) | collective-permute-done | bytes 655392 | tf_op jit(solution)/shard_map/ppermute | solution.py:284
  66.9 3.2 %collective-permute-done.13.refs_2_ = f32[80,16,128]{2,1,0:T(8,128)S(1)} collective-permute-done((f32[80,16,128]{2,1,0:T(8,128)S(1)}, f32[80,16,128]{2,1,0:T(8,128)S(1)}, u32[]{:S(2)}, u32[]{:S(2)}) %collective-permute-start.13) | collective-permute-done | bytes 655392 | tf_op jit(solution)/shard_map/ppermute | solution.py:284
  70.1 0.9 copy-done.3
  70.9 1.1 slice.25
  72.2 0.8 copy-done.5
  73.1 14.5 %collective-permute-done.8.extra = f32[2,64,1024]{2,1,0:T(8,128)S(1)} collective-permute-done((f32[2,64,1024]{2,1,0:T(8,128)S(1)}, f32[2,64,1024]{2,1,0:T(8,128)S(1)}, u32[]{:S(2)}, u32[]{:S(2)}) %collective-permute-start.8) | collective-permute-done | bytes 524320 | tf_op jit(solution)/shard_map/ppermute | solution.py:275
  87.6 1.6 copy-done
  89.2 1.1 copy-done.2
  90.3 1.1 copy-done.4
  91.4 1.1 copy-done.6
  92.5 0.6 copy-done.8
  93.1 0.6 copy-done.10
  93.7 0.7 copy-done.12
  94.3 0.7 copy-done.13
  95.0 6.4 %ladder.1 = (f32[8,64,1024]{2,1,0:T(8,128)S(1)}, f32[2,64,1024]{2,1,0:T(8,128)}) custom-call(s32[2]{0:T(128)S(1)} %copy-done.8, s32[84]{0:T(128)S(1)} %copy-done.12, s32[84]{0:T(128)S(1)} %copy-done.13, s32[8]{0:T(128)S(1)} %copy-done.10, f32[8,64,1024]{2,1,0:T(8,128)S(1)} %bitcast.36, f32[2,64,1024]{2,1,0:T(8,128)S(1)} %collective-permute-done.8.extra, ...), custom_call_target="tpu_custom_call" | custom-call | tf_op jit(solution)/shard_map/ladder/pallas_call | solution.py:248
  101.6 13.7 %collective-permute-done.19 = f32[2,64,1024]{2,1,0:T(8,128)S(1)} collective-permute-done((f32[2,64,1024]{2,1,0:T(8,128)}, f32[2,64,1024]{2,1,0:T(8,128)S(1)}, u32[]{:S(2)}, u32[]{:S(2)}) %collective-permute-start.19) | collective-permute-done | bytes 524320 | tf_op jit(solution)/shard_map/ppermute | solution.py:290
  115.3 1.5 pad_maximum_fusion
  117.0 0.6 slice.12
  118.2 2.9 %collective-permute-start.3 = (f32[1]{0:T(128)}, f32[1]{0:T(128)}, u32[]{:S(2)}, u32[]{:S(2)}) collective-permute-start(f32[1]{0:T(128)} %convert_element_type.16), channel_id=1, source_target_pairs={{0,64},{8,72},{16,80},{24,88},{32,96},{40,104},{48,112},{56,120},{... | collective-permute-start | bytes 20 | tf_op jit(solution)/shard_map/ppermute | solution.py:297
  121.1 0.9 collective-permute-done.3
  122.5 2.3 %collective-permute-start.4 = (f32[1]{0:T(128)}, f32[1]{0:T(128)}, u32[]{:S(2)}, u32[]{:S(2)}) collective-permute-start(f32[1]{0:T(128)} %max.15), channel_id=1, source_target_pairs={{0,128},{8,136},{16,144},{24,152},{32,160},{40,168},{48,176},{56,1... | collective-permute-start | bytes 20 | tf_op jit(solution)/shard_map/ppermute | solution.py:297
  124.8 2.8 %collective-permute-done.4 = f32[1]{0:T(128)} collective-permute-done((f32[1]{0:T(128)}, f32[1]{0:T(128)}, u32[]{:S(2)}, u32[]{:S(2)}) %collective-permute-start.4) | collective-permute-done | bytes 36 | tf_op jit(solution)/shard_map/ppermute | solution.py:297
  128.3 3.8 %collective-permute-start.5 = (f32[1]{0:T(128)}, f32[1]{0:T(128)}, u32[]{:S(2)}, u32[]{:S(2)}) collective-permute-start(f32[1]{0:T(128)} %max.16), channel_id=1, source_target_pairs={{0,8},{8,16},{16,24},{24,32},{32,40},{40,48},{48,56},{56,0},{64,72... | collective-permute-start | bytes 20 | tf_op jit(solution)/shard_map/ppermute | solution.py:299
  132.0 2.9 %collective-permute-done.5 = f32[1]{0:T(128)} collective-permute-done((f32[1]{0:T(128)}, f32[1]{0:T(128)}, u32[]{:S(2)}, u32[]{:S(2)}) %collective-permute-start.5) | collective-permute-done | bytes 36 | tf_op jit(solution)/shard_map/ppermute | solution.py:299
  135.7 1.4 collective-permute-start.6
  137.0 5.2 %collective-permute-done.6 = f32[1]{0:T(128)} collective-permute-done((f32[1]{0:T(128)}, f32[1]{0:T(128)}, u32[]{:S(2)}, u32[]{:S(2)}) %collective-permute-start.6) | collective-permute-done | bytes 36 | tf_op jit(solution)/shard_map/ppermute | solution.py:299
  142.9 4.8 %collective-permute-start.7 = (f32[1]{0:T(128)}, f32[1]{0:T(128)}, u32[]{:S(2)}, u32[]{:S(2)}) collective-permute-start(f32[1]{0:T(128)} %max.18), channel_id=1, source_target_pairs={{0,32},{8,40},{16,48},{24,56},{32,0},{40,8},{48,16},{56,24},{64,96... | collective-permute-start | bytes 20 | tf_op jit(solution)/shard_map/ppermute | solution.py:299
  147.7 2.7 %collective-permute-done.7 = f32[1]{0:T(128)} collective-permute-done((f32[1]{0:T(128)}, f32[1]{0:T(128)}, u32[]{:S(2)}, u32[]{:S(2)}) %collective-permute-start.7) | collective-permute-done | bytes 36 | tf_op jit(solution)/shard_map/ppermute | solution.py:299
  151.1 8.9 %reduce-scatter.5.cloned.1.call-done = f32[1,64,1024]{2,1,0:T(8,128)} async-done(((f32[8,64,1024]{2,1,0:T(8,128)}), f32[1,64,1024]{2,1,0:T(8,128)}) %reduce-scatter.5.cloned.1.call-update) | async-done | bytes 262160 | tf_op jit(solution)/shard_map/reduce_scatter | solution.py:293
  160.0 1.0 conditional.1
  160.0 1.0 fusion
  161.1 0.7 copy-done.19
  (61 shorter events, 1.9 us)
Async XLA Ops:
  6.5 64.4 %all-gather.6.cloned.1.call-start = ((), (), s32[]{:S(2)}) async-start(), calls=%async_computation.5 | async-start | bytes 2359296 | tf_op jit(solution)/shard_map/all_gather | solution.py:274
  7.3 152.7 %reduce-scatter.5.cloned.1.call-start = ((), (), s32[]{:S(2)}) async-start(), calls=%async_computation.4 | async-start | bytes 2359296 | tf_op jit(solution)/shard_map/reduce_scatter | solution.py:293
  8.0 21.4 %copy-start.7 = (s32[2]{0:T(128)}, s32[2]{0:T(128)S(1)}, u32[]{:S(2)}) copy-start(s32[2]{0:T(128)S(1)} %pad_add_fusion.place) | copy-start | bytes 28
  10.1 23.9 %collective-permute-start.9 = (f32[32,16,128]{2,1,0:T(8,128)S(1)}, f32[32,16,128]{2,1,0:T(8,128)S(1)}, u32[]{:S(2)}, u32[]{:S(2)}) collective-permute-start(f32[32,16,128]{2,1,0:T(8,128)S(1)} %get-tuple-element.99), channel_id=1, source_target_pairs={{0,64},{8,72},{16,80},{24,88},{32,96},{40,104},{48,112},{56,120},{... | collective-permute-start | bytes 786440 | tf_op jit(solution)/shard_map/ppermute | solution.py:282
  12.7 21.3 %collective-permute-start.10 = (f32[32,16,128]{2,1,0:T(8,128)S(1)}, f32[32,16,128]{2,1,0:T(8,128)S(1)}, u32[]{:S(2)}, u32[]{:S(2)}) collective-permute-start(f32[32,16,128]{2,1,0:T(8,128)S(1)} %get-tuple-element.100), channel_id=1, source_target_pairs={{0,128},{8,136},{16,144},{24,152},{32,160},{40,168},{48,176},{56,1... | collective-permute-start | bytes 786440 | tf_op jit(solution)/shard_map/ppermute | solution.py:282
  14.1 19.9 %collective-permute-start.11 = (f32[32,16,128]{2,1,0:T(8,128)S(1)}, f32[32,16,128]{2,1,0:T(8,128)S(1)}, u32[]{:S(2)}, u32[]{:S(2)}) collective-permute-start(f32[32,16,128]{2,1,0:T(8,128)S(1)} %get-tuple-element.101), channel_id=1, source_target_pairs={{0,192},{8,200},{16,208},{24,216},{32,224},{40,232},{48,240},{56,2... | collective-permute-start | bytes 786440 | tf_op jit(solution)/shard_map/ppermute | solution.py:282
  15.0 14.4 %copy-start.20 = (s32[3,64]{1,0:T(4,128)}, s32[3,64]{1,0:T(4,128)S(1)}, u32[]{:S(2)}) copy-start(s32[3,64]{1,0:T(4,128)S(1)} %add_add_fusion.refs_0_) | copy-start | bytes 2308
  15.0 10.8 %collective-permute-start.2 = (s32[3,64]{1,0:T(4,128)S(1)}, s32[3,64]{1,0:T(4,128)S(1)}, u32[]{:S(2)}, u32[]{:S(2)}) collective-permute-start(s32[3,64]{1,0:T(4,128)S(1)} %add_add_fusion.refs_0_), channel_id=1, source_target_pairs={{0,192},{8,200},{16,208},{24,216},{32,224},{40,232},{48,240},{56,2... | collective-permute-start | bytes 2312 | tf_op jit(solution)/shard_map/ppermute | solution.py:278
  17.1 9.4 %collective-permute-start.1 = (s32[3,64]{1,0:T(4,128)S(1)}, s32[3,64]{1,0:T(4,128)S(1)}, u32[]{:S(2)}, u32[]{:S(2)}) collective-permute-start(s32[3,64]{1,0:T(4,128)S(1)} %add_add_fusion.refs_0_), channel_id=1, source_target_pairs={{0,128},{8,136},{16,144},{24,152},{32,160},{40,168},{48,176},{56,1... | collective-permute-start | bytes 2312 | tf_op jit(solution)/shard_map/ppermute | solution.py:278
  25.8 3.6 %copy-start.22 = (s32[3,64]{1,0:T(4,128)}, s32[3,64]{1,0:T(4,128)S(1)}, u32[]{:S(2)}) copy-start(s32[3,64]{1,0:T(4,128)S(1)} %collective-permute-done.2.refs_3_) | copy-start | bytes 2308
  25.8 3.6 %collective-permute-start = (s32[3,64]{1,0:T(4,128)S(1)}, s32[3,64]{1,0:T(4,128)S(1)}, u32[]{:S(2)}, u32[]{:S(2)}) collective-permute-start(s32[3,64]{1,0:T(4,128)S(1)} %add_add_fusion.refs_0_), channel_id=1, source_target_pairs={{0,64},{8,72},{16,80},{24,88},{32,96},{40,104},{48,112},{56,120},{... | collective-permute-start | bytes 2312 | tf_op jit(solution)/shard_map/ppermute | solution.py:278
  26.4 3.0 %copy-start.23 = (s32[3,64]{1,0:T(4,128)}, s32[3,64]{1,0:T(4,128)S(1)}, u32[]{:S(2)}) copy-start(s32[3,64]{1,0:T(4,128)S(1)} %collective-permute-done.1.refs_2_) | copy-start | bytes 2308
  29.5 0.6 copy-start.24
  34.0 0.6 copy-start.9
  35.7 30.7 %collective-permute-start.17 = (f32[80,16,128]{2,1,0:T(8,128)S(1)}, f32[80,16,128]{2,1,0:T(8,128)S(1)}, u32[]{:S(2)}, u32[]{:S(2)}) collective-permute-start(f32[80,16,128]{2,1,0:T(8,128)S(1)} %compact.1.refs_0_), channel_id=1, source_target_pairs={{0,6},{1,7},{2,0},{3,1},{4,2},{5,3},{6,4},{7,5},{8,14},{9,15},{10,... | collective-permute-start | bytes 1966088 | tf_op jit(solution)/shard_map/ppermute | solution.py:284
  38.9 27.5 %collective-permute-start.15 = (f32[80,16,128]{2,1,0:T(8,128)S(1)}, f32[80,16,128]{2,1,0:T(8,128)S(1)}, u32[]{:S(2)}, u32[]{:S(2)}) collective-permute-start(f32[80,16,128]{2,1,0:T(8,128)S(1)} %compact.1.refs_0_), channel_id=1, source_target_pairs={{0,4},{1,5},{2,6},{3,7},{4,0},{5,1},{6,2},{7,3},{8,12},{9,13},{10,... | collective-permute-start | bytes 1966088 | tf_op jit(solution)/shard_map/ppermute | solution.py:284
  39.5 30.5 %collective-permute-start.13 = (f32[80,16,128]{2,1,0:T(8,128)S(1)}, f32[80,16,128]{2,1,0:T(8,128)S(1)}, u32[]{:S(2)}, u32[]{:S(2)}) collective-permute-start(f32[80,16,128]{2,1,0:T(8,128)S(1)} %compact.1.refs_0_), channel_id=1, source_target_pairs={{0,2},{1,3},{2,4},{3,5},{4,6},{5,7},{6,0},{7,1},{8,10},{9,11},{10,... | collective-permute-start | bytes 1966088 | tf_op jit(solution)/shard_map/ppermute | solution.py:284
  40.5 31.8 %collective-permute-start.12 = (f32[80,16,128]{2,1,0:T(8,128)S(1)}, f32[80,16,128]{2,1,0:T(8,128)S(1)}, u32[]{:S(2)}, u32[]{:S(2)}) collective-permute-start(f32[80,16,128]{2,1,0:T(8,128)S(1)} %compact.1.refs_0_), channel_id=1, source_target_pairs={{0,1},{1,0},{2,3},{3,2},{4,5},{5,4},{6,7},{7,6},{8,9},{9,8},{10,11... | collective-permute-start | bytes 1966088 | tf_op jit(solution)/shard_map/ppermute | solution.py:287
  66.3 6.8 %collective-permute-start.18 = (f32[80,16,128]{2,1,0:T(8,128)S(1)}, f32[80,16,128]{2,1,0:T(8,128)}, u32[]{:S(2)}, u32[]{:S(2)}) collective-permute-start(f32[80,16,128]{2,1,0:T(8,128)S(1)} %collective-permute-done.17.refs_6_), channel_id=1, source_target_pairs={{0,1},{1,0},{2,3},{3,2},{4,5},{5,4},{6,7},{7,6},{8,9},{9,8},{10,11... | collective-permute-start | bytes 1966088 | tf_op jit(solution)/shard_map/ppermute | solution.py:287
  66.3 21.3 %copy-start.1 = (f32[80,16,128]{2,1,0:T(8,128)}, f32[80,16,128]{2,1,0:T(8,128)S(1)}, u32[]{:S(2)}) copy-start(f32[80,16,128]{2,1,0:T(8,128)S(1)} %collective-permute-done.15.refs_4_) | copy-start | bytes 1966084
  66.3 6.7 %collective-permute-start.16 = (f32[80,16,128]{2,1,0:T(8,128)S(1)}, f32[80,16,128]{2,1,0:T(8,128)}, u32[]{:S(2)}, u32[]{:S(2)}) collective-permute-start(f32[80,16,128]{2,1,0:T(8,128)S(1)} %collective-permute-done.15.refs_4_), channel_id=1, source_target_pairs={{0,1},{1,0},{2,3},{3,2},{4,5},{5,4},{6,7},{7,6},{8,9},{9,8},{10,11... | collective-permute-start | bytes 1966088 | tf_op jit(solution)/shard_map/ppermute | solution.py:287
  70.0 3.1 %collective-permute-start.14 = (f32[80,16,128]{2,1,0:T(8,128)S(1)}, f32[80,16,128]{2,1,0:T(8,128)}, u32[]{:S(2)}, u32[]{:S(2)}) collective-permute-start(f32[80,16,128]{2,1,0:T(8,128)S(1)} %collective-permute-done.13.refs_2_), channel_id=1, source_target_pairs={{0,1},{1,0},{2,3},{3,2},{4,5},{5,4},{6,7},{7,6},{8,9},{9,8},{10,11... | collective-permute-start | bytes 1966088 | tf_op jit(solution)/shard_map/ppermute | solution.py:287
  70.1 0.9 copy-start.3
  72.0 15.6 %collective-permute-start.8 = (f32[2,64,1024]{2,1,0:T(8,128)S(1)}, f32[2,64,1024]{2,1,0:T(8,128)S(1)}, u32[]{:S(2)}, u32[]{:S(2)}) collective-permute-start(f32[2,64,1024]{2,1,0:T(8,128)S(1)} %bitcast.39), channel_id=1, source_target_pairs={{0,192},{8,200},{16,208},{24,216},{32,224},{40,232},{48,240},{56,2... | collective-permute-start | bytes 1572872 | tf_op jit(solution)/shard_map/ppermute | solution.py:275
  72.2 0.8 copy-start.5
  87.6 1.6 copy-start
  89.2 1.1 copy-start.2
  90.3 1.1 copy-start.4
  91.4 1.1 copy-start.6
  92.5 0.6 copy-start.8
  93.1 0.6 copy-start.10
  93.7 0.7 copy-start.12
  94.3 0.7 copy-start.13
  95.0 21.8 %copy-start.21 = (f32[1024]{0:T(1024)S(1)}, f32[1024]{0:T(1024)}, u32[]{:S(2)}) copy-start(f32[1024]{0:T(1024)} %param.21) | copy-start | bytes 12292
  95.0 21.8 %copy-start.25 = (f32[64]{0:T(128)S(1)}, f32[64]{0:T(128)}, u32[]{:S(2)}) copy-start(f32[64]{0:T(128)} %param.20) | copy-start | bytes 772
  95.0 21.9 %copy-start.11 = (s32[8]{0:T(128)S(1)}, s32[8]{0:T(128)}, u32[]{:S(2)}) copy-start(s32[8]{0:T(128)} %get-tuple-element.95.info) | copy-start | bytes 100
  95.0 65.0 %copy-start.14 = (s32[64]{0:T(128)S(1)}, s32[64]{0:T(128)}, u32[]{:S(2)}) copy-start(s32[64]{0:T(128)} %cols.1) | copy-start | bytes 772
  95.0 65.0 %copy-start.15 = (s32[64]{0:T(128)S(1)}, s32[64]{0:T(128)}, u32[]{:S(2)}) copy-start(s32[64]{0:T(128)} %rows.1) | copy-start | bytes 772
  101.5 58.5 %copy-start.16 = (f32[64,1024]{1,0:T(8,128)S(1)}, f32[64,1024]{1,0:T(8,128)}, u32[]{:S(2)}) copy-start(f32[64,1024]{1,0:T(8,128)} %param.15) | copy-start | bytes 786436
  101.5 13.8 %collective-permute-start.19 = (f32[2,64,1024]{2,1,0:T(8,128)}, f32[2,64,1024]{2,1,0:T(8,128)S(1)}, u32[]{:S(2)}, u32[]{:S(2)}) collective-permute-start(f32[2,64,1024]{2,1,0:T(8,128)} %get-tuple-element.103), channel_id=1, source_target_pairs={{0,64},{8,72},{16,80},{24,88},{32,96},{40,104},{48,112},{56,120},{... | collective-permute-start | bytes 1572872 | tf_op jit(solution)/shard_map/ppermute | solution.py:290
  118.2 3.7 %collective-permute-start.3 = (f32[1]{0:T(128)}, f32[1]{0:T(128)}, u32[]{:S(2)}, u32[]{:S(2)}) collective-permute-start(f32[1]{0:T(128)} %convert_element_type.16), channel_id=1, source_target_pairs={{0,64},{8,72},{16,80},{24,88},{32,96},{40,104},{48,112},{56,120},{... | collective-permute-start | bytes 20 | tf_op jit(solution)/shard_map/ppermute | solution.py:297
  122.5 5.1 %collective-permute-start.4 = (f32[1]{0:T(128)}, f32[1]{0:T(128)}, u32[]{:S(2)}, u32[]{:S(2)}) collective-permute-start(f32[1]{0:T(128)} %max.15), channel_id=1, source_target_pairs={{0,128},{8,136},{16,144},{24,152},{32,160},{40,168},{48,176},{56,1... | collective-permute-start | bytes 20 | tf_op jit(solution)/shard_map/ppermute | solution.py:297
  128.3 6.7 %collective-permute-start.5 = (f32[1]{0:T(128)}, f32[1]{0:T(128)}, u32[]{:S(2)}, u32[]{:S(2)}) collective-permute-start(f32[1]{0:T(128)} %max.16), channel_id=1, source_target_pairs={{0,8},{8,16},{16,24},{24,32},{32,40},{40,48},{48,56},{56,0},{64,72... | collective-permute-start | bytes 20 | tf_op jit(solution)/shard_map/ppermute | solution.py:299
  135.7 6.6 %collective-permute-start.6 = (f32[1]{0:T(128)}, f32[1]{0:T(128)}, u32[]{:S(2)}, u32[]{:S(2)}) collective-permute-start(f32[1]{0:T(128)} %max.17), channel_id=1, source_target_pairs={{0,16},{8,24},{16,32},{24,40},{32,48},{40,56},{48,0},{56,8},{64,80... | collective-permute-start | bytes 20 | tf_op jit(solution)/shard_map/ppermute | solution.py:299
  142.9 7.5 %collective-permute-start.7 = (f32[1]{0:T(128)}, f32[1]{0:T(128)}, u32[]{:S(2)}, u32[]{:S(2)}) collective-permute-start(f32[1]{0:T(128)} %max.18), channel_id=1, source_target_pairs={{0,32},{8,40},{16,48},{24,56},{32,0},{40,8},{48,16},{56,24},{64,96... | collective-permute-start | bytes 20 | tf_op jit(solution)/shard_map/ppermute | solution.py:299
  161.0 0.7 copy-start.19
Sparse Core Ops, SparseCore 0:
  9.3 44.2 all-gather.5
  117.0 43.0 reduce-scatter.4

commit v2 on v0

--- a/solution.py
+++ b/solution.py
@@ -1,7 +1,38 @@
 import jax
 import jax.numpy as jnp
 from jax import lax
+from jax.experimental import pallas as pl
+from jax.experimental.pallas import tpu as pltpu
 from jax.sharding import PartitionSpec as P
+
+XS = 4
+ZS = 8
+YS = 4
+CAP = 32
+TOTAL_CAP = 68
+SLOTS = 64
+GROUP = 4
+EXTRA = 16
+HERE = 64
+PIECE = 16
+WIDTH = 128
+
+Z_GROUPS = [[x * ZS + z for z in range(ZS)] for x in range(XS)]
+
+
+def x_shift(step):
+    return [(x * ZS + z, ((x + step) % XS) * ZS + z) for x in range(XS) for z in range(ZS)]
+
+
+def z_shift(step):
+    return [(x * ZS + z, x * ZS + (z + step) % ZS) for x in range(XS) for z in range(ZS)]
+
+
+def y_shift(step):
+    return [(y * 2 + core, ((y + step) % YS) * 2 + core) for y in range(YS) for core in range(2)]
+
+
+CORE_SWAP = [(y * 2 + core, y * 2 + 1 - core) for y in range(YS) for core in range(2)]
 
 
 def contract(blocks, stored, row_list, col_list, live_count):
@@ -27,21 +58,367 @@
     return lax.fori_loop(0, groups, group_step, start_totals)
 
 
+def dense_ladder(amplitudes, integrals, tile_rows, tile_cols, tile_count):
+    rows_here = amplitudes.shape[0]
+    columns_all = amplitudes.shape[1] * lax.axis_size("tile")
+    gathered = lax.all_gather(amplitudes, "tile", axis=1, tiled=True)
+    blocks = gathered.reshape(rows_here, columns_all // WIDTH, WIDTH)
+    partial_value = contract(blocks, integrals, tile_rows, tile_cols, tile_count[0])
+    partial_value = partial_value.reshape(rows_here, columns_all)
+    return lax.psum_scatter(partial_value, "tile", scatter_dimension=1, tiled=True)
+
+
+def home(row, col):
+    return jnp.minimum(row, col) // HERE
+
+
+def pack_kernel(place, rows, cols, count, stored, *refs):
+    outs, own, sizes, packed = refs[:XS - 1], refs[XS - 1], refs[XS], refs[XS + 1]
+    mine = place[0]
+    low = mine * HERE
+    lane = lax.broadcasted_iota(jnp.int32, (PIECE, WIDTH), 1)
+    line = lax.broadcasted_iota(jnp.int32, (PIECE, WIDTH), 0)
+    for j in range(1, XS):
+        packed[j * (CAP + 1) + CAP] = jnp.full((PIECE, WIDTH), -1.0, jnp.float32)
+
+    def step(slot, counts):
+        row, col = rows[slot], cols[slot]
+        target = lax.rem(home(row, col) - mine + XS, XS)
+        outside = (target == 0) & (col - low >= HERE)
+        position = jnp.int32(0)
+        for j in range(1, XS):
+            position = jnp.where(target == j, counts[j], position)
+
+        @pl.when((target > 0) & (position < CAP))
+        def _():
+            packed[target * (CAP + 1) + position] = stored[slot]
+            at = target * (CAP + 1) + CAP
+            entry = jnp.where(line == 0, row, col).astype(jnp.float32)
+            packed[at] = jnp.where((lane == position) & (line < 2), entry, packed[at])
+
+        @pl.when(outside)
+        def _():
+            at = counts[XS]
+            own[0, at] = slot
+            own[1, at] = row - low
+            own[2, at] = col - low
+
+        @pl.when((target == 0) & jnp.logical_not(outside))
+        def _():
+            at = counts[0]
+            own[3, at] = slot
+            own[4, at] = row - low
+            own[5, at] = col - low
+
+        hits = [(target == j).astype(jnp.int32) for j in range(XS)]
+        far = outside.astype(jnp.int32)
+        return (counts[0] + hits[0] - far,) + tuple(counts[j] + hits[j] for j in range(1, XS)) + (counts[XS] + far,)
+
+    counts = lax.fori_loop(0, count[0], step, (jnp.int32(0),) * (XS + 1))
+    most = counts[1]
+    for j in range(2, XS):
+        most = jnp.maximum(most, counts[j])
+    over = (most > CAP).astype(jnp.float32)
+    sizes[0] = counts[XS]
+    sizes[1] = counts[0]
+    sizes[2] = (most > CAP).astype(jnp.int32)
+    for rest in range(3, 8):
+        sizes[rest] = 0
+    for list_at, size in ((0, counts[XS]), (3, counts[0])):
+        for pad in range(GROUP):
+            own[list_at, size + pad] = 0
+            own[list_at + 1, size + pad] = 0
+            own[list_at + 2, size + pad] = HERE + EXTRA
+    for j in range(1, XS):
+        at = j * (CAP + 1) + CAP
+        packed[at] = jnp.where(line == 2, over, packed[at])
+        outs[j - 1][...] = packed[j * (CAP + 1):(j + 1) * (CAP + 1)]
+
+
+def pack(place, rows, cols, count, integrals):
+    slots = integrals.shape[0]
+    spec = pltpu.PrefetchScalarGridSpec(
+        num_scalar_prefetch=4,
+        grid=(1,),
+        in_specs=[pl.BlockSpec((slots, PIECE, WIDTH), lambda i, place, *_: (0, place[1], 0))],
+        out_specs=[pl.BlockSpec((CAP + 1, PIECE, WIDTH), lambda i, *_: (0, 0, 0))] * (XS - 1)
+        + [pl.BlockSpec(memory_space=pltpu.SMEM)] * 2,
+        scratch_shapes=[pltpu.VMEM((XS * (CAP + 1), PIECE, WIDTH), jnp.float32)],
+    )
+    return pl.pallas_call(
+        pack_kernel,
+        grid_spec=spec,
+        out_shape=[jax.ShapeDtypeStruct((CAP + 1, PIECE, WIDTH), jnp.float32)] * (XS - 1)
+        + [jax.ShapeDtypeStruct((6, SLOTS + GROUP), jnp.int32), jax.ShapeDtypeStruct((8,), jnp.int32)],
+        compiler_params=pltpu.CompilerParams(vmem_limit_bytes=8 * 2**20),
+        name="pack",
+    )(place, rows, cols, count, integrals)
+
+
+def compact_kernel(place, sizes, *refs):
+    sources, (out, moved, totals, entries, sems) = refs[:XS - 1], refs[XS - 1:]
+    low = place[0] * HERE
+    copies = [
+        pltpu.make_async_copy(sources[j].at[CAP, pl.ds(0, 8)], entries.at[j], sems.at[j]) for j in range(XS - 1)
+    ]
+    for copy in copies:
+        copy.start()
+    for copy in copies:
+        copy.wait()
+    total = jnp.int32(0)
+    near = jnp.int32(0)
+    far = jnp.int32(0)
+    over = sizes[2] > 0
+    for j in range(XS - 1):
+        source = sources[j]
+        over = over | (entries[j, 2, 0] > 0.5)
+
+        def step(item, carry):
+            total, near, far = carry
+            row = entries[j, 0, item].astype(jnp.int32)
+            col = entries[j, 1, item].astype(jnp.int32)
+            live = row >= 0
+            fits = live & (total < TOTAL_CAP)
+            outside = col - low >= HERE
+
+            @pl.when(fits)
+            def _():
+                out[total] = source[item]
+
+            @pl.when(fits & outside)
+            def _():
+                moved[0, far] = total
+                moved[1, far] = row - low
+                moved[2, far] = col - low
+
+            @pl.when(fits & jnp.logical_not(outside))
+            def _():
+                moved[3, near] = total
+                moved[4, near] = row - low
+                moved[5, near] = col - low
+
+            return (
+                total + live.astype(jnp.int32),
+                near + (fits & jnp.logical_not(outside)).astype(jnp.int32),
+                far + (fits & outside).astype(jnp.int32),
+            )
+
+        total, near, far = lax.fori_loop(0, CAP, step, (total, near, far))
+    over = over | (total > TOTAL_CAP)
+    totals[0] = far
+    totals[1] = near
+    totals[2] = over.astype(jnp.int32)
+    for rest in range(3, 8):
+        totals[rest] = 0
+    for list_at, size in ((0, far), (3, near)):
+        for pad in range(GROUP):
+            moved[list_at, size + pad] = 0
+            moved[list_at + 1, size + pad] = 0
+            moved[list_at + 2, size + pad] = HERE + EXTRA
+
+
+def compact(place, sizes, sources):
+    vmem = pl.BlockSpec(memory_space=pltpu.VMEM)
+    smem = pl.BlockSpec(memory_space=pltpu.SMEM)
+    return pl.pallas_call(
+        compact_kernel,
+        in_specs=[smem] * 2 + [vmem] * (XS - 1),
+        out_specs=[vmem, smem, smem],
+        out_shape=[
+            jax.ShapeDtypeStruct((TOTAL_CAP, PIECE, WIDTH), jnp.float32),
+            jax.ShapeDtypeStruct((6, TOTAL_CAP + GROUP), jnp.int32),
+            jax.ShapeDtypeStruct((8,), jnp.int32),
+        ],
+        scratch_shapes=[pltpu.SMEM((XS - 1, 8, WIDTH), jnp.float32), pltpu.SemaphoreType.DMA((XS - 1,))],
+        compiler_params=pltpu.CompilerParams(vmem_limit_bytes=8 * 2**20),
+        name="compact",
+    )(place, sizes, *sources)
+
+
+def split_of(value):
+    high = value.astype(jnp.bfloat16)
+    return high, (value - high.astype(jnp.float32)).astype(jnp.bfloat16)
+
+
+def products_of(place, lists, list_at, size, fetch, split, sums):
+    blank = jnp.zeros((WIDTH, WIDTH), jnp.bfloat16)
+
+    def step(group, _):
+        products = []
+        for member in range(GROUP):
+            item = group * GROUP + member
+            high, low = split_of(fetch(member, lists[list_at, item]))
+            right = jnp.concatenate(
+                [jnp.concatenate([high, low], axis=1), jnp.concatenate([high, blank], axis=1)], axis=0
+            )
+            product = jnp.dot(split[lists[list_at + 1, item]], right, preferred_element_type=jnp.float32)
+            products.append(product[:, :WIDTH] + product[:, WIDTH:])
+        for member in range(GROUP):
+            sums[lists[list_at + 2, group * GROUP + member]] += products[member]
+        return 0
+
+    lax.fori_loop(0, lax.div(size + GROUP - 1, GROUP), step, 0)
+
+
+def fill_split(split, source, first):
+    for block in range(source.shape[0]):
+        for part in range(ZS):
+            high, low = split_of(source[block, :, part * WIDTH:(part + 1) * WIDTH])
+            split[first + block * ZS + part, :, :WIDTH] = high
+            split[first + block * ZS + part, :, WIDTH:] = low
+
+
+def fetchers(place, stored, pieces, tile):
+    my_y = lax.div(place[1], 2)
+    my_core = lax.rem(place[1], 2)
+
+    def own(member, index):
+        return stored[index]
+
+    def moved(member, index):
+        for shift in range(YS):
+            for swapped in range(2):
+                core = my_core if swapped == 0 else 1 - my_core
+                origin = lax.rem(my_y - shift + YS, YS) * 2 + core
+                at = pl.multiple_of(origin * PIECE, PIECE)
+                tile[member, pl.ds(at, PIECE), :] = pieces[shift * 2 + swapped][index]
+        return tile[member]
+
+    return own, moved
+
+
+def outer_kernel(place, own, sizes, moved, totals, near, stored, *refs):
+    pieces, (out, split, tile, sums) = refs[:2 * YS], refs[2 * YS:]
+
+    @pl.when(sizes[0] + totals[0] > 0)
+    def _():
+        fill_split(split, near, 0)
+
+    sums[...] = jnp.zeros_like(sums)
+    fetch_own, fetch_moved = fetchers(place, stored, pieces, tile)
+    products_of(place, own, 0, sizes[0], fetch_own, split, sums)
+    products_of(place, moved, 0, totals[0], fetch_moved, split, sums)
+    for block in range(2):
+        for part in range(ZS):
+            out[block, :, part * WIDTH:(part + 1) * WIDTH] = sums[HERE + block * ZS + part]
+
+
+def inner_kernel(place, own, sizes, moved, totals, marks, near, extra, stored, *refs):
+    pieces, outs, (split, tile, sums) = refs[:2 * YS], refs[2 * YS:2 * YS + ZS + 1], refs[2 * YS + ZS + 1:]
+    fill_split(split, near, 0)
+    fill_split(split, extra, HERE)
+    sums[...] = jnp.zeros_like(sums)
+    fetch_own, fetch_moved = fetchers(place, stored, pieces, tile)
+    products_of(place, own, 3, sizes[1], fetch_own, split, sums)
+    products_of(place, moved, 3, totals[1], fetch_moved, split, sums)
+    mark = jnp.where(marks[0] > 0.5, jnp.float32(jnp.nan), jnp.float32(0.0))
+    half = near.shape[1] // 2
+    for step in range(ZS):
+        block = lax.rem(place[2] + step, ZS)
+        for part in range(ZS):
+            value = sums[block * ZS + part] + mark
+            lanes = slice(part * WIDTH, (part + 1) * WIDTH)
+            if step == ZS // 2:
+                outs[step][:, lanes] = value[:half]
+                outs[ZS][:, lanes] = value[half:]
+            else:
+                outs[step][:, lanes] = value
+
+
+def scratch_of(rows_here):
+    return [
+        pltpu.VMEM((HERE + EXTRA, rows_here, 2 * WIDTH), jnp.bfloat16),
+        pltpu.VMEM((GROUP, WIDTH, WIDTH), jnp.float32),
+        pltpu.VMEM((HERE + EXTRA + 1, rows_here, WIDTH), jnp.float32),
+    ]
+
+
+def outer_sums(place, own, sizes, moved, totals, near, stored, pieces):
+    _, rows_here, wide = near.shape
+    vmem = pl.BlockSpec(memory_space=pltpu.VMEM)
+    smem = pl.BlockSpec(memory_space=pltpu.SMEM)
+    return pl.pallas_call(
+        outer_kernel,
+        in_specs=[smem] * 5 + [vmem] * (2 + 2 * YS),
+        out_specs=vmem,
+        out_shape=jax.ShapeDtypeStruct((2, rows_here, wide), jnp.float32),
+        scratch_shapes=scratch_of(rows_here),
+        compiler_params=pltpu.CompilerParams(vmem_limit_bytes=12 * 2**20),
+        name="outer",
+    )(place, own, sizes, moved, totals, near, stored, *pieces)
+
+
+def inner_sums(place, own, sizes, moved, totals, marks, near, extra, stored, pieces):
+    _, rows_here, wide = near.shape
+    vmem = pl.BlockSpec(memory_space=pltpu.VMEM)
+    smem = pl.BlockSpec(memory_space=pltpu.SMEM)
+    heights = [rows_here] * (ZS // 2) + [rows_here // 2] + [rows_here] * (ZS // 2 - 1) + [rows_here // 2]
+    return pl.pallas_call(
+        inner_kernel,
+        in_specs=[smem] * 6 + [vmem] * (3 + 2 * YS),
+        out_specs=[vmem] * (ZS + 1),
+        out_shape=[jax.ShapeDtypeStruct((height, wide), jnp.float32) for height in heights],
+        scratch_shapes=scratch_of(rows_here),
+        compiler_params=pltpu.CompilerParams(vmem_limit_bytes=12 * 2**20),
+        name="inner",
+    )(place, own, sizes, moved, totals, marks, near, extra, stored, *pieces)
+
+
+def ring_sum(parts, more):
+    half = ZS // 2
+    rows_here = parts[0].shape[0]
+    middle = more(half)
+    up = lax.ppermute(parts[half] + middle[:rows_here // 2], "tile", z_shift(1))
+    down = lax.ppermute(parts[ZS] + middle[rows_here // 2:], "tile", z_shift(-1))
+    up = jnp.concatenate([up, jnp.zeros_like(up)], axis=0)
+    down = jnp.concatenate([jnp.zeros_like(down), down], axis=0)
+    for step in range(half - 1, 0, -1):
+        up = lax.ppermute(up + parts[step] + more(step), "tile", z_shift(1))
+        down = lax.ppermute(down + parts[ZS - step] + more(ZS - step), "tile", z_shift(-1))
+    return parts[0] + more(0) + up + down
+
+
 def shards(
     amplitudes, driver, integrals, tile_rows, tile_cols, tile_count, pair_energy, virt_energy
 ):
-    tile_width = integrals.shape[1]
-    rows_here = amplitudes.shape[0]
-    columns_all = amplitudes.shape[1] * lax.axis_size("tile")
-    tiles_total = columns_all // tile_width
-    live_count = tile_count[0]
-    gathered = lax.all_gather(amplitudes, "tile", axis=1, tiled=True)
-    blocks = gathered.reshape(rows_here, tiles_total, tile_width)
-    partial_value = contract(blocks, integrals, tile_rows, tile_cols, live_count)
-    partial_value = partial_value.reshape(rows_here, columns_all)
-    ladder = lax.psum_scatter(partial_value, "tile", scatter_dimension=1, tiled=True)
+    my_tile = lax.axis_index("tile")
+    my_x = my_tile // ZS
+    my_z = lax.rem(my_tile, ZS)
+    place = jnp.stack([my_x, lax.axis_index("pair"), my_z]).astype(jnp.int32)
+
+    near = lax.all_gather(amplitudes, "tile", axis=0, axis_index_groups=Z_GROUPS)
+    extra = lax.ppermute(near[:2], "tile", x_shift(-1))
+
+    *packed, own, sizes = pack(place, tile_rows, tile_cols, tile_count, integrals)
+    arrived = [lax.ppermute(packed[step - 1], "tile", x_shift(step)) for step in range(1, XS)]
+    mine, moved, totals = compact(place, sizes, arrived)
+    along_y = [mine] + [lax.ppermute(mine, "pair", y_shift(step)) for step in range(1, YS)]
+    pieces = []
+    for piece in along_y:
+        pieces += [piece, lax.ppermute(piece, "pair", CORE_SWAP)]
+
+    marks = totals[2:3].astype(jnp.float32)
+    for step in (1, 2):
+        marks = jnp.maximum(marks, lax.ppermute(marks, "tile", x_shift(step)))
+
+    beyond = outer_sums(place, own, sizes, moved, totals, near, integrals, pieces)
+    from_left = lax.ppermute(beyond, "tile", x_shift(1))
+    from_left = jnp.where(my_x > 0, from_left, 0.0)
+    parts = inner_sums(place, own, sizes, moved, totals, marks, near, extra, integrals, pieces)
+
+    def more(step):
+        block = lax.rem(my_z + step, ZS)
+        return jnp.where(block == 0, from_left[0], jnp.where(block == 1, from_left[1], 0.0))
+
+    ladder = ring_sum(parts, more)
     denominator = virt_energy[None, :] - pair_energy[:, None]
-    return (driver + ladder) / denominator
+    result = (driver + ladder) / denominator
+
+    def slow():
+        full = dense_ladder(amplitudes, integrals, tile_rows, tile_cols, tile_count)
+        return (driver + full) / denominator
+
+    return lax.cond(jnp.isnan(ladder[0, 0]), slow, lambda: result)
 
 
 def solution(mesh):

time: 459 us -> 186 us (0.41)
  waiting for transfers between devices: 375 us -> 77.1 us
  starting transfers between devices: 0.04 us -> 35.1 us
  local copies, waits for them, and re-layouts: 51.3 us -> 26.7 us
  Pallas kernels: 0 us -> 17.9 us
  other arithmetic: 13.7 us -> 8.25 us
    reduce_scatter x1 -> x0, waiting for transfers between devices: 273 us -> none  [shards(): lax.psum_scatter(partial_value, 'tile', scatter_dimension=1, tiled=True)]
    all_gather x1, waiting for transfers between devices: 101 us -> 0.01 us  [shards(): lax.all_gather(amplitudes, 'tile', axis=0, axis_index_groups=Z_GROUPS)]
    ppermute x0 -> x22, waiting for transfers between devices: none -> 76.4 us  [the longest x3 24.9 us: shards(): lax.ppermute(mine, 'pair', y_shift(step))]
    ppermute x0 -> x22, starting transfers between devices: none -> 35.1 us  [the longest x2 12.3 us: shards(): marks = jnp.maximum(marks, lax.ppermute(marks, 'tile', x_shift(step)))]
    gather x16 -> x0, local copies, waits for them, and re-layouts: 32 us -> none  [the longest x4 15.8 us: group_step(): inputs = jnp.take(blocks, row_ids, axis=1)]
    unnamed x10 -> x68, local copies, waits for them, and re-layouts: 0.02 us -> 24.7 us
    pallas_call x0 -> x4, Pallas kernels: none -> 17.9 us  [the longest x1 6.21 us: inner_sums(): pl.pallas_call(inner_kernel, in_specs=[smem] * 6 + [vmem] * (3 + 2 * YS),...]
    scatter-add x4 -> x0, other arithmetic: 9.13 us -> none  [group_step(): return totals.at[:, col_ids, :].add(product)]
  transfers between devices with their start and end apart: 2 -> 23, of which waited for: 2 -> 14; matrix products, arithmetic and copies ran while one was open for 0% -> 2% of each run, Pallas kernels for 0% -> 5%
where the time goes in v2:
time: 186 us; the launch traced here: 183 us
  waiting for transfers between devices  77.1 us (41%)
  starting transfers between devices  35.1 us (19%)
  local copies, waits for them, and re-layouts  26.7 us (14%)
  Pallas kernels  17.9 us (10%)
  between operations  17.5 us (9%)
  other arithmetic  8.25 us (4%)
    ppermute x3, waiting for transfers between devices, shards(): lax.ppermute(mine, 'pair', y_shift(step))  24.9 us
    unnamed x68, local copies, waits for them, and re-layouts  24.7 us
    ppermute x3, waiting for transfers between devices, ring_sum(): lax.ppermute(down + parts[ZS - step] + more(ZS - step), 'tile', z_shift(-1))  17.2 us
    ppermute x2, starting transfers between devices, shards(): marks = jnp.maximum(marks, lax.ppermute(marks, 'tile', x_shift(step)))  12.3 us
    ppermute x3, waiting for transfers between devices, shards(): lax.ppermute(packed[step - 1], 'tile', x_shift(step))  12.1 us
    ppermute x3, waiting for transfers between devices, ring_sum(): up = lax.ppermute(up + parts[step] + more(step), 'tile', z_shift(1))  9.38 us
    ppermute x1, waiting for transfers between devices, ring_sum(): up = lax.ppermute(parts[half] + middle[:rows_here // 2], 'tile', z_shift(1))  6.92 us
    ppermute x3, starting transfers between devices, ring_sum(): lax.ppermute(down + parts[ZS - step] + more(ZS - step), 'tile', z_shift(-1))  6.54 us
  transfers between devices with their start and end apart: 23, of which 14 were waited for; matrix products, arithmetic and copies ran while one was open for 2% of the time, Pallas kernels for 5%

profile of v2, /device:TPU:6, one launch (start us, length us, event | category | flops | bytes accessed | tf_op | source)
XLA Modules:
  0.0 182.6 jit_solution(5600000894104415426)
XLA Ops:
  8.0 3.9 %pack.1 = (f32[33,16,128]{2,1,0:T(8,128)S(1)}, f32[33,16,128]{2,1,0:T(8,128)S(1)}, f32[33,16,128]{2,1,0:T(8,128)S(1)}, s32[6,68]{1,0:T(8,128)S(1)}, s32[8]{0:T(128)S(1)}) custom-call(s32[3]{0:T(128)S(1)} %pad_add_fusion.place, s32[64]{0:T(128)} %rows.1, s32[64]{0:T(128)} %cols.1, s32[1]{0:T(128)S(6)} %copy.30.count, f32[64,128,128]{2,1,0:T(8,128)} %stored.5), custom_call_target="tpu_custom_call" | custom-call | tf_op jit(solution)/shard_map/pack/pallas_call | solution.py:148
  11.9 2.6 %collective-permute-start = (f32[33,16,128]{2,1,0:T(8,128)S(1)}, f32[33,16,128]{2,1,0:T(8,128)S(1)}, u32[]{:S(2)}, u32[]{:S(2)}) collective-permute-start(f32[33,16,128]{2,1,0:T(8,128)S(1)} %get-tuple-element.104), channel_id=1, source_target_pairs={{0,64},{8,72},{16,80},{24,88},{32,96},{40,104},{48,112},{56,120},{... | collective-permute-start | bytes 811016 | tf_op jit(solution)/shard_map/ppermute | solution.py:393
  15.5 5.8 %collective-permute-done.refs_0_ = f32[33,16,128]{2,1,0:T(8,128)S(1)} collective-permute-done((f32[33,16,128]{2,1,0:T(8,128)S(1)}, f32[33,16,128]{2,1,0:T(8,128)S(1)}, u32[]{:S(2)}, u32[]{:S(2)}) %collective-permute-start) | collective-permute-done | bytes 270368 | tf_op jit(solution)/shard_map/ppermute | solution.py:393
  21.3 3.4 %collective-permute-done.1.refs_1_ = f32[33,16,128]{2,1,0:T(8,128)S(1)} collective-permute-done((f32[33,16,128]{2,1,0:T(8,128)S(1)}, f32[33,16,128]{2,1,0:T(8,128)S(1)}, u32[]{:S(2)}, u32[]{:S(2)}) %collective-permute-start.1) | collective-permute-done | bytes 270368 | tf_op jit(solution)/shard_map/ppermute | solution.py:393
  24.7 2.8 %collective-permute-done.2.refs_2_ = f32[33,16,128]{2,1,0:T(8,128)S(1)} collective-permute-done((f32[33,16,128]{2,1,0:T(8,128)S(1)}, f32[33,16,128]{2,1,0:T(8,128)S(1)}, u32[]{:S(2)}, u32[]{:S(2)}) %collective-permute-start.2) | collective-permute-done | bytes 270368 | tf_op jit(solution)/shard_map/ppermute | solution.py:393
  27.6 4.5 %compact.1 = (f32[68,16,128]{2,1,0:T(8,128)S(1)}, s32[6,72]{1,0:T(8,128)S(1)}, s32[8]{0:T(128)S(1)}) custom-call(s32[3]{0:T(128)S(1)} %pad_add_fusion.place, s32[8]{0:T(128)S(1)} %get-tuple-element.103.sizes, f32[33,16,128]{2,1,0:T(8,128)S(1)} %collective-permute-done.refs_0_, f32[33,16,128]{2,1,0:T(8,128)S(1)} %collective-permute-done.1.refs_1_, ...), custom_call_target="tpu_custom_call" | custom-call | tf_op jit(solution)/shard_map/compact/pallas_call | solution.py:223
  32.1 3.5 %collective-permute-start.11 = (f32[68,16,128]{2,1,0:T(8,128)S(1)}, f32[68,16,128]{2,1,0:T(8,128)S(1)}, u32[]{:S(2)}, u32[]{:S(2)}) collective-permute-start(f32[68,16,128]{2,1,0:T(8,128)S(1)} %get-tuple-element.109.refs_0_), channel_id=1, source_target_pairs={{0,6},{1,7},{2,0},{3,1},{4,2},{5,3},{6,4},{7,5},{8,14},{9,15},{10,... | collective-permute-start | bytes 1671176 | tf_op jit(solution)/shard_map/ppermute | solution.py:395
  37.2 22.5 %collective-permute-done.11.refs_6_ = f32[68,16,128]{2,1,0:T(8,128)S(1)} collective-permute-done((f32[68,16,128]{2,1,0:T(8,128)S(1)}, f32[68,16,128]{2,1,0:T(8,128)S(1)}, u32[]{:S(2)}, u32[]{:S(2)}) %collective-permute-start.11) | collective-permute-done | bytes 557088 | tf_op jit(solution)/shard_map/ppermute | solution.py:395
  61.0 2.4 %collective-permute-done.7.refs_2_ = f32[68,16,128]{2,1,0:T(8,128)S(1)} collective-permute-done((f32[68,16,128]{2,1,0:T(8,128)S(1)}, f32[68,16,128]{2,1,0:T(8,128)S(1)}, u32[]{:S(2)}, u32[]{:S(2)}) %collective-permute-start.7) | collective-permute-done | bytes 557088 | tf_op jit(solution)/shard_map/ppermute | solution.py:395
  67.5 1.6 copy-done
  69.1 1.1 copy-done.3
  70.2 1.1 copy-done.6
  71.2 1.1 copy-done.9
  72.3 1.1 copy-done.12
  73.3 1.1 copy-done.15
  74.4 1.1 copy-done.18
  75.4 3.4 %outer.1 = f32[2,64,1024]{2,1,0:T(8,128)} custom-call(s32[3]{0:T(128)S(1)} %pad_add_fusion.place, s32[6,68]{1,0:T(8,128)S(1)} %get-tuple-element.102.own, s32[8]{0:T(128)S(1)} %get-tuple-element.103.sizes, s32[6,72]{1,0:T(8,128)S(1)} %get-tuple-element.107.moved, s32[8]{0:T(128)S(1)} %get-tuple-element.108.totals, f32[8,64,1024]{2,1,0:T(8,128)S(1)} %bitcast.56, ...), custom_call_target="tpu_custom_call" | custom-call | tf_op jit(solution)/shard_map/outer/pallas_call | solution.py:340
  79.6 2.0 %collective-permute-start.5 = (f32[2,64,1024]{2,1,0:T(8,128)}, f32[2,64,1024]{2,1,0:T(8,128)}, u32[]{:S(2)}, u32[]{:S(2)}) collective-permute-start(f32[2,64,1024]{2,1,0:T(8,128)} %bitcast.8), channel_id=1, source_target_pairs={{0,192},{8,200},{16,208},{24,216},{32,224},{40,232},{48,240},{56,2... | collective-permute-start | bytes 1572872 | tf_op jit(solution)/shard_map/ppermute | solution.py:390
  82.9 8.4 %collective-permute-start.3 = (f32[1]{0:T(128)}, f32[1]{0:T(128)}, u32[]{:S(2)}, u32[]{:S(2)}) collective-permute-start(f32[1]{0:T(128)} %convert_element_type.16), channel_id=1, source_target_pairs={{0,64},{8,72},{16,80},{24,88},{32,96},{40,104},{48,112},{56,120},{... | collective-permute-start | bytes 20 | tf_op jit(solution)/shard_map/ppermute | solution.py:402
  91.3 2.2 %collective-permute-done.3 = f32[1]{0:T(128)} collective-permute-done((f32[1]{0:T(128)}, f32[1]{0:T(128)}, u32[]{:S(2)}, u32[]{:S(2)}) %collective-permute-start.3) | collective-permute-done | bytes 36 | tf_op jit(solution)/shard_map/ppermute | solution.py:402
  94.1 3.9 %collective-permute-start.4 = (f32[1]{0:T(128)}, f32[1]{0:T(128)}, u32[]{:S(2)}, u32[]{:S(2)}) collective-permute-start(f32[1]{0:T(128)} %max.6), channel_id=1, source_target_pairs={{0,128},{8,136},{16,144},{24,152},{32,160},{40,168},{48,176},{56,1... | collective-permute-start | bytes 20 | tf_op jit(solution)/shard_map/ppermute | solution.py:402
  98.0 1.2 collective-permute-done.4
  99.9 1.1 broadcast_select_fusion
  101.8 1.1 copy-done.4
  102.8 1.1 copy-done.7
  103.9 1.1 copy-done.10
  104.9 1.1 copy-done.13
  106.0 1.1 copy-done.16
  107.0 1.1 copy-done.19
  108.1 6.2 %inner.1 = (f32[64,1024]{1,0:T(8,128)S(1)}, f32[64,1024]{1,0:T(8,128)S(1)}, f32[64,1024]{1,0:T(8,128)S(1)}, f32[64,1024]{1,0:T(8,128)S(1)}, f32[32,1024]{1,0:T(8...) custom-call(s32[3]{0:T(128)S(1)} %pad_add_fusion.place, ...), custom_call_target="tpu_custom_call" | custom-call | tf_op jit(solution)/shard_map/inner/pallas_call | solution.py:356
  118.5 1.6 collective-permute-start.14
  120.2 6.9 %collective-permute-done.14 = f32[32,1024]{1,0:T(8,128)S(1)} collective-permute-done((f32[32,1024]{1,0:T(8,128)S(1)}, f32[32,1024]{1,0:T(8,128)S(1)}, u32[]{:S(2)}, u32[]{:S(2)}) %collective-permute-start.14) | collective-permute-done | bytes 131104 | tf_op jit(solution)/shard_map/ppermute | solution.py:371
  127.1 1.2 bitcast_add_fusion.5
  128.3 7.6 %collective-permute-done.15 = f32[64,1024]{1,0:T(8,128)S(1)} collective-permute-done((f32[64,1024]{1,0:T(8,128)S(1)}, f32[64,1024]{1,0:T(8,128)S(1)}, u32[]{:S(2)}, u32[]{:S(2)}) %collective-permute-start.15) | collective-permute-done | bytes 262176 | tf_op jit(solution)/shard_map/ppermute | solution.py:376
  135.9 1.2 bitcast_add_fusion.4
  137.2 3.2 %collective-permute-start.18 = (f32[32,1024]{1,0:T(8,128)S(1)}, f32[32,1024]{1,0:T(8,128)S(1)}, u32[]{:S(2)}, u32[]{:S(2)}) collective-permute-start(f32[32,1024]{1,0:T(8,128)S(1)} %get-tuple-element.151), channel_id=1, source_target_pairs={{0,56},{8,0},{16,8},{24,16},{32,24},{40,32},{48,40},{56,48},{64,12... | collective-permute-start | bytes 393224 | tf_op jit(solution)/shard_map/ppermute | solution.py:372
  140.4 2.5 %collective-permute-done.18 = f32[32,1024]{1,0:T(8,128)S(1)} collective-permute-done((f32[32,1024]{1,0:T(8,128)S(1)}, f32[32,1024]{1,0:T(8,128)S(1)}, u32[]{:S(2)}, u32[]{:S(2)}) %collective-permute-start.18) | collective-permute-done | bytes 131104 | tf_op jit(solution)/shard_map/ppermute | solution.py:372
  142.9 1.8 collective-permute-done.16
  144.7 1.2 bitcast_add_fusion.3
  145.9 1.9 %collective-permute-start.19 = (f32[64,1024]{1,0:T(8,128)S(1)}, f32[64,1024]{1,0:T(8,128)S(1)}, u32[]{:S(2)}, u32[]{:S(2)}) collective-permute-start(f32[64,1024]{1,0:T(8,128)S(1)} %get-tuple-element.149), channel_id=1, source_target_pairs={{0,56},{8,0},{16,8},{24,16},{32,24},{40,32},{48,40},{56,48},{64,12... | collective-permute-start | bytes 786440 | tf_op jit(solution)/shard_map/ppermute | solution.py:377
  147.9 6.3 %collective-permute-done.19 = f32[64,1024]{1,0:T(8,128)S(1)} collective-permute-done((f32[64,1024]{1,0:T(8,128)S(1)}, f32[64,1024]{1,0:T(8,128)S(1)}, u32[]{:S(2)}, u32[]{:S(2)}) %collective-permute-start.19) | collective-permute-done | bytes 262176 | tf_op jit(solution)/shard_map/ppermute | solution.py:377
  154.1 1.2 bitcast_add_fusion.1
  155.3 2.1 %collective-permute-start.20 = (f32[64,1024]{1,0:T(8,128)S(1)}, f32[64,1024]{1,0:T(8,128)S(1)}, u32[]{:S(2)}, u32[]{:S(2)}) collective-permute-start(f32[64,1024]{1,0:T(8,128)S(1)} %bitcast_add_fusion.1), channel_id=1, source_target_pairs={{0,56},{8,0},{16,8},{24,16},{32,24},{40,32},{48,40},{56,48},{64,12... | collective-permute-start | bytes 786440 | tf_op jit(solution)/shard_map/ppermute | solution.py:377
  157.4 7.1 %collective-permute-done.20 = f32[64,1024]{1,0:T(8,128)S(1)} collective-permute-done((f32[64,1024]{1,0:T(8,128)S(1)}, f32[64,1024]{1,0:T(8,128)S(1)}, u32[]{:S(2)}, u32[]{:S(2)}) %collective-permute-start.20) | collective-permute-done | bytes 262176 | tf_op jit(solution)/shard_map/ppermute | solution.py:377
  164.5 1.2 bitcast_add_fusion
  165.7 2.5 %collective-permute-start.21 = (f32[64,1024]{1,0:T(8,128)S(1)}, f32[64,1024]{1,0:T(8,128)S(1)}, u32[]{:S(2)}, u32[]{:S(2)}) collective-permute-start(f32[64,1024]{1,0:T(8,128)S(1)} %bitcast_add_fusion), channel_id=1, source_target_pairs={{0,56},{8,0},{16,8},{24,16},{32,24},{40,32},{48,40},{56,48},{64,12... | collective-permute-start | bytes 786440 | tf_op jit(solution)/shard_map/ppermute | solution.py:377
  168.3 3.8 %collective-permute-done.21 = f32[64,1024]{1,0:T(8,128)S(1)} collective-permute-done((f32[64,1024]{1,0:T(8,128)S(1)}, f32[64,1024]{1,0:T(8,128)S(1)}, u32[]{:S(2)}, u32[]{:S(2)}) %collective-permute-start.21) | collective-permute-done | bytes 262176 | tf_op jit(solution)/shard_map/ppermute | solution.py:377
  174.0 1.0 conditional.1
  (87 shorter events, 17.8 us)
Async XLA Ops:
  6.5 61.0 %all-gather.6.cloned.1.call-start = ((), (), s32[]{:S(2)}) async-start(), calls=%async_computation.3 | async-start | bytes 2359296 | tf_op jit(solution)/shard_map/all_gather | solution.py:389
  11.9 9.4 %collective-permute-start = (f32[33,16,128]{2,1,0:T(8,128)S(1)}, f32[33,16,128]{2,1,0:T(8,128)S(1)}, u32[]{:S(2)}, u32[]{:S(2)}) collective-permute-start(f32[33,16,128]{2,1,0:T(8,128)S(1)} %get-tuple-element.104), channel_id=1, source_target_pairs={{0,64},{8,72},{16,80},{24,88},{32,96},{40,104},{48,112},{56,120},{... | collective-permute-start | bytes 811016 | tf_op jit(solution)/shard_map/ppermute | solution.py:393
  14.5 10.2 %collective-permute-start.1 = (f32[33,16,128]{2,1,0:T(8,128)S(1)}, f32[33,16,128]{2,1,0:T(8,128)S(1)}, u32[]{:S(2)}, u32[]{:S(2)}) collective-permute-start(f32[33,16,128]{2,1,0:T(8,128)S(1)} %get-tuple-element.105), channel_id=1, source_target_pairs={{0,128},{8,136},{16,144},{24,152},{32,160},{40,168},{48,176},{56,1... | collective-permute-start | bytes 811016 | tf_op jit(solution)/shard_map/ppermute | solution.py:393
  14.5 13.0 %collective-permute-start.2 = (f32[33,16,128]{2,1,0:T(8,128)S(1)}, f32[33,16,128]{2,1,0:T(8,128)S(1)}, u32[]{:S(2)}, u32[]{:S(2)}) collective-permute-start(f32[33,16,128]{2,1,0:T(8,128)S(1)} %get-tuple-element.106), channel_id=1, source_target_pairs={{0,192},{8,200},{16,208},{24,216},{32,224},{40,232},{48,240},{56,2... | collective-permute-start | bytes 811016 | tf_op jit(solution)/shard_map/ppermute | solution.py:393
  32.1 27.6 %collective-permute-start.11 = (f32[68,16,128]{2,1,0:T(8,128)S(1)}, f32[68,16,128]{2,1,0:T(8,128)S(1)}, u32[]{:S(2)}, u32[]{:S(2)}) collective-permute-start(f32[68,16,128]{2,1,0:T(8,128)S(1)} %get-tuple-element.109.refs_0_), channel_id=1, source_target_pairs={{0,6},{1,7},{2,0},{3,1},{4,2},{5,3},{6,4},{7,5},{8,14},{9,15},{10,... | collective-permute-start | bytes 1671176 | tf_op jit(solution)/shard_map/ppermute | solution.py:395
  35.6 24.1 %collective-permute-start.9 = (f32[68,16,128]{2,1,0:T(8,128)S(1)}, f32[68,16,128]{2,1,0:T(8,128)S(1)}, u32[]{:S(2)}, u32[]{:S(2)}) collective-permute-start(f32[68,16,128]{2,1,0:T(8,128)S(1)} %get-tuple-element.109.refs_0_), channel_id=1, source_target_pairs={{0,4},{1,5},{2,6},{3,7},{4,0},{5,1},{6,2},{7,3},{8,12},{9,13},{10,... | collective-permute-start | bytes 1671176 | tf_op jit(solution)/shard_map/ppermute | solution.py:395
  36.2 27.2 %collective-permute-start.7 = (f32[68,16,128]{2,1,0:T(8,128)S(1)}, f32[68,16,128]{2,1,0:T(8,128)S(1)}, u32[]{:S(2)}, u32[]{:S(2)}) collective-permute-start(f32[68,16,128]{2,1,0:T(8,128)S(1)} %get-tuple-element.109.refs_0_), channel_id=1, source_target_pairs={{0,2},{1,3},{2,4},{3,5},{4,6},{5,7},{6,0},{7,1},{8,10},{9,11},{10,... | collective-permute-start | bytes 1671176 | tf_op jit(solution)/shard_map/ppermute | solution.py:395
  37.2 27.0 %collective-permute-start.6 = (f32[68,16,128]{2,1,0:T(8,128)S(1)}, f32[68,16,128]{2,1,0:T(8,128)S(1)}, u32[]{:S(2)}, u32[]{:S(2)}) collective-permute-start(f32[68,16,128]{2,1,0:T(8,128)S(1)} %get-tuple-element.109.refs_0_), channel_id=1, source_target_pairs={{0,1},{1,0},{2,3},{3,2},{4,5},{5,4},{6,7},{7,6},{8,9},{9,8},{10,11... | collective-permute-start | bytes 1671176 | tf_op jit(solution)/shard_map/ppermute | solution.py:398
  59.7 5.3 %collective-permute-start.12 = (f32[68,16,128]{2,1,0:T(8,128)S(1)}, f32[68,16,128]{2,1,0:T(8,128)S(1)}, u32[]{:S(2)}, u32[]{:S(2)}) collective-permute-start(f32[68,16,128]{2,1,0:T(8,128)S(1)} %collective-permute-done.11.refs_6_), channel_id=1, source_target_pairs={{0,1},{1,0},{2,3},{3,2},{4,5},{5,4},{6,7},{7,6},{8,9},{9,8},{10,11... | collective-permute-start | bytes 1671176 | tf_op jit(solution)/shard_map/ppermute | solution.py:398
  59.7 6.2 %collective-permute-start.10 = (f32[68,16,128]{2,1,0:T(8,128)S(1)}, f32[68,16,128]{2,1,0:T(8,128)S(1)}, u32[]{:S(2)}, u32[]{:S(2)}) collective-permute-start(f32[68,16,128]{2,1,0:T(8,128)S(1)} %collective-permute-done.9.refs_4_), channel_id=1, source_target_pairs={{0,1},{1,0},{2,3},{3,2},{4,5},{5,4},{6,7},{7,6},{8,9},{9,8},{10,11... | collective-permute-start | bytes 1671176 | tf_op jit(solution)/shard_map/ppermute | solution.py:398
  60.2 0.8 copy-start.2
  63.4 3.3 %collective-permute-start.8 = (f32[68,16,128]{2,1,0:T(8,128)S(1)}, f32[68,16,128]{2,1,0:T(8,128)S(1)}, u32[]{:S(2)}, u32[]{:S(2)}) collective-permute-start(f32[68,16,128]{2,1,0:T(8,128)S(1)} %collective-permute-done.7.refs_2_), channel_id=1, source_target_pairs={{0,1},{1,0},{2,3},{3,2},{4,5},{5,4},{6,7},{7,6},{8,9},{9,8},{10,11... | collective-permute-start | bytes 1671176 | tf_op jit(solution)/shard_map/ppermute | solution.py:398
  63.4 0.8 copy-start.5
  64.2 0.8 copy-start.8
  65.0 0.8 copy-start.11
  65.9 0.8 copy-start.14
  67.5 1.6 copy-start
  69.1 1.1 copy-start.3
  70.2 1.1 copy-start.6
  71.2 1.1 copy-start.9
  72.3 1.1 copy-start.12
  73.3 1.1 copy-start.15
  74.4 1.1 copy-start.18
  75.4 26.3 %copy-start.1 = (f32[512,1024]{1,0:T(8,128)S(1)}, f32[512,1024]{1,0:T(8,128)}, u32[]{:S(2)}) copy-start(f32[512,1024]{1,0:T(8,128)} %all-gather.6.cloned.1.call-done) | copy-start | bytes 6291460
  78.8 21.0 %collective-permute-start.13 = (f32[2,64,1024]{2,1,0:T(8,128)}, f32[2,64,1024]{2,1,0:T(8,128)}, u32[]{:S(2)}, u32[]{:S(2)}) collective-permute-start(f32[2,64,1024]{2,1,0:T(8,128)} %outer.1), channel_id=1, source_target_pairs={{0,64},{8,72},{16,80},{24,88},{32,96},{40,104},{48,112},{56,120},{... | collective-permute-start | bytes 1572872 | tf_op jit(solution)/shard_map/ppermute | solution.py:405
  79.6 22.1 %collective-permute-start.5 = (f32[2,64,1024]{2,1,0:T(8,128)}, f32[2,64,1024]{2,1,0:T(8,128)}, u32[]{:S(2)}, u32[]{:S(2)}) collective-permute-start(f32[2,64,1024]{2,1,0:T(8,128)} %bitcast.8), channel_id=1, source_target_pairs={{0,192},{8,200},{16,208},{24,216},{32,224},{40,232},{48,240},{56,2... | collective-permute-start | bytes 1572872 | tf_op jit(solution)/shard_map/ppermute | solution.py:390
  82.9 10.5 %collective-permute-start.3 = (f32[1]{0:T(128)}, f32[1]{0:T(128)}, u32[]{:S(2)}, u32[]{:S(2)}) collective-permute-start(f32[1]{0:T(128)} %convert_element_type.16), channel_id=1, source_target_pairs={{0,64},{8,72},{16,80},{24,88},{32,96},{40,104},{48,112},{56,120},{... | collective-permute-start | bytes 20 | tf_op jit(solution)/shard_map/ppermute | solution.py:402
  94.1 5.1 %collective-permute-start.4 = (f32[1]{0:T(128)}, f32[1]{0:T(128)}, u32[]{:S(2)}, u32[]{:S(2)}) collective-permute-start(f32[1]{0:T(128)} %max.6), channel_id=1, source_target_pairs={{0,128},{8,136},{16,144},{24,152},{32,160},{40,168},{48,176},{56,1... | collective-permute-start | bytes 20 | tf_op jit(solution)/shard_map/ppermute | solution.py:402
  101.8 1.1 copy-start.4
  102.8 1.1 copy-start.7
  103.9 1.1 copy-start.10
  104.9 1.1 copy-start.13
  106.0 1.1 copy-start.16
  107.0 1.1 copy-start.19
  108.1 60.1 %copy-start.33 = (f32[1024]{0:T(1024)S(1)}, f32[1024]{0:T(1024)}, u32[]{:S(2)}) copy-start(f32[1024]{0:T(1024)} %param.21) | copy-start | bytes 12292
  108.1 60.1 %copy-start.34 = (f32[64]{0:T(128)S(1)}, f32[64]{0:T(128)}, u32[]{:S(2)}) copy-start(f32[64]{0:T(128)} %param.20) | copy-start | bytes 772
  108.1 65.9 %copy-start.27 = (s32[64]{0:T(128)S(1)}, s32[64]{0:T(128)}, u32[]{:S(2)}) copy-start(s32[64]{0:T(128)} %rows.1) | copy-start | bytes 772
  108.1 65.9 %copy-start.28 = (s32[64]{0:T(128)S(1)}, s32[64]{0:T(128)}, u32[]{:S(2)}) copy-start(s32[64]{0:T(128)} %cols.1) | copy-start | bytes 772
  118.5 53.6 %copy-start.30 = (f32[2,64,1024]{2,1,0:T(8,128)S(1)}, f32[2,64,1024]{2,1,0:T(8,128)}, u32[]{:S(2)}) copy-start(f32[2,64,1024]{2,1,0:T(8,128)} %copy-done.29) | copy-start | bytes 1572868
  118.5 53.6 %copy-start.22 = (f32[64,1024]{1,0:T(8,128)S(1)}, f32[64,1024]{1,0:T(8,128)}, u32[]{:S(2)}) copy-start(f32[64,1024]{1,0:T(8,128)} %copy-done.21) | copy-start | bytes 786436
  118.5 8.6 %collective-permute-start.14 = (f32[32,1024]{1,0:T(8,128)S(1)}, f32[32,1024]{1,0:T(8,128)S(1)}, u32[]{:S(2)}, u32[]{:S(2)}) collective-permute-start(f32[32,1024]{1,0:T(8,128)S(1)} %get-tuple-element.150), channel_id=1, source_target_pairs={{0,8},{8,16},{16,24},{24,32},{32,40},{40,48},{48,56},{56,0},{64,72... | collective-permute-start | bytes 393224 | tf_op jit(solution)/shard_map/ppermute | solution.py:371
  128.2 7.7 %collective-permute-start.15 = (f32[64,1024]{1,0:T(8,128)S(1)}, f32[64,1024]{1,0:T(8,128)S(1)}, u32[]{:S(2)}, u32[]{:S(2)}) collective-permute-start(f32[64,1024]{1,0:T(8,128)S(1)} %bitcast_add_fusion.5), channel_id=1, source_target_pairs={{0,8},{8,16},{16,24},{24,32},{32,40},{40,48},{48,56},{56,0},{64,72... | collective-permute-start | bytes 786440 | tf_op jit(solution)/shard_map/ppermute | solution.py:376
  137.1 7.7 %collective-permute-start.16 = (f32[64,1024]{1,0:T(8,128)S(1)}, f32[64,1024]{1,0:T(8,128)S(1)}, u32[]{:S(2)}, u32[]{:S(2)}) collective-permute-start(f32[64,1024]{1,0:T(8,128)S(1)} %bitcast_add_fusion.4), channel_id=1, source_target_pairs={{0,8},{8,16},{16,24},{24,32},{32,40},{40,48},{48,56},{56,0},{64,72... | collective-permute-start | bytes 786440 | tf_op jit(solution)/shard_map/ppermute | solution.py:376
  137.2 5.7 %collective-permute-start.18 = (f32[32,1024]{1,0:T(8,128)S(1)}, f32[32,1024]{1,0:T(8,128)S(1)}, u32[]{:S(2)}, u32[]{:S(2)}) collective-permute-start(f32[32,1024]{1,0:T(8,128)S(1)} %get-tuple-element.151), channel_id=1, source_target_pairs={{0,56},{8,0},{16,8},{24,16},{32,24},{40,32},{48,40},{56,48},{64,12... | collective-permute-start | bytes 393224 | tf_op jit(solution)/shard_map/ppermute | solution.py:372
  145.9 8.2 %collective-permute-start.19 = (f32[64,1024]{1,0:T(8,128)S(1)}, f32[64,1024]{1,0:T(8,128)S(1)}, u32[]{:S(2)}, u32[]{:S(2)}) collective-permute-start(f32[64,1024]{1,0:T(8,128)S(1)} %get-tuple-element.149), channel_id=1, source_target_pairs={{0,56},{8,0},{16,8},{24,16},{32,24},{40,32},{48,40},{56,48},{64,12... | collective-permute-start | bytes 786440 | tf_op jit(solution)/shard_map/ppermute | solution.py:377
  155.3 9.2 %collective-permute-start.20 = (f32[64,1024]{1,0:T(8,128)S(1)}, f32[64,1024]{1,0:T(8,128)S(1)}, u32[]{:S(2)}, u32[]{:S(2)}) collective-permute-start(f32[64,1024]{1,0:T(8,128)S(1)} %bitcast_add_fusion.1), channel_id=1, source_target_pairs={{0,56},{8,0},{16,8},{24,16},{32,24},{40,32},{48,40},{56,48},{64,12... | collective-permute-start | bytes 786440 | tf_op jit(solution)/shard_map/ppermute | solution.py:377
  157.4 10.8 %collective-permute-start.17 = (f32[64,1024]{1,0:T(8,128)S(1)}, f32[64,1024]{1,0:T(8,128)S(1)}, u32[]{:S(2)}, u32[]{:S(2)}) collective-permute-start(f32[64,1024]{1,0:T(8,128)S(1)} %get-tuple-element.148), channel_id=1, source_target_pairs={{0,8},{8,16},{16,24},{24,32},{32,40},{40,48},{48,56},{56,0},{64,72... | collective-permute-start | bytes 786440 | tf_op jit(solution)/shard_map/ppermute | solution.py:376
  165.7 6.5 %collective-permute-start.21 = (f32[64,1024]{1,0:T(8,128)S(1)}, f32[64,1024]{1,0:T(8,128)S(1)}, u32[]{:S(2)}, u32[]{:S(2)}) collective-permute-start(f32[64,1024]{1,0:T(8,128)S(1)} %bitcast_add_fusion), channel_id=1, source_target_pairs={{0,56},{8,0},{16,8},{24,16},{32,24},{40,32},{48,40},{56,48},{64,12... | collective-permute-start | bytes 786440 | tf_op jit(solution)/shard_map/ppermute | solution.py:377
  (9 other events, 6.5 us)
Sparse Core Ops, SparseCore 0:
  9.3 44.2 all-gather.5

commit v3 on v2

v3 whole, which is shorter than its diff:
```python
import jax
import jax.numpy as jnp
from jax import lax
from jax.experimental import pallas as pl
from jax.experimental.pallas import tpu as pltpu
from jax.sharding import PartitionSpec as P

XS = 4
ZS = 8
YS = 4
CAP = 32
TOTAL_CAP = 68
LIST = 72
GROUP = 4
EXTRA = 16
HERE = 64
PIECE = 16
WIDTH = 128

Z_GROUPS = [[x * ZS + z for z in range(ZS)] for x in range(XS)]


def x_shift(step):
    return [(x * ZS + z, ((x + step) % XS) * ZS + z) for x in range(XS) for z in range(ZS)]


def z_shift(step):
    return [(x * ZS + z, x * ZS + (z + step) % ZS) for x in range(XS) for z in range(ZS)]


def y_shift(step):
    return [(y * 2 + core, ((y + step) % YS) * 2 + core) for y in range(YS) for core in range(2)]


CORE_SWAP = [(y * 2 + core, y * 2 + 1 - core) for y in range(YS) for core in range(2)]


def contract(blocks, stored, row_list, col_list, live_count):
    tile_width = stored.shape[1]
    group_size = 8
    slot_total = stored.shape[0]
    rows_here = blocks.shape[0]
    groups = (live_count + group_size - 1) // group_size

    def group_step(group, totals):
        index_list = group * group_size + jnp.arange(group_size, dtype=jnp.int32)
        safe_index = jnp.minimum(index_list, slot_total - 1)
        pieces = jnp.take(stored, safe_index, axis=0)
        row_ids = jnp.take(row_list, safe_index, axis=0)
        col_ids = jnp.take(col_list, safe_index, axis=0)
        active = (index_list < live_count).astype(jnp.float32)
        inputs = jnp.take(blocks, row_ids, axis=1)
        product = jnp.einsum("pgk,gkn->pgn", inputs, pieces, precision=lax.Precision.HIGHEST)
        product = product * active[None, :, None]
        return totals.at[:, col_ids, :].add(product)

    start_totals = jnp.zeros((rows_here, blocks.shape[1], tile_width), jnp.float32)
    return lax.fori_loop(0, groups, group_step, start_totals)


def dense_ladder(amplitudes, integrals, tile_rows, tile_cols, tile_count):
    rows_here = amplitudes.shape[0]
    columns_all = amplitudes.shape[1] * lax.axis_size("tile")
    gathered = lax.all_gather(amplitudes, "tile", axis=1, tiled=True)
    blocks = gathered.reshape(rows_here, columns_all // WIDTH, WIDTH)
    partial_value = contract(blocks, integrals, tile_rows, tile_cols, tile_count[0])
    partial_value = partial_value.reshape(rows_here, columns_all)
    return lax.psum_scatter(partial_value, "tile", scatter_dimension=1, tiled=True)


def home(row, col):
    return jnp.minimum(row, col) // HERE


def pad_list(table, first, size, low):
    for pad in range(GROUP):
        table[0, first + size + pad] = 0
        table[1, first + size + pad] = low
        table[2, first + size + pad] = low + HERE + EXTRA


def pack_kernel(place, rows, cols, count, stored, *refs):
    outs, table, sizes, entries, sems = refs[:XS - 1], refs[XS - 1], refs[XS], refs[XS + 1], refs[XS + 2]
    mine = place[0]
    low = mine * HERE
    for each in range(8):
        sizes[each] = 0

    def sort_step(slot, _):
        row, col = rows[slot], cols[slot]
        target = lax.rem(home(row, col) - mine + XS, XS)
        kind = jnp.where(target == 0, jnp.where(col - low >= HERE, 0, XS), target)
        position = sizes[kind]
        at = kind * LIST + position
        table[0, at] = slot
        table[1, at] = row
        table[2, at] = col
        sizes[kind] = position + 1
        return 0

    lax.fori_loop(0, count[0], sort_step, 0)
    over = jnp.int32(0)
    for j in range(1, XS):
        over = jnp.maximum(over, (sizes[j] > CAP).astype(jnp.int32))
    sizes[XS + 1] = over
    pad_list(table, 0, sizes[0], low)
    pad_list(table, XS * LIST, sizes[XS], low)
    copies = []
    for j in range(1, XS):
        out = outs[j - 1]
        entries[j - 1, 2, 0] = over.astype(jnp.float32)
        entries[j - 1, 3, mine] = 0.0
        for other in range(1, XS):
            entries[j - 1, 3, lax.rem(mine + other, XS)] = sizes[other].astype(jnp.float32)

        def move_step(item, _):
            at = j * LIST + item
            out[item] = stored[table[0, at]]
            entries[j - 1, 0, item] = table[1, at].astype(jnp.float32)
            entries[j - 1, 1, item] = table[2, at].astype(jnp.float32)
            return 0

        lax.fori_loop(0, jnp.minimum(sizes[j], CAP), move_step, 0)
        copy = pltpu.make_async_copy(entries.at[j - 1], out.at[CAP, pl.ds(0, 8)], sems.at[j - 1])
        copy.start()
        copies.append(copy)
    for copy in copies:
        copy.wait()


def pack(place, rows, cols, count, integrals):
    slots = integrals.shape[0]
    spec = pltpu.PrefetchScalarGridSpec(
        num_scalar_prefetch=4,
        grid=(1,),
        in_specs=[pl.BlockSpec((slots, PIECE, WIDTH), lambda i, place, *_: (0, place[1], 0))],
        out_specs=[pl.BlockSpec((CAP + 1, PIECE, WIDTH), lambda i, *_: (0, 0, 0))] * (XS - 1)
        + [pl.BlockSpec(memory_space=pltpu.SMEM)] * 2,
        scratch_shapes=[pltpu.SMEM((XS - 1, 8, WIDTH), jnp.float32), pltpu.SemaphoreType.DMA((XS - 1,))],
    )
    return pl.pallas_call(
        pack_kernel,
        grid_spec=spec,
        out_shape=[jax.ShapeDtypeStruct((CAP + 1, PIECE, WIDTH), jnp.float32)] * (XS - 1)
        + [jax.ShapeDtypeStruct((3, (XS + 1) * LIST), jnp.int32), jax.ShapeDtypeStruct((8,), jnp.int32)],
        compiler_params=pltpu.CompilerParams(vmem_limit_bytes=8 * 2**20),
        name="pack",
    )(place, rows, cols, count, integrals)


def compact_kernel(place, sizes, *refs):
    sources, (out, table, totals, entries, sems) = refs[:XS - 1], refs[XS - 1:]
    mine = place[0]
    low = mine * HERE
    copies = [
        pltpu.make_async_copy(sources[j].at[CAP, pl.ds(0, 8)], entries.at[j], sems.at[j]) for j in range(XS - 1)
    ]
    for copy in copies:
        copy.start()
    for copy in copies:
        copy.wait()
    for each in range(8):
        totals[each] = 0
    over = sizes[XS + 1] > 0
    for j in range(XS - 1):
        over = over | (entries[j, 2, 0] > 0.5)
    for j in range(XS):
        there = lax.rem(mine + j, XS)
        total = jnp.int32(0) if j == 0 else sizes[j]
        for source in range(XS - 1):
            total = total + entries[source, 3, there].astype(jnp.int32)
        over = over | (total > TOTAL_CAP)
    base = jnp.int32(0)
    for j in range(XS - 1):
        source = sources[j]
        size = jnp.minimum(jnp.minimum(entries[j, 3, mine].astype(jnp.int32), CAP), TOTAL_CAP - base)

        def step(item, _):
            row = entries[j, 0, item].astype(jnp.int32)
            col = entries[j, 1, item].astype(jnp.int32)
            out[base + item] = source[item]
            kind = jnp.where(col - low >= HERE, 0, 1)
            position = totals[kind]
            at = kind * LIST + position
            table[0, at] = base + item
            table[1, at] = row
            table[2, at] = col
            totals[kind] = position + 1
            return 0

        lax.fori_loop(0, size, step, 0)
        base = base + size
    totals[2] = over.astype(jnp.int32)
    pad_list(table, 0, totals[0], low)
    pad_list(table, LIST, totals[1], low)


def compact(place, sizes, sources):
    vmem = pl.BlockSpec(memory_space=pltpu.VMEM)
    smem = pl.BlockSpec(memory_space=pltpu.SMEM)
    return pl.pallas_call(
        compact_kernel,
        in_specs=[smem] * 2 + [vmem] * (XS - 1),
        out_specs=[vmem, smem, smem],
        out_shape=[
            jax.ShapeDtypeStruct((TOTAL_CAP, PIECE, WIDTH), jnp.float32),
            jax.ShapeDtypeStruct((3, 2 * LIST), jnp.int32),
            jax.ShapeDtypeStruct((8,), jnp.int32),
        ],
        scratch_shapes=[pltpu.SMEM((XS - 1, 8, WIDTH), jnp.float32), pltpu.SemaphoreType.DMA((XS - 1,))],
        compiler_params=pltpu.CompilerParams(vmem_limit_bytes=8 * 2**20),
        name="compact",
    )(place, sizes, *sources)


def split_of(value):
    high = value.astype(jnp.bfloat16)
    return high, (value - high.astype(jnp.float32)).astype(jnp.bfloat16)


def products_of(low_tile, table, first, size, fetch, split, sums):
    blank = jnp.zeros((WIDTH, WIDTH), jnp.bfloat16)

    def step(group, _):
        products = []
        for member in range(GROUP):
            at = first + group * GROUP + member
            high, low = split_of(fetch(member, table[0, at]))
            right = jnp.concatenate(
                [jnp.concatenate([high, low], axis=1), jnp.concatenate([high, blank], axis=1)], axis=0
            )
            product = jnp.dot(split[table[1, at] - low_tile], right, preferred_element_type=jnp.float32)
            products.append(product[:, :WIDTH] + product[:, WIDTH:])
        for member in range(GROUP):
            col = table[2, first + group * GROUP + member] - low_tile
            lanes = pl.ds(pl.multiple_of(lax.rem(col, ZS) * WIDTH, WIDTH), WIDTH)
            sums[lax.div(col, ZS), :, lanes] += products[member]
        return 0

    lax.fori_loop(0, lax.div(size + GROUP - 1, GROUP), step, 0)


def fill_split(split, source, first):
    for block in range(source.shape[0]):
        for part in range(ZS):
            high, low = split_of(source[block, :, part * WIDTH:(part + 1) * WIDTH])
            split[first + block * ZS + part, :, :WIDTH] = high
            split[first + block * ZS + part, :, WIDTH:] = low


def fetchers(place, stored, pieces, tile):
    my_y = lax.div(place[1], 2)
    my_core = lax.rem(place[1], 2)

    def own(member, index):
        return stored[index]

    def moved(member, index):
        for shift in range(YS):
            for swapped in range(2):
                core = my_core if swapped == 0 else 1 - my_core
                origin = lax.rem(my_y - shift + YS, YS) * 2 + core
                at = pl.multiple_of(origin * PIECE, PIECE)
                tile[member, pl.ds(at, PIECE), :] = pieces[shift * 2 + swapped, index]
        return tile[member]

    return own, moved


def outer_kernel(place, own, sizes, moved, totals, near_hbm, stored_hbm, *refs):
    pieces_hbm, (out_hbm, near, stored, pieces, split, tile, sums, sems) = refs[:2 * YS], refs[2 * YS:]
    low_tile = place[0] * HERE
    sums[...] = jnp.zeros_like(sums)

    @pl.when(sizes[0] + totals[0] > 0)
    def _():
        copies = [
            pltpu.make_async_copy(near_hbm, near, sems.at[0]),
            pltpu.make_async_copy(stored_hbm, stored, sems.at[1]),
        ] + [pltpu.make_async_copy(pieces_hbm[k], pieces.at[k], sems.at[2 + k]) for k in range(2 * YS)]
        for copy in copies:
            copy.start()
        copies[0].wait()
        fill_split(split, near, 0)
        fetch_own, fetch_moved = fetchers(place, stored, pieces, tile)
        copies[1].wait()
        products_of(low_tile, own, 0, sizes[0], fetch_own, split, sums)
        for copy in copies[2:]:
            copy.wait()
        products_of(low_tile, moved, 0, totals[0], fetch_moved, split, sums)

    back = pltpu.make_async_copy(sums.at[pl.ds(ZS, 2)], out_hbm, sems.at[2 + 2 * YS])
    back.start()
    back.wait()


def inner_kernel(place, own, sizes, moved, totals, near_hbm, extra_hbm, stored_hbm, *refs):
    pieces_hbm, outs = refs[:2 * YS], refs[2 * YS:2 * YS + ZS + 1]
    near, extra, stored, pieces, split, tile, sums, sems = refs[2 * YS + ZS + 1:]
    low_tile = place[0] * HERE
    copies = [
        pltpu.make_async_copy(near_hbm, near, sems.at[0]),
        pltpu.make_async_copy(extra_hbm, extra, sems.at[1]),
        pltpu.make_async_copy(stored_hbm, stored, sems.at[2]),
    ] + [pltpu.make_async_copy(pieces_hbm[k], pieces.at[k], sems.at[3 + k]) for k in range(2 * YS)]
    for copy in copies:
        copy.start()
    sums[...] = jnp.zeros_like(sums)
    copies[0].wait()
    fill_split(split, near, 0)
    copies[1].wait()
    fill_split(split, extra, HERE)
    fetch_own, fetch_moved = fetchers(place, stored, pieces, tile)
    copies[2].wait()
    products_of(low_tile, own, XS * LIST, sizes[XS], fetch_own, split, sums)
    for copy in copies[3:]:
        copy.wait()
    products_of(low_tile, moved, LIST, totals[1], fetch_moved, split, sums)

    @pl.when(totals[2] > 0)
    def _():
        sums[...] = jnp.full_like(sums, jnp.nan)

    half = near.shape[1] // 2
    first_sem = 3 + 2 * YS
    backs = []
    for step in range(ZS + 1):
        block = lax.rem(place[2] + (step if step < ZS else ZS // 2), ZS)
        source = sums.at[block]
        if step == ZS // 2:
            source = sums.at[block, pl.ds(0, half)]
        if step == ZS:
            source = sums.at[block, pl.ds(half, half)]
        backs.append(pltpu.make_async_copy(source, outs[step], sems.at[first_sem + step]))
    for back in backs:
        back.start()
    for back in backs:
        back.wait()


def scratch_of(near, extra, integrals, sem_count):
    _, rows_here, wide = near.shape
    shapes = [near.shape] + ([extra.shape] if extra is not None else []) + [integrals.shape]
    return [pltpu.VMEM(shape, jnp.float32) for shape in shapes] + [
        pltpu.VMEM((2 * YS, TOTAL_CAP, PIECE, WIDTH), jnp.float32),
        pltpu.VMEM((HERE + EXTRA, rows_here, 2 * WIDTH), jnp.bfloat16),
        pltpu.VMEM((GROUP, WIDTH, WIDTH), jnp.float32),
        pltpu.VMEM((ZS + 3, rows_here, wide), jnp.float32),
        pltpu.SemaphoreType.DMA((sem_count,)),
    ]


def outer_sums(place, own, sizes, moved, totals, near, stored, pieces):
    _, rows_here, wide = near.shape
    smem = pl.BlockSpec(memory_space=pltpu.SMEM)
    anywhere = pl.BlockSpec(memory_space=pl.ANY)
    return pl.pallas_call(
        outer_kernel,
        in_specs=[smem] * 5 + [anywhere] * (2 + 2 * YS),
        out_specs=anywhere,
        out_shape=jax.ShapeDtypeStruct((2, rows_here, wide), jnp.float32),
        scratch_shapes=scratch_of(near, None, stored, 3 + 2 * YS),
        cost_estimate=pl.CostEstimate(flops=5 * 10**9, bytes_accessed=10**7, transcendentals=0),
        compiler_params=pltpu.CompilerParams(vmem_limit_bytes=28 * 2**20),
        name="outer",
    )(place, own, sizes, moved, totals, near, stored, *pieces)


def inner_sums(place, own, sizes, moved, totals, near, extra, stored, pieces):
    _, rows_here, wide = near.shape
    smem = pl.BlockSpec(memory_space=pltpu.SMEM)
    anywhere = pl.BlockSpec(memory_space=pl.ANY)
    heights = [rows_here] * (ZS // 2) + [rows_here // 2] + [rows_here] * (ZS // 2 - 1) + [rows_here // 2]
    return pl.pallas_call(
        inner_kernel,
        in_specs=[smem] * 5 + [anywhere] * (3 + 2 * YS),
        out_specs=[anywhere] * (ZS + 1),
        out_shape=[jax.ShapeDtypeStruct((height, wide), jnp.float32) for height in heights],
        scratch_shapes=scratch_of(near, extra, stored, 3 + 2 * YS + ZS + 1),
        cost_estimate=pl.CostEstimate(flops=10**10, bytes_accessed=10**7, transcendentals=0),
        compiler_params=pltpu.CompilerParams(vmem_limit_bytes=28 * 2**20),
        name="inner",
    )(place, own, sizes, moved, totals, near, extra, stored, *pieces)


def ring_sum(parts, more):
    half = ZS // 2
    rows_here = parts[0].shape[0]
    middle = more(half)
    up, down = parts[half] + middle[:rows_here // 2], parts[ZS] + middle[rows_here // 2:]
    for step in range(half - 1, -1, -1):
        up, down = lax.optimization_barrier((up, down))
        up = lax.ppermute(up, "tile", z_shift(1))
        down = lax.ppermute(down, "tile", z_shift(-1))
        up, down = lax.optimization_barrier((up, down))
        if step == half - 1:
            up = jnp.concatenate([up, jnp.zeros_like(up)], axis=0)
            down = jnp.concatenate([jnp.zeros_like(down), down], axis=0)
        if step > 0:
            up = up + parts[step] + more(step)
            down = down + parts[ZS - step] + more(ZS - step)
    return parts[0] + more(0) + up + down


def shards(
    amplitudes, driver, integrals, tile_rows, tile_cols, tile_count, pair_energy, virt_energy
):
    my_tile = lax.axis_index("tile")
    my_x = my_tile // ZS
    my_z = lax.rem(my_tile, ZS)
    place = jnp.stack([my_x, lax.axis_index("pair"), my_z]).astype(jnp.int32)

    near = lax.all_gather(amplitudes, "tile", axis=0, axis_index_groups=Z_GROUPS)

    *packed, own, sizes = pack(place, tile_rows, tile_cols, tile_count, integrals)
    arrived = [lax.ppermute(packed[step - 1], "tile", x_shift(step)) for step in range(1, XS)]
    mine, moved, totals = compact(place, sizes, arrived)
    along_y = [mine] + [lax.ppermute(mine, "pair", y_shift(step)) for step in range(1, YS)]
    along_y[1], near = lax.optimization_barrier((along_y[1], near))
    extra = lax.ppermute(near[:2], "tile", x_shift(-1))
    pieces = []
    for piece in along_y:
        pieces += [piece, lax.ppermute(piece, "pair", CORE_SWAP)]

    beyond = outer_sums(place, own, sizes, moved, totals, near, integrals, pieces)
    from_left = lax.ppermute(beyond, "tile", x_shift(1))
    parts = inner_sums(place, own, sizes, moved, totals, near, extra, integrals, pieces)

    def more(step):
        block = lax.rem(my_z + step, ZS)
        return jnp.where(
            (my_x > 0) & (block == 0), from_left[0], jnp.where((my_x > 0) & (block == 1), from_left[1], 0.0)
        )

    ladder = ring_sum(parts, more)
    denominator = virt_energy[None, :] - pair_energy[:, None]
    result = (driver + ladder) / denominator

    def slow():
        full = dense_ladder(amplitudes, integrals, tile_rows, tile_cols, tile_count)
        return (driver + full) / denominator

    return lax.cond(jnp.isnan(ladder[0, 0]), slow, lambda: result)


def solution(mesh):
    return jax.shard_map(
        shards,
        mesh=mesh,
        in_specs=(
            P("pair", "tile"),
            P("pair", "tile"),
            P("tile", None, None),
            P("tile"),
            P("tile"),
            P("tile"),
            P("pair"),
            P("tile"),
        ),
        out_specs=P("pair", "tile"),
        check_vma=False,
    )
```

time: 186 us -> 138 us (0.74); the launches traced: 183 us -> 137 us
  local copies, waits for them, and re-layouts: 26.7 us -> 9.17 us
  waiting for transfers between devices: 77.1 us -> 64.1 us
  starting transfers between devices: 35.1 us -> 29.3 us
  Pallas kernels: 17.9 us -> 13.7 us
  other arithmetic: 8.25 us -> 4.81 us
  between operations: 17.5 us -> 15.6 us
    ppermute x10 -> x8, waiting for transfers between devices: 39.4 us -> 16.8 us  [the longest x4 16.7 us: ring_sum(): up = lax.ppermute(up, 'tile', z_shift(1))]
    unnamed x68 -> x30, local copies, waits for them, and re-layouts: 24.7 us -> 6.56 us
    ppermute x1, waiting for transfers between devices: 0.01 us -> 9.22 us  [shards(): extra = lax.ppermute(near[:2], 'tile', x_shift(-1))]
    ppermute x10 -> x8, starting transfers between devices: 23.8 us -> 15.6 us  [the longest x4 14.9 us: ring_sum(): down = lax.ppermute(down, 'tile', z_shift(-1))]
    ppermute x1, starting transfers between devices: 0.01 us -> 3.31 us  [shards(): from_left = lax.ppermute(beyond, 'tile', x_shift(1))]
    add x6 -> x4, other arithmetic: 5.9 us -> 3.45 us  [the longest x3 3.42 us: ring_sum(): down = down + parts[ZS - step] + more(ZS - step)]
    pallas_call x2, Pallas kernels: 9.59 us -> 7.4 us  [the longest x1 6.35 us: inner_sums(): pl.pallas_call(inner_kernel, in_specs=[smem] * 5 + [anywhere] * (3 + 2 *...]
    ppermute x1, starting transfers between devices: 2.02 us -> 0.01 us  [shards(): extra = lax.ppermute(near[:2], 'tile', x_shift(-1))]
  transfers between devices with their start and end apart: 23 -> 21, of which waited for: 14 -> 10; matrix products, arithmetic and copies ran while one was open for 2% -> 2% of each run, Pallas kernels for 5% -> 10%
where the time goes in v3:
time: 138 us; the launch traced here: 137 us
  waiting for transfers between devices  64.1 us (46%)
  starting transfers between devices  29.3 us (21%)
  between operations  15.6 us (11%)
  Pallas kernels  13.7 us (10%)
  local copies, waits for them, and re-layouts  9.17 us (7%)
  other arithmetic  4.81 us (3%)
    ppermute x3, waiting for transfers between devices, shards(): lax.ppermute(mine, 'pair', y_shift(step))  25.7 us
    ppermute x4, waiting for transfers between devices, ring_sum(): up = lax.ppermute(up, 'tile', z_shift(1))  16.7 us
    ppermute x4, starting transfers between devices, ring_sum(): down = lax.ppermute(down, 'tile', z_shift(-1))  14.9 us
    ppermute x3, waiting for transfers between devices, shards(): lax.ppermute(packed[step - 1], 'tile', x_shift(step))  11.7 us
    ppermute x1, waiting for transfers between devices, shards(): extra = lax.ppermute(near[:2], 'tile', x_shift(-1))  9.22 us
    unnamed x30, local copies, waits for them, and re-layouts  6.56 us
    pallas_call x1, Pallas kernels, inner_sums(): pl.pallas_call(inner_kernel, in_specs=[smem] * 5 + [anywhere] * (3 + 2 *...  6.35 us
    ppermute x3, starting transfers between devices, shards(): lax.ppermute(mine, 'pair', y_shift(step))  5.52 us
  transfers between devices with their start and end apart: 21, of which 10 were waited for; matrix products, arithmetic and copies ran while one was open for 2% of the time, Pallas kernels for 10%

profile of v3, /device:TPU:6, one launch (start us, length us, event | category | flops | bytes accessed | tf_op | source)
XLA Modules:
  0.0 136.7 jit_solution(12040550327281260217)
XLA Ops:
  6.5 0.7 all-gather.6.cloned.1.call-update
  7.9 0.1 pad_add_fusion.place
  8.0 3.5 %pack.1 = (f32[33,16,128]{2,1,0:T(8,128)S(1)}, f32[33,16,128]{2,1,0:T(8,128)S(1)}, f32[33,16,128]{2,1,0:T(8,128)S(1)}, s32[3,360]{1,0:T(4,128)S(1)}, s32[8]{0:T(128)S(1)}) custom-call(s32[3]{0:T(128)S(1)} %pad_add_fusion.place, s32[64]{0:T(128)} %rows.1, s32[64]{0:T(128)} %cols.1, s32[1]{0:T(128)S(6)} %copy.30.count, f32[64,128,128]{2,1,0:T(8,128)} %stored_hbm.3), custom_call_target="tpu_custom_call" | custom-call | tf_op jit(solution)/shard_map/pack/pallas_call | solution.py:141
  11.5 3.4 %collective-permute-start = (f32[33,16,128]{2,1,0:T(8,128)S(1)}, f32[33,16,128]{2,1,0:T(8,128)S(1)}, u32[]{:S(2)}, u32[]{:S(2)}) collective-permute-start(f32[33,16,128]{2,1,0:T(8,128)S(1)} %get-tuple-element.122), channel_id=1, source_target_pairs={{0,64},{8,72},{16,80},{24,88},{32,96},{40,104},{48,112},{56,120},{... | collective-permute-start | bytes 811016 | tf_op jit(solution)/shard_map/ppermute | solution.py:416
  14.9 1.0 collective-permute-start.2
  15.8 5.1 %collective-permute-done.refs_0_ = f32[33,16,128]{2,1,0:T(8,128)S(1)} collective-permute-done((f32[33,16,128]{2,1,0:T(8,128)S(1)}, f32[33,16,128]{2,1,0:T(8,128)S(1)}, u32[]{:S(2)}, u32[]{:S(2)}) %collective-permute-start) | collective-permute-done | bytes 270368 | tf_op jit(solution)/shard_map/ppermute | solution.py:416
  21.0 3.8 %collective-permute-done.1.refs_1_ = f32[33,16,128]{2,1,0:T(8,128)S(1)} collective-permute-done((f32[33,16,128]{2,1,0:T(8,128)S(1)}, f32[33,16,128]{2,1,0:T(8,128)S(1)}, u32[]{:S(2)}, u32[]{:S(2)}) %collective-permute-start.1) | collective-permute-done | bytes 270368 | tf_op jit(solution)/shard_map/ppermute | solution.py:416
  24.7 2.8 %collective-permute-done.2.refs_2_ = f32[33,16,128]{2,1,0:T(8,128)S(1)} collective-permute-done((f32[33,16,128]{2,1,0:T(8,128)S(1)}, f32[33,16,128]{2,1,0:T(8,128)S(1)}, u32[]{:S(2)}, u32[]{:S(2)}) %collective-permute-start.2) | collective-permute-done | bytes 270368 | tf_op jit(solution)/shard_map/ppermute | solution.py:416
  27.6 2.8 %compact.1 = (f32[68,16,128]{2,1,0:T(8,128)S(1)}, s32[3,144]{1,0:T(4,128)S(1)}, s32[8]{0:T(128)S(1)}) custom-call(s32[3]{0:T(128)S(1)} %pad_add_fusion.place, s32[8]{0:T(128)S(1)} %get-tuple-element.121.sizes, f32[33,16,128]{2,1,0:T(8,128)S(1)} %collective-permute-done.refs_0_, f32[33,16,128]{2,1,0:T(8,128)S(1)} %collective-permute-done.1.refs_1_, ...), custom_call_target="tpu_custom_call" | custom-call | tf_op jit(solution)/shard_map/compact/pallas_call | solution.py:201
  30.3 3.9 %collective-permute-start.9 = (f32[68,16,128]{2,1,0:T(8,128)S(1)}, f32[68,16,128]{2,1,0:T(8,128)S(1)}, u32[]{:S(2)}, u32[]{:S(2)}) collective-permute-start(f32[68,16,128]{2,1,0:T(8,128)S(1)} %get-tuple-element.127.refs_0_), channel_id=1, source_target_pairs={{0,6},{1,7},{2,0},{3,1},{4,2},{5,3},{6,4},{7,5},{8,14},{9,15},{10,... | collective-permute-start | bytes 1671176 | tf_op jit(solution)/shard_map/ppermute | solution.py:418
  34.3 0.6 collective-permute-start.7
  34.9 1.0 collective-permute-start.3
  35.9 22.5 %collective-permute-done.9.refs_6_ = f32[68,16,128]{2,1,0:T(8,128)S(1)} collective-permute-done((f32[68,16,128]{2,1,0:T(8,128)S(1)}, f32[68,16,128]{2,1,0:T(8,128)S(1)}, u32[]{:S(2)}, u32[]{:S(2)}) %collective-permute-start.9) | collective-permute-done | bytes 557088 | tf_op jit(solution)/shard_map/ppermute | solution.py:418
  58.4 0.5 collective-permute-start.8
  58.9 3.2 %collective-permute-done.3.refs_2_ = f32[68,16,128]{2,1,0:T(8,128)S(1)} collective-permute-done((f32[68,16,128]{2,1,0:T(8,128)S(1)}, f32[68,16,128]{2,1,0:T(8,128)S(1)}, u32[]{:S(2)}, u32[]{:S(2)}) %collective-permute-start.3) | collective-permute-done | bytes 557088 | tf_op jit(solution)/shard_map/ppermute | solution.py:418
  62.1 0.0 collective-permute-start.6
  62.1 2.1 %slice.18 = f32[2,64,1024]{2,1,0:T(8,128)} slice(f32[8,64,1024]{2,1,0:T(8,128)} %bitcast.55), slice={[0:2], [0:64], [0:1024]} | slice | bytes 1048576 | tf_op jit(solution)/shard_map/slice | solution.py:420
  64.3 2.0 %copy-done = f32[512,1024]{1,0:T(8,128)S(1)} copy-done((f32[512,1024]{1,0:T(8,128)S(1)}, f32[512,1024]{1,0:T(8,128)}, u32[]{:S(2)}) %copy-start) | copy-done | bytes 2097176
  66.2 1.0 outer.1
  67.3 3.3 %collective-permute-start.11 = (f32[2,64,1024]{2,1,0:T(8,128)S(1)}, f32[2,64,1024]{2,1,0:T(8,128)S(1)}, u32[]{:S(2)}, u32[]{:S(2)}) collective-permute-start(f32[2,64,1024]{2,1,0:T(8,128)S(1)} %outer.1), channel_id=1, source_target_pairs={{0,64},{8,72},{16,80},{24,88},{32,96},{40,104},{48,112},{56,120},{... | collective-permute-start | bytes 1572872 | tf_op jit(solution)/shard_map/ppermute | solution.py:426
  70.6 9.2 %collective-permute-done.4.extra_hbm = f32[2,64,1024]{2,1,0:T(8,128)} collective-permute-done((f32[2,64,1024]{2,1,0:T(8,128)}, f32[2,64,1024]{2,1,0:T(8,128)}, u32[]{:S(2)}, u32[]{:S(2)}) %collective-permute-start.4) | collective-permute-done | bytes 524320 | tf_op jit(solution)/shard_map/ppermute | solution.py:420
  79.8 1.1 copy-done.2
  80.9 1.1 copy-done.4
  82.0 1.1 copy-done.6
  83.0 6.3 %inner.1 = (f32[64,1024]{1,0:T(8,128)S(1)}, f32[64,1024]{1,0:T(8,128)S(1)}, f32[64,1024]{1,0:T(8,128)S(1)}, f32[64,1024]{1,0:T(8,128)S(1)}, f32[32,1024]{1,0:T(8...) custom-call(s32[3]{0:T(128)S(1)} %pad_add_fusion.place, ...), custom_call_target="tpu_custom_call" | custom-call | flops 10000000000 | bytes 10000000 | tf_op jit(solution)/shard_map/inner/pallas_call | solution.py:374
  89.4 0.0 copy-start.7
  89.4 0.0 copy-start.8
  89.5 0.7 copy-done.9
  90.2 5.6 %collective-permute-start.13 = (f32[32,1024]{1,0:T(8,128)S(1)}, f32[32,1024]{1,0:T(8,128)S(1)}, u32[]{:S(2)}, u32[]{:S(2)}) collective-permute-start(f32[32,1024]{1,0:T(8,128)S(1)} %get-tuple-element.134), channel_id=1, source_target_pairs={{0,56},{8,0},{16,8},{24,16},{32,24},{40,32},{48,40},{56,48},{64,12... | collective-permute-start | bytes 393224 | tf_op jit(solution)/shard_map/ppermute | solution.py:394
  95.8 3.2 %collective-permute-done.12 = f32[32,1024]{1,0:T(8,128)S(1)} collective-permute-done((f32[32,1024]{1,0:T(8,128)S(1)}, f32[32,1024]{1,0:T(8,128)S(1)}, u32[]{:S(2)}, u32[]{:S(2)}) %collective-permute-start.12) | collective-permute-done | bytes 131104 | tf_op jit(solution)/shard_map/ppermute | solution.py:393
  99.0 1.1 bitcast_add_fusion.4
  100.1 0.1 collective-permute-start.14
  100.2 3.2 %collective-permute-start.15 = (f32[64,1024]{1,0:T(8,128)S(1)}, f32[64,1024]{1,0:T(8,128)S(1)}, u32[]{:S(2)}, u32[]{:S(2)}) collective-permute-start(f32[64,1024]{1,0:T(8,128)S(1)} %get-tuple-element.140), channel_id=1, source_target_pairs={{0,56},{8,0},{16,8},{24,16},{32,24},{40,32},{48,40},{56,48},{64,12... | collective-permute-start | bytes 786440 | tf_op jit(solution)/shard_map/ppermute | solution.py:394
  103.4 5.1 %collective-permute-done.14 = f32[64,1024]{1,0:T(8,128)S(1)} collective-permute-done((f32[64,1024]{1,0:T(8,128)S(1)}, f32[64,1024]{1,0:T(8,128)S(1)}, u32[]{:S(2)}, u32[]{:S(2)}) %collective-permute-start.14) | collective-permute-done | bytes 262176 | tf_op jit(solution)/shard_map/ppermute | solution.py:393
  108.5 1.1 bitcast_add_fusion.2
  109.6 0.1 collective-permute-start.16
  109.7 3.2 %collective-permute-start.17 = (f32[64,1024]{1,0:T(8,128)S(1)}, f32[64,1024]{1,0:T(8,128)S(1)}, u32[]{:S(2)}, u32[]{:S(2)}) collective-permute-start(f32[64,1024]{1,0:T(8,128)S(1)} %get-tuple-element.146), channel_id=1, source_target_pairs={{0,56},{8,0},{16,8},{24,16},{32,24},{40,32},{48,40},{56,48},{64,12... | collective-permute-start | bytes 786440 | tf_op jit(solution)/shard_map/ppermute | solution.py:394
  112.9 4.3 %collective-permute-done.16 = f32[64,1024]{1,0:T(8,128)S(1)} collective-permute-done((f32[64,1024]{1,0:T(8,128)S(1)}, f32[64,1024]{1,0:T(8,128)S(1)}, u32[]{:S(2)}, u32[]{:S(2)}) %collective-permute-start.16) | collective-permute-done | bytes 262176 | tf_op jit(solution)/shard_map/ppermute | solution.py:393
  117.3 1.1 bitcast_add_fusion
  118.4 0.5 collective-permute-start.18
  118.9 2.9 %collective-permute-start.19 = (f32[64,1024]{1,0:T(8,128)S(1)}, f32[64,1024]{1,0:T(8,128)S(1)}, u32[]{:S(2)}, u32[]{:S(2)}) collective-permute-start(f32[64,1024]{1,0:T(8,128)S(1)} %get-tuple-element.152), channel_id=1, source_target_pairs={{0,56},{8,0},{16,8},{24,16},{32,24},{40,32},{48,40},{56,48},{64,12... | collective-permute-start | bytes 786440 | tf_op jit(solution)/shard_map/ppermute | solution.py:394
  121.8 0.1 broadcast_subtract_fusion
  121.9 4.2 %collective-permute-done.18 = f32[64,1024]{1,0:T(8,128)S(1)} collective-permute-done((f32[64,1024]{1,0:T(8,128)S(1)}, f32[64,1024]{1,0:T(8,128)S(1)}, u32[]{:S(2)}, u32[]{:S(2)}) %collective-permute-start.18) | collective-permute-done | bytes 262176 | tf_op jit(solution)/shard_map/ppermute | solution.py:393
  126.1 1.1 fusion.11
  127.2 0.5 slice.58
  129.0 0.1 conditional.1
  129.1 0.1 add_divide_fusion
  129.1 0.7 copy-done.12
  (41 shorter events, 0.2 us)
Async XLA Ops:
  6.5 55.5 %all-gather.6.cloned.1.call-start = ((), (), s32[]{:S(2)}) async-start(), calls=%async_computation.3 | async-start | bytes 2359296 | tf_op jit(solution)/shard_map/all_gather | solution.py:413
  11.5 9.4 %collective-permute-start = (f32[33,16,128]{2,1,0:T(8,128)S(1)}, f32[33,16,128]{2,1,0:T(8,128)S(1)}, u32[]{:S(2)}, u32[]{:S(2)}) collective-permute-start(f32[33,16,128]{2,1,0:T(8,128)S(1)} %get-tuple-element.122), channel_id=1, source_target_pairs={{0,64},{8,72},{16,80},{24,88},{32,96},{40,104},{48,112},{56,120},{... | collective-permute-start | bytes 811016 | tf_op jit(solution)/shard_map/ppermute | solution.py:416
  14.9 9.8 %collective-permute-start.1 = (f32[33,16,128]{2,1,0:T(8,128)S(1)}, f32[33,16,128]{2,1,0:T(8,128)S(1)}, u32[]{:S(2)}, u32[]{:S(2)}) collective-permute-start(f32[33,16,128]{2,1,0:T(8,128)S(1)} %get-tuple-element.123), channel_id=1, source_target_pairs={{0,128},{8,136},{16,144},{24,152},{32,160},{40,168},{48,176},{56,1... | collective-permute-start | bytes 811016 | tf_op jit(solution)/shard_map/ppermute | solution.py:416
  14.9 12.7 %collective-permute-start.2 = (f32[33,16,128]{2,1,0:T(8,128)S(1)}, f32[33,16,128]{2,1,0:T(8,128)S(1)}, u32[]{:S(2)}, u32[]{:S(2)}) collective-permute-start(f32[33,16,128]{2,1,0:T(8,128)S(1)} %get-tuple-element.124), channel_id=1, source_target_pairs={{0,192},{8,200},{16,208},{24,216},{32,224},{40,232},{48,240},{56,2... | collective-permute-start | bytes 811016 | tf_op jit(solution)/shard_map/ppermute | solution.py:416
  30.3 28.0 %collective-permute-start.9 = (f32[68,16,128]{2,1,0:T(8,128)S(1)}, f32[68,16,128]{2,1,0:T(8,128)S(1)}, u32[]{:S(2)}, u32[]{:S(2)}) collective-permute-start(f32[68,16,128]{2,1,0:T(8,128)S(1)} %get-tuple-element.127.refs_0_), channel_id=1, source_target_pairs={{0,6},{1,7},{2,0},{3,1},{4,2},{5,3},{6,4},{7,5},{8,14},{9,15},{10,... | collective-permute-start | bytes 1671176 | tf_op jit(solution)/shard_map/ppermute | solution.py:418
  34.3 24.1 %collective-permute-start.7 = (f32[68,16,128]{2,1,0:T(8,128)S(1)}, f32[68,16,128]{2,1,0:T(8,128)S(1)}, u32[]{:S(2)}, u32[]{:S(2)}) collective-permute-start(f32[68,16,128]{2,1,0:T(8,128)S(1)} %get-tuple-element.127.refs_0_), channel_id=1, source_target_pairs={{0,4},{1,5},{2,6},{3,7},{4,0},{5,1},{6,2},{7,3},{8,12},{9,13},{10,... | collective-permute-start | bytes 1671176 | tf_op jit(solution)/shard_map/ppermute | solution.py:418
  34.9 27.2 %collective-permute-start.3 = (f32[68,16,128]{2,1,0:T(8,128)S(1)}, f32[68,16,128]{2,1,0:T(8,128)S(1)}, u32[]{:S(2)}, u32[]{:S(2)}) collective-permute-start(f32[68,16,128]{2,1,0:T(8,128)S(1)} %get-tuple-element.127.refs_0_), channel_id=1, source_target_pairs={{0,2},{1,3},{2,4},{3,5},{4,6},{5,7},{6,0},{7,1},{8,10},{9,11},{10,... | collective-permute-start | bytes 1671176 | tf_op jit(solution)/shard_map/ppermute | solution.py:418
  35.9 28.3 %collective-permute-start.5 = (f32[68,16,128]{2,1,0:T(8,128)S(1)}, f32[68,16,128]{2,1,0:T(8,128)S(1)}, u32[]{:S(2)}, u32[]{:S(2)}) collective-permute-start(f32[68,16,128]{2,1,0:T(8,128)S(1)} %get-tuple-element.127.refs_0_), channel_id=1, source_target_pairs={{0,1},{1,0},{2,3},{3,2},{4,5},{5,4},{6,7},{7,6},{8,9},{9,8},{10,11... | collective-permute-start | bytes 1671176 | tf_op jit(solution)/shard_map/ppermute | solution.py:423
  58.4 5.8 %collective-permute-start.10 = (f32[68,16,128]{2,1,0:T(8,128)S(1)}, f32[68,16,128]{2,1,0:T(8,128)S(1)}, u32[]{:S(2)}, u32[]{:S(2)}) collective-permute-start(f32[68,16,128]{2,1,0:T(8,128)S(1)} %collective-permute-done.9.refs_6_), channel_id=1, source_target_pairs={{0,1},{1,0},{2,3},{3,2},{4,5},{5,4},{6,7},{7,6},{8,9},{9,8},{10,11... | collective-permute-start | bytes 1671176 | tf_op jit(solution)/shard_map/ppermute | solution.py:423
  58.4 5.9 %collective-permute-start.8 = (f32[68,16,128]{2,1,0:T(8,128)S(1)}, f32[68,16,128]{2,1,0:T(8,128)}, u32[]{:S(2)}, u32[]{:S(2)}) collective-permute-start(f32[68,16,128]{2,1,0:T(8,128)S(1)} %collective-permute-done.7.refs_4_), channel_id=1, source_target_pairs={{0,1},{1,0},{2,3},{3,2},{4,5},{5,4},{6,7},{7,6},{8,9},{9,8},{10,11... | collective-permute-start | bytes 1671176 | tf_op jit(solution)/shard_map/ppermute | solution.py:423
  62.1 5.2 %copy-start.1 = (f32[68,16,128]{2,1,0:T(8,128)}, f32[68,16,128]{2,1,0:T(8,128)S(1)}, u32[]{:S(2)}) copy-start(f32[68,16,128]{2,1,0:T(8,128)S(1)} %collective-permute-done.3.refs_2_) | copy-start | bytes 1671172
  62.1 2.2 %collective-permute-start.6 = (f32[68,16,128]{2,1,0:T(8,128)S(1)}, f32[68,16,128]{2,1,0:T(8,128)}, u32[]{:S(2)}, u32[]{:S(2)}) collective-permute-start(f32[68,16,128]{2,1,0:T(8,128)S(1)} %collective-permute-done.3.refs_2_), channel_id=1, source_target_pairs={{0,1},{1,0},{2,3},{3,2},{4,5},{5,4},{6,7},{7,6},{8,9},{9,8},{10,11... | collective-permute-start | bytes 1671176 | tf_op jit(solution)/shard_map/ppermute | solution.py:423
  64.2 15.6 %collective-permute-start.4 = (f32[2,64,1024]{2,1,0:T(8,128)}, f32[2,64,1024]{2,1,0:T(8,128)}, u32[]{:S(2)}, u32[]{:S(2)}) collective-permute-start(f32[2,64,1024]{2,1,0:T(8,128)} %slice.18), channel_id=1, source_target_pairs={{0,192},{8,200},{16,208},{24,216},{32,224},{40,232},{48,240},{56,2... | collective-permute-start | bytes 1572872 | tf_op jit(solution)/shard_map/ppermute | solution.py:420
  64.2 3.1 %copy-start.3 = (f32[68,16,128]{2,1,0:T(8,128)}, f32[68,16,128]{2,1,0:T(8,128)S(1)}, u32[]{:S(2)}) copy-start(f32[68,16,128]{2,1,0:T(8,128)S(1)} %collective-permute-done.5.refs_1_) | copy-start | bytes 1671172
  64.2 3.1 %copy-start.5 = (f32[68,16,128]{2,1,0:T(8,128)}, f32[68,16,128]{2,1,0:T(8,128)S(1)}, u32[]{:S(2)}) copy-start(f32[68,16,128]{2,1,0:T(8,128)S(1)} %collective-permute-done.10.refs_7_) | copy-start | bytes 1671172
  64.2 2.0 %copy-start = (f32[512,1024]{1,0:T(8,128)S(1)}, f32[512,1024]{1,0:T(8,128)}, u32[]{:S(2)}) copy-start(f32[512,1024]{1,0:T(8,128)} %all-gather.6.cloned.1.call-done) | copy-start | bytes 6291460
  66.2 13.6 %copy-start.10 = (f32[64,128,128]{2,1,0:T(8,128)S(1)}, f32[64,128,128]{2,1,0:T(8,128)}, u32[]{:S(2)}) copy-start(f32[64,128,128]{2,1,0:T(8,128)} %stored_hbm.3) | copy-start | bytes 12582916
  66.2 55.6 %copy-start.13 = (f32[1024]{0:T(1024)S(1)}, f32[1024]{0:T(1024)}, u32[]{:S(2)}) copy-start(f32[1024]{0:T(1024)} %param.21) | copy-start | bytes 12292
  66.2 55.6 %copy-start.14 = (f32[64]{0:T(128)S(1)}, f32[64]{0:T(128)}, u32[]{:S(2)}) copy-start(f32[64]{0:T(128)} %param.20) | copy-start | bytes 772
  67.3 22.1 %collective-permute-start.11 = (f32[2,64,1024]{2,1,0:T(8,128)S(1)}, f32[2,64,1024]{2,1,0:T(8,128)S(1)}, u32[]{:S(2)}, u32[]{:S(2)}) collective-permute-start(f32[2,64,1024]{2,1,0:T(8,128)S(1)} %outer.1), channel_id=1, source_target_pairs={{0,64},{8,72},{16,80},{24,88},{32,96},{40,104},{48,112},{56,120},{... | collective-permute-start | bytes 1572872 | tf_op jit(solution)/shard_map/ppermute | solution.py:426
  79.8 1.1 copy-start.2
  80.9 1.1 copy-start.4
  82.0 1.1 copy-start.6
  89.4 39.7 %copy-start.7 = (s32[64]{0:T(128)S(1)}, s32[64]{0:T(128)}, u32[]{:S(2)}) copy-start(s32[64]{0:T(128)} %rows.1) | copy-start | bytes 772
  89.4 39.7 %copy-start.8 = (s32[64]{0:T(128)S(1)}, s32[64]{0:T(128)}, u32[]{:S(2)}) copy-start(s32[64]{0:T(128)} %cols.1) | copy-start | bytes 772
  89.4 39.6 %copy-start.11 = (f32[64,1024]{1,0:T(8,128)S(1)}, f32[64,1024]{1,0:T(8,128)}, u32[]{:S(2)}) copy-start(f32[64,1024]{1,0:T(8,128)} %param.15) | copy-start | bytes 786436
  89.4 0.8 copy-start.9
  90.2 8.7 %collective-permute-start.12 = (f32[32,1024]{1,0:T(8,128)S(1)}, f32[32,1024]{1,0:T(8,128)S(1)}, u32[]{:S(2)}, u32[]{:S(2)}) collective-permute-start(f32[32,1024]{1,0:T(8,128)S(1)} %get-tuple-element.133), channel_id=1, source_target_pairs={{0,8},{8,16},{16,24},{24,32},{32,40},{40,48},{48,56},{56,0},{64,72... | collective-permute-start | bytes 393224 | tf_op jit(solution)/shard_map/ppermute | solution.py:393
  90.2 8.7 %collective-permute-start.13 = (f32[32,1024]{1,0:T(8,128)S(1)}, f32[32,1024]{1,0:T(8,128)S(1)}, u32[]{:S(2)}, u32[]{:S(2)}) collective-permute-start(f32[32,1024]{1,0:T(8,128)S(1)} %get-tuple-element.134), channel_id=1, source_target_pairs={{0,56},{8,0},{16,8},{24,16},{32,24},{40,32},{48,40},{56,48},{64,12... | collective-permute-start | bytes 393224 | tf_op jit(solution)/shard_map/ppermute | solution.py:394
  100.1 8.4 %collective-permute-start.14 = (f32[64,1024]{1,0:T(8,128)S(1)}, f32[64,1024]{1,0:T(8,128)S(1)}, u32[]{:S(2)}, u32[]{:S(2)}) collective-permute-start(f32[64,1024]{1,0:T(8,128)S(1)} %get-tuple-element.139), channel_id=1, source_target_pairs={{0,8},{8,16},{16,24},{24,32},{32,40},{40,48},{48,56},{56,0},{64,72... | collective-permute-start | bytes 786440 | tf_op jit(solution)/shard_map/ppermute | solution.py:393
  100.2 8.3 %collective-permute-start.15 = (f32[64,1024]{1,0:T(8,128)S(1)}, f32[64,1024]{1,0:T(8,128)S(1)}, u32[]{:S(2)}, u32[]{:S(2)}) collective-permute-start(f32[64,1024]{1,0:T(8,128)S(1)} %get-tuple-element.140), channel_id=1, source_target_pairs={{0,56},{8,0},{16,8},{24,16},{32,24},{40,32},{48,40},{56,48},{64,12... | collective-permute-start | bytes 786440 | tf_op jit(solution)/shard_map/ppermute | solution.py:394
  109.6 7.7 %collective-permute-start.16 = (f32[64,1024]{1,0:T(8,128)S(1)}, f32[64,1024]{1,0:T(8,128)S(1)}, u32[]{:S(2)}, u32[]{:S(2)}) collective-permute-start(f32[64,1024]{1,0:T(8,128)S(1)} %get-tuple-element.145), channel_id=1, source_target_pairs={{0,8},{8,16},{16,24},{24,32},{32,40},{40,48},{48,56},{56,0},{64,72... | collective-permute-start | bytes 786440 | tf_op jit(solution)/shard_map/ppermute | solution.py:393
  109.7 7.6 %collective-permute-start.17 = (f32[64,1024]{1,0:T(8,128)S(1)}, f32[64,1024]{1,0:T(8,128)S(1)}, u32[]{:S(2)}, u32[]{:S(2)}) collective-permute-start(f32[64,1024]{1,0:T(8,128)S(1)} %get-tuple-element.146), channel_id=1, source_target_pairs={{0,56},{8,0},{16,8},{24,16},{32,24},{40,32},{48,40},{56,48},{64,12... | collective-permute-start | bytes 786440 | tf_op jit(solution)/shard_map/ppermute | solution.py:394
  118.4 7.7 %collective-permute-start.18 = (f32[64,1024]{1,0:T(8,128)S(1)}, f32[64,1024]{1,0:T(8,128)S(1)}, u32[]{:S(2)}, u32[]{:S(2)}) collective-permute-start(f32[64,1024]{1,0:T(8,128)S(1)} %get-tuple-element.151), channel_id=1, source_target_pairs={{0,8},{8,16},{16,24},{24,32},{32,40},{40,48},{48,56},{56,0},{64,72... | collective-permute-start | bytes 786440 | tf_op jit(solution)/shard_map/ppermute | solution.py:393
  118.9 7.2 %collective-permute-start.19 = (f32[64,1024]{1,0:T(8,128)S(1)}, f32[64,1024]{1,0:T(8,128)S(1)}, u32[]{:S(2)}, u32[]{:S(2)}) collective-permute-start(f32[64,1024]{1,0:T(8,128)S(1)} %get-tuple-element.152), channel_id=1, source_target_pairs={{0,56},{8,0},{16,8},{24,16},{32,24},{40,32},{48,40},{56,48},{64,12... | collective-permute-start | bytes 786440 | tf_op jit(solution)/shard_map/ppermute | solution.py:394
  129.1 0.7 copy-start.12
Sparse Core Ops, SparseCore 0:
  9.3 44.2 all-gather.5

commit v4 on v3

--- a/solution.py
+++ b/solution.py
@@ -170,26 +170,26 @@
         for source in range(XS - 1):
             total = total + entries[source, 3, there].astype(jnp.int32)
         over = over | (total > TOTAL_CAP)
-    base = jnp.int32(0)
     for j in range(XS - 1):
         source = sources[j]
-        size = jnp.minimum(jnp.minimum(entries[j, 3, mine].astype(jnp.int32), CAP), TOTAL_CAP - base)
+        size = jnp.minimum(entries[j, 3, mine].astype(jnp.int32), CAP)
 
         def step(item, _):
             row = entries[j, 0, item].astype(jnp.int32)
             col = entries[j, 1, item].astype(jnp.int32)
-            out[base + item] = source[item]
-            kind = jnp.where(col - low >= HERE, 0, 1)
-            position = totals[kind]
+            far = col - low >= HERE
+            kind = jnp.where(far, 0, 1)
+            spot = jnp.minimum(totals[0] + totals[1], TOTAL_CAP - 1)
+            out[spot] = source[item]
+            position = jnp.minimum(totals[kind], TOTAL_CAP - 1)
             at = kind * LIST + position
-            table[0, at] = base + item
+            table[0, at] = spot
             table[1, at] = row
             table[2, at] = col
             totals[kind] = position + 1
             return 0
 
         lax.fori_loop(0, size, step, 0)
-        base = base + size
     totals[2] = over.astype(jnp.int32)
     pad_list(table, 0, totals[0], low)
     pad_list(table, LIST, totals[1], low)
@@ -218,111 +218,137 @@
     return high, (value - high.astype(jnp.float32)).astype(jnp.bfloat16)
 
 
-def products_of(low_tile, table, first, size, fetch, split, sums):
+def products_of(low_tile, table, first, size, load, left, tile, sums, first_block):
     blank = jnp.zeros((WIDTH, WIDTH), jnp.bfloat16)
 
     def step(group, _):
+        start = first + group * GROUP
+        load([table[0, start + member] for member in range(GROUP)])
+        rows = [left(member, table[1, start + member] - low_tile) for member in range(GROUP)]
         products = []
         for member in range(GROUP):
-            at = first + group * GROUP + member
-            high, low = split_of(fetch(member, table[0, at]))
+            high, low = split_of(tile[member])
             right = jnp.concatenate(
                 [jnp.concatenate([high, low], axis=1), jnp.concatenate([high, blank], axis=1)], axis=0
             )
-            product = jnp.dot(split[table[1, at] - low_tile], right, preferred_element_type=jnp.float32)
+            product = jnp.dot(rows[member], right, preferred_element_type=jnp.float32)
             products.append(product[:, :WIDTH] + product[:, WIDTH:])
         for member in range(GROUP):
-            col = table[2, first + group * GROUP + member] - low_tile
+            col = table[2, start + member] - low_tile
             lanes = pl.ds(pl.multiple_of(lax.rem(col, ZS) * WIDTH, WIDTH), WIDTH)
-            sums[lax.div(col, ZS), :, lanes] += products[member]
+            sums[lax.div(col, ZS) - first_block, :, lanes] += products[member]
         return 0
 
     lax.fori_loop(0, lax.div(size + GROUP - 1, GROUP), step, 0)
 
 
-def fill_split(split, source, first):
-    for block in range(source.shape[0]):
-        for part in range(ZS):
-            high, low = split_of(source[block, :, part * WIDTH:(part + 1) * WIDTH])
-            split[first + block * ZS + part, :, :WIDTH] = high
-            split[first + block * ZS + part, :, WIDTH:] = low
-
-
-def fetchers(place, stored, pieces, tile):
+def origins(place):
     my_y = lax.div(place[1], 2)
     my_core = lax.rem(place[1], 2)
-
-    def own(member, index):
-        return stored[index]
-
-    def moved(member, index):
-        for shift in range(YS):
-            for swapped in range(2):
-                core = my_core if swapped == 0 else 1 - my_core
-                origin = lax.rem(my_y - shift + YS, YS) * 2 + core
-                at = pl.multiple_of(origin * PIECE, PIECE)
-                tile[member, pl.ds(at, PIECE), :] = pieces[shift * 2 + swapped, index]
-        return tile[member]
-
-    return own, moved
-
-
-def outer_kernel(place, own, sizes, moved, totals, near_hbm, stored_hbm, *refs):
-    pieces_hbm, (out_hbm, near, stored, pieces, split, tile, sums, sems) = refs[:2 * YS], refs[2 * YS:]
+    rows = []
+    for shift in range(YS):
+        for swapped in range(2):
+            core = my_core if swapped == 0 else 1 - my_core
+            rows.append(pl.multiple_of((lax.rem(my_y - shift + YS, YS) * 2 + core) * PIECE, PIECE))
+    return rows
+
+
+def load_own(stored_hbm, tile, sems):
+    def load(indices):
+        copies = [
+            pltpu.make_async_copy(stored_hbm.at[indices[member]], tile.at[member], sems.at[member, 0])
+            for member in range(GROUP)
+        ]
+        for copy in copies:
+            copy.start()
+        for copy in copies:
+            copy.wait()
+
+    return load
+
+
+def outer_kernel(
+    place, own, sizes, moved, totals, near_hbm, stored_hbm, *refs
+):
+    pieces_hbm, (out_hbm, block, tile, sums, sems, end) = refs[:2 * YS], refs[2 * YS:]
     low_tile = place[0] * HERE
     sums[...] = jnp.zeros_like(sums)
-
-    @pl.when(sizes[0] + totals[0] > 0)
-    def _():
-        copies = [
-            pltpu.make_async_copy(near_hbm, near, sems.at[0]),
-            pltpu.make_async_copy(stored_hbm, stored, sems.at[1]),
-        ] + [pltpu.make_async_copy(pieces_hbm[k], pieces.at[k], sems.at[2 + k]) for k in range(2 * YS)]
+    rows_of = origins(place)
+
+    def load_far(indices):
+        copies = []
+        for member in range(GROUP):
+            for k in range(2 * YS):
+                copies.append(
+                    pltpu.make_async_copy(
+                        pieces_hbm[k].at[indices[member]],
+                        tile.at[member, pl.ds(rows_of[k], PIECE)],
+                        sems.at[member, k],
+                    )
+                )
         for copy in copies:
             copy.start()
-        copies[0].wait()
-        fill_split(split, near, 0)
-        fetch_own, fetch_moved = fetchers(place, stored, pieces, tile)
-        copies[1].wait()
-        products_of(low_tile, own, 0, sizes[0], fetch_own, split, sums)
-        for copy in copies[2:]:
+        for copy in copies:
             copy.wait()
-        products_of(low_tile, moved, 0, totals[0], fetch_moved, split, sums)
-
-    back = pltpu.make_async_copy(sums.at[pl.ds(ZS, 2)], out_hbm, sems.at[2 + 2 * YS])
+
+    def left(member, row):
+        lanes = pl.ds(pl.multiple_of(lax.rem(row, ZS) * WIDTH, WIDTH), WIDTH)
+        copy = pltpu.make_async_copy(near_hbm.at[lax.div(row, ZS), :, lanes], block.at[member], sems.at[member, 2 * YS])
+        copy.start()
+        copy.wait()
+        return jnp.concatenate(split_of(block[member]), axis=1)
+
+    products_of(low_tile, own, 0, sizes[0], load_own(stored_hbm, tile, sems), left, tile, sums, ZS)
+    products_of(low_tile, moved, 0, totals[0], load_far, left, tile, sums, ZS)
+    back = pltpu.make_async_copy(sums.at[pl.ds(0, 2)], out_hbm, end.at[0])
     back.start()
     back.wait()
 
 
 def inner_kernel(place, own, sizes, moved, totals, near_hbm, extra_hbm, stored_hbm, *refs):
     pieces_hbm, outs = refs[:2 * YS], refs[2 * YS:2 * YS + ZS + 1]
-    near, extra, stored, pieces, split, tile, sums, sems = refs[2 * YS + ZS + 1:]
+    near, extra, pieces, split, tile, sums, sems, tile_sems = refs[2 * YS + ZS + 1:]
     low_tile = place[0] * HERE
     copies = [
         pltpu.make_async_copy(near_hbm, near, sems.at[0]),
         pltpu.make_async_copy(extra_hbm, extra, sems.at[1]),
-        pltpu.make_async_copy(stored_hbm, stored, sems.at[2]),
-    ] + [pltpu.make_async_copy(pieces_hbm[k], pieces.at[k], sems.at[3 + k]) for k in range(2 * YS)]
+    ] + [pltpu.make_async_copy(pieces_hbm[k], pieces.at[k], sems.at[2 + k]) for k in range(2 * YS)]
     for copy in copies:
         copy.start()
     sums[...] = jnp.zeros_like(sums)
     copies[0].wait()
-    fill_split(split, near, 0)
+    for z in range(ZS):
+        for part in range(ZS):
+            high, low = split_of(near[z, :, part * WIDTH:(part + 1) * WIDTH])
+            split[z * ZS + part, :, :WIDTH] = high
+            split[z * ZS + part, :, WIDTH:] = low
     copies[1].wait()
-    fill_split(split, extra, HERE)
-    fetch_own, fetch_moved = fetchers(place, stored, pieces, tile)
-    copies[2].wait()
-    products_of(low_tile, own, XS * LIST, sizes[XS], fetch_own, split, sums)
-    for copy in copies[3:]:
+    for z in range(2):
+        for part in range(ZS):
+            high, low = split_of(extra[z, :, part * WIDTH:(part + 1) * WIDTH])
+            split[HERE + z * ZS + part, :, :WIDTH] = high
+            split[HERE + z * ZS + part, :, WIDTH:] = low
+    rows_of = origins(place)
+
+    def load_moved(indices):
+        for member in range(GROUP):
+            for k in range(2 * YS):
+                tile[member, pl.ds(rows_of[k], PIECE), :] = pieces[k, indices[member]]
+
+    def left(member, row):
+        return split[row]
+
+    products_of(low_tile, own, XS * LIST, sizes[XS], load_own(stored_hbm, tile, tile_sems), left, tile, sums, 0)
+    for copy in copies[2:]:
         copy.wait()
-    products_of(low_tile, moved, LIST, totals[1], fetch_moved, split, sums)
+    products_of(low_tile, moved, LIST, totals[1], load_moved, left, tile, sums, 0)
 
     @pl.when(totals[2] > 0)
     def _():
         sums[...] = jnp.full_like(sums, jnp.nan)
 
     half = near.shape[1] // 2
-    first_sem = 3 + 2 * YS
+    first_sem = 2 + 2 * YS
     backs = []
     for step in range(ZS + 1):
         block = lax.rem(place[2] + (step if step < ZS else ZS // 2), ZS)
@@ -338,30 +364,24 @@
         back.wait()
 
 
-def scratch_of(near, extra, integrals, sem_count):
-    _, rows_here, wide = near.shape
-    shapes = [near.shape] + ([extra.shape] if extra is not None else []) + [integrals.shape]
-    return [pltpu.VMEM(shape, jnp.float32) for shape in shapes] + [
-        pltpu.VMEM((2 * YS, TOTAL_CAP, PIECE, WIDTH), jnp.float32),
-        pltpu.VMEM((HERE + EXTRA, rows_here, 2 * WIDTH), jnp.bfloat16),
-        pltpu.VMEM((GROUP, WIDTH, WIDTH), jnp.float32),
-        pltpu.VMEM((ZS + 3, rows_here, wide), jnp.float32),
-        pltpu.SemaphoreType.DMA((sem_count,)),
-    ]
-
-
 def outer_sums(place, own, sizes, moved, totals, near, stored, pieces):
     _, rows_here, wide = near.shape
     smem = pl.BlockSpec(memory_space=pltpu.SMEM)
-    anywhere = pl.BlockSpec(memory_space=pl.ANY)
+    hbm = pl.BlockSpec(memory_space=pltpu.HBM)
     return pl.pallas_call(
         outer_kernel,
-        in_specs=[smem] * 5 + [anywhere] * (2 + 2 * YS),
-        out_specs=anywhere,
+        in_specs=[smem] * 5 + [hbm] * (2 + 2 * YS),
+        out_specs=pl.BlockSpec(memory_space=pl.ANY),
         out_shape=jax.ShapeDtypeStruct((2, rows_here, wide), jnp.float32),
-        scratch_shapes=scratch_of(near, None, stored, 3 + 2 * YS),
-        cost_estimate=pl.CostEstimate(flops=5 * 10**9, bytes_accessed=10**7, transcendentals=0),
-        compiler_params=pltpu.CompilerParams(vmem_limit_bytes=28 * 2**20),
+        scratch_shapes=[
+            pltpu.VMEM((GROUP, rows_here, WIDTH), jnp.float32),
+            pltpu.VMEM((GROUP, WIDTH, WIDTH), jnp.float32),
+            pltpu.VMEM((3, rows_here, wide), jnp.float32),
+            pltpu.SemaphoreType.DMA((GROUP, 2 * YS + 1)),
+            pltpu.SemaphoreType.DMA((1,)),
+        ],
+        cost_estimate=pl.CostEstimate(flops=10**6, bytes_accessed=10**4, transcendentals=0),
+        compiler_params=pltpu.CompilerParams(vmem_limit_bytes=4 * 2**20),
         name="outer",
     )(place, own, sizes, moved, totals, near, stored, *pieces)
 
@@ -369,16 +389,25 @@
 def inner_sums(place, own, sizes, moved, totals, near, extra, stored, pieces):
     _, rows_here, wide = near.shape
     smem = pl.BlockSpec(memory_space=pltpu.SMEM)
-    anywhere = pl.BlockSpec(memory_space=pl.ANY)
+    hbm = pl.BlockSpec(memory_space=pltpu.HBM)
     heights = [rows_here] * (ZS // 2) + [rows_here // 2] + [rows_here] * (ZS // 2 - 1) + [rows_here // 2]
     return pl.pallas_call(
         inner_kernel,
-        in_specs=[smem] * 5 + [anywhere] * (3 + 2 * YS),
-        out_specs=[anywhere] * (ZS + 1),
+        in_specs=[smem] * 5 + [hbm] * (3 + 2 * YS),
+        out_specs=[pl.BlockSpec(memory_space=pl.ANY)] * (ZS + 1),
         out_shape=[jax.ShapeDtypeStruct((height, wide), jnp.float32) for height in heights],
-        scratch_shapes=scratch_of(near, extra, stored, 3 + 2 * YS + ZS + 1),
+        scratch_shapes=[
+            pltpu.VMEM(near.shape, jnp.float32),
+            pltpu.VMEM(extra.shape, jnp.float32),
+            pltpu.VMEM((2 * YS, TOTAL_CAP, PIECE, WIDTH), jnp.float32),
+            pltpu.VMEM((HERE + EXTRA, rows_here, 2 * WIDTH), jnp.bfloat16),
+            pltpu.VMEM((GROUP, WIDTH, WIDTH), jnp.float32),
+            pltpu.VMEM((ZS + 3, rows_here, wide), jnp.float32),
+            pltpu.SemaphoreType.DMA((2 + 2 * YS + ZS + 1,)),
+            pltpu.SemaphoreType.DMA((GROUP, 1)),
+        ],
         cost_estimate=pl.CostEstimate(flops=10**10, bytes_accessed=10**7, transcendentals=0),
-        compiler_params=pltpu.CompilerParams(vmem_limit_bytes=28 * 2**20),
+        compiler_params=pltpu.CompilerParams(vmem_limit_bytes=18 * 2**20),
         name="inner",
     )(place, own, sizes, moved, totals, near, extra, stored, *pieces)
 
@@ -416,21 +445,21 @@
     arrived = [lax.ppermute(packed[step - 1], "tile", x_shift(step)) for step in range(1, XS)]
     mine, moved, totals = compact(place, sizes, arrived)
     along_y = [mine] + [lax.ppermute(mine, "pair", y_shift(step)) for step in range(1, YS)]
-    along_y[1], near = lax.optimization_barrier((along_y[1], near))
-    extra = lax.ppermute(near[:2], "tile", x_shift(-1))
-    pieces = []
-    for piece in along_y:
+    across = lax.ppermute(mine, "pair", CORE_SWAP)
+    along_y[YS - 1], across = lax.optimization_barrier((along_y[YS - 1], across))
+    first = near[:2]
+    extra = lax.ppermute(first, "tile", x_shift(-1))
+    along_y[1], along_y[2], first = lax.optimization_barrier((along_y[1], along_y[2], first))
+    pieces = [mine, across]
+    for piece in along_y[1:]:
         pieces += [piece, lax.ppermute(piece, "pair", CORE_SWAP)]
-
     beyond = outer_sums(place, own, sizes, moved, totals, near, integrals, pieces)
     from_left = lax.ppermute(beyond, "tile", x_shift(1))
     parts = inner_sums(place, own, sizes, moved, totals, near, extra, integrals, pieces)
 
     def more(step):
         block = lax.rem(my_z + step, ZS)
-        return jnp.where(
-            (my_x > 0) & (block == 0), from_left[0], jnp.where((my_x > 0) & (block == 1), from_left[1], 0.0)
-        )
+        return jnp.where(block == 0, from_left[0], jnp.where(block == 1, from_left[1], 0.0))
 
     ladder = ring_sum(parts, more)
     denominator = virt_energy[None, :] - pair_energy[:, None]

time: 138 us -> 139 us (level)
  starting transfers between devices: 29.3 us -> 27.1 us
  waiting for transfers between devices: 64.1 us -> 65.9 us
    ppermute x4, starting transfers between devices: 0.68 us -> 7.97 us  [ring_sum(): up = lax.ppermute(up, 'tile', z_shift(1))]
    ppermute x4, starting transfers between devices: 14.9 us -> 8 us  [ring_sum(): down = lax.ppermute(down, 'tile', z_shift(-1))]
    ppermute x1, starting transfers between devices: 3.31 us -> 0.95 us  [shards(): from_left = lax.ppermute(beyond, 'tile', x_shift(1))]
    ppermute x4, waiting for transfers between devices: 0.01 us -> 2.16 us  [ring_sum(): down = lax.ppermute(down, 'tile', z_shift(-1))]
    ppermute x1 -> x2, starting transfers between devices: 0.01 us -> 1.41 us  [the longest x1 1.32 us: shards(): extra = lax.ppermute(first, 'tile', x_shift(-1))]
    unnamed x30 -> x34, local copies, waits for them, and re-layouts: 6.56 us -> 7.91 us
    ppermute x1 -> x2, waiting for transfers between devices: 9.22 us -> 9.26 us  [the longest x1 9.26 us: shards(): extra = lax.ppermute(first, 'tile', x_shift(-1))]
  transfers between devices with their start and end apart: 21 -> 21, of which waited for: 10 -> 14; matrix products, arithmetic and copies ran while one was open for 2% -> 1% of each run, Pallas kernels for 10% -> 10%
where the time goes in v4:
time: 139 us
  waiting for transfers between devices  65.9 us (47%)
  starting transfers between devices  27.1 us (19%)
  between operations  15.5 us (11%)
  Pallas kernels  14.4 us (10%)
  local copies, waits for them, and re-layouts  10.3 us (7%)
  other arithmetic  5.49 us (4%)
    ppermute x3, waiting for transfers between devices, shards(): lax.ppermute(mine, 'pair', y_shift(step))  24.6 us
    ppermute x4, waiting for transfers between devices, ring_sum(): up = lax.ppermute(up, 'tile', z_shift(1))  15.9 us
    ppermute x3, waiting for transfers between devices, shards(): lax.ppermute(packed[step - 1], 'tile', x_shift(step))  12.2 us
    ppermute x1, waiting for transfers between devices, shards(): extra = lax.ppermute(first, 'tile', x_shift(-1))  9.26 us
    ppermute x4, starting transfers between devices, ring_sum(): down = lax.ppermute(down, 'tile', z_shift(-1))  8 us
    ppermute x4, starting transfers between devices, ring_sum(): up = lax.ppermute(up, 'tile', z_shift(1))  7.97 us
    unnamed x34, local copies, waits for them, and re-layouts  7.91 us
    pallas_call x1, Pallas kernels, inner_sums(): pl.pallas_call(inner_kernel, in_specs=[smem] * 5 + [hbm] * (3 + 2 * YS),...  7 us
  transfers between devices with their start and end apart: 21, of which 14 were waited for; matrix products, arithmetic and copies ran while one was open for 1% of the time, Pallas kernels for 10%

profile of v4, /device:TPU:6, one launch (start us, length us, event | category | flops | bytes accessed | tf_op | source)
XLA Modules:
  0.0 138.7 jit_solution(11689203443931222351)
XLA Ops:
  6.5 0.7 all-gather.6.cloned.1.call-update
  8.0 3.4 %pack.1 = (f32[33,16,128]{2,1,0:T(8,128)S(1)}, f32[33,16,128]{2,1,0:T(8,128)S(1)}, f32[33,16,128]{2,1,0:T(8,128)S(1)}, s32[3,360]{1,0:T(4,128)S(1)}, s32[8]{0:T(128)S(1)}) custom-call(s32[3]{0:T(128)S(1)} %pad_add_fusion.place, s32[64]{0:T(128)} %rows.1, s32[64]{0:T(128)} %cols.1, s32[1]{0:T(128)S(6)} %copy.30.count, f32[64,128,128]{2,1,0:T(8,128)} %stored_hbm.3), custom_call_target="tpu_custom_call" | custom-call | tf_op jit(solution)/shard_map/pack/pallas_call | solution.py:141
  11.4 2.2 %collective-permute-start = (f32[33,16,128]{2,1,0:T(8,128)S(1)}, f32[33,16,128]{2,1,0:T(8,128)S(1)}, u32[]{:S(2)}, u32[]{:S(2)}) collective-permute-start(f32[33,16,128]{2,1,0:T(8,128)S(1)} %get-tuple-element.124), channel_id=1, source_target_pairs={{0,64},{8,72},{16,80},{24,88},{32,96},{40,104},{48,112},{56,120},{... | collective-permute-start | bytes 811016 | tf_op jit(solution)/shard_map/ppermute | solution.py:445
  13.5 1.3 collective-permute-start.1
  14.9 5.9 %collective-permute-done.refs_0_ = f32[33,16,128]{2,1,0:T(8,128)S(1)} collective-permute-done((f32[33,16,128]{2,1,0:T(8,128)S(1)}, f32[33,16,128]{2,1,0:T(8,128)S(1)}, u32[]{:S(2)}, u32[]{:S(2)}) %collective-permute-start) | collective-permute-done | bytes 270368 | tf_op jit(solution)/shard_map/ppermute | solution.py:445
  20.8 3.4 %collective-permute-done.1.refs_1_ = f32[33,16,128]{2,1,0:T(8,128)S(1)} collective-permute-done((f32[33,16,128]{2,1,0:T(8,128)S(1)}, f32[33,16,128]{2,1,0:T(8,128)S(1)}, u32[]{:S(2)}, u32[]{:S(2)}) %collective-permute-start.1) | collective-permute-done | bytes 270368 | tf_op jit(solution)/shard_map/ppermute | solution.py:445
  24.2 2.9 %collective-permute-done.2.refs_2_ = f32[33,16,128]{2,1,0:T(8,128)S(1)} collective-permute-done((f32[33,16,128]{2,1,0:T(8,128)S(1)}, f32[33,16,128]{2,1,0:T(8,128)S(1)}, u32[]{:S(2)}, u32[]{:S(2)}) %collective-permute-start.2) | collective-permute-done | bytes 270368 | tf_op jit(solution)/shard_map/ppermute | solution.py:445
  27.1 2.8 %compact.1 = (f32[68,16,128]{2,1,0:T(8,128)S(1)}, s32[3,144]{1,0:T(4,128)S(1)}, s32[8]{0:T(128)S(1)}) custom-call(s32[3]{0:T(128)S(1)} %pad_add_fusion.place, s32[8]{0:T(128)S(1)} %get-tuple-element.123.sizes, f32[33,16,128]{2,1,0:T(8,128)S(1)} %collective-permute-done.refs_0_, f32[33,16,128]{2,1,0:T(8,128)S(1)} %collective-permute-done.1.refs_1_, ...), custom_call_target="tpu_custom_call" | custom-call | tf_op jit(solution)/shard_map/compact/pallas_call | solution.py:201
  30.0 3.1 %collective-permute-start.4 = (f32[68,16,128]{2,1,0:T(8,128)S(1)}, f32[68,16,128]{2,1,0:T(8,128)S(1)}, u32[]{:S(2)}, u32[]{:S(2)}) collective-permute-start(f32[68,16,128]{2,1,0:T(8,128)S(1)} %get-tuple-element.129.refs_0_), channel_id=1, source_target_pairs={{0,6},{1,7},{2,0},{3,1},{4,2},{5,3},{6,4},{7,5},{8,14},{9,15},{10,... | collective-permute-start | bytes 1671176 | tf_op jit(solution)/shard_map/ppermute | solution.py:447
  33.1 0.6 collective-permute-start.7
  33.7 1.0 collective-permute-start.6
  34.7 22.8 %collective-permute-done.4.refs_6_ = f32[68,16,128]{2,1,0:T(8,128)S(1)} collective-permute-done((f32[68,16,128]{2,1,0:T(8,128)S(1)}, f32[68,16,128]{2,1,0:T(8,128)S(1)}, u32[]{:S(2)}, u32[]{:S(2)}) %collective-permute-start.4) | collective-permute-done | bytes 557088 | tf_op jit(solution)/shard_map/ppermute | solution.py:447
  57.5 1.9 %slice.55 = f32[128,1024]{1,0:T(8,128)} slice(f32[512,1024]{1,0:T(8,128)} %all-gather.6.cloned.1.call-done), slice={[0:128], [0:1024]} | slice | bytes 1048576 | tf_op jit(solution)/shard_map/slice | solution.py:450
  59.4 1.8 %collective-permute-done.6.refs_2_ = f32[68,16,128]{2,1,0:T(8,128)S(1)} collective-permute-done((f32[68,16,128]{2,1,0:T(8,128)S(1)}, f32[68,16,128]{2,1,0:T(8,128)S(1)}, u32[]{:S(2)}, u32[]{:S(2)}) %collective-permute-start.6) | collective-permute-done | bytes 557088 | tf_op jit(solution)/shard_map/ppermute | solution.py:447
  61.3 0.5 collective-permute-start.9
  61.7 1.3 collective-permute-start.3
  63.3 0.8 collective-permute-done.9.refs_5_
  64.1 1.6 %copy-done = f32[512,1024]{1,0:T(8,128)S(1)} copy-done((f32[512,1024]{1,0:T(8,128)S(1)}, f32[512,1024]{1,0:T(8,128)}, u32[]{:S(2)}) %copy-start) | copy-done | bytes 2097176
  65.7 1.2 outer.1
  66.9 1.0 collective-permute-start.11
  67.9 9.3 %collective-permute-done.3.extra_hbm = f32[2,64,1024]{2,1,0:T(8,128)} collective-permute-done((f32[2,64,1024]{2,1,0:T(8,128)}, f32[2,64,1024]{2,1,0:T(8,128)}, u32[]{:S(2)}, u32[]{:S(2)}) %collective-permute-start.3) | collective-permute-done | bytes 524320 | tf_op jit(solution)/shard_map/ppermute | solution.py:451
  77.1 7.0 %inner.1 = (f32[64,1024]{1,0:T(8,128)S(1)}, f32[64,1024]{1,0:T(8,128)S(1)}, f32[64,1024]{1,0:T(8,128)S(1)}, f32[64,1024]{1,0:T(8,128)S(1)}, f32[32,1024]{1,0:T(8...) custom-call(s32[3]{0:T(128)S(1)} %pad_add_fusion.place, ...), custom_call_target="tpu_custom_call" | custom-call | flops 10000000000 | bytes 10000000 | tf_op jit(solution)/shard_map/inner/pallas_call | solution.py:394
  84.1 0.7 copy-done.2
  84.8 0.7 copy-done.3
  85.5 0.7 copy-done.4
  86.2 0.7 copy-done.5
  86.9 0.7 copy-done.6
  87.6 0.7 copy-done.7
  88.3 0.7 copy-done.8
  89.1 0.7 copy-done.12
  89.8 3.2 %collective-permute-start.12 = (f32[32,1024]{1,0:T(8,128)S(1)}, f32[32,1024]{1,0:T(8,128)S(1)}, u32[]{:S(2)}, u32[]{:S(2)}) collective-permute-start(f32[32,1024]{1,0:T(8,128)S(1)} %get-tuple-element.137), channel_id=1, source_target_pairs={{0,8},{8,16},{16,24},{24,32},{32,40},{40,48},{48,56},{56,0},{64,72... | collective-permute-start | bytes 393224 | tf_op jit(solution)/shard_map/ppermute | solution.py:422
  93.0 2.8 %collective-permute-start.13 = (f32[32,1024]{1,0:T(8,128)S(1)}, f32[32,1024]{1,0:T(8,128)S(1)}, u32[]{:S(2)}, u32[]{:S(2)}) collective-permute-start(f32[32,1024]{1,0:T(8,128)S(1)} %get-tuple-element.138), channel_id=1, source_target_pairs={{0,56},{8,0},{16,8},{24,16},{32,24},{40,32},{48,40},{56,48},{64,12... | collective-permute-start | bytes 393224 | tf_op jit(solution)/shard_map/ppermute | solution.py:423
  95.8 2.9 %collective-permute-done.12 = f32[32,1024]{1,0:T(8,128)S(1)} collective-permute-done((f32[32,1024]{1,0:T(8,128)S(1)}, f32[32,1024]{1,0:T(8,128)S(1)}, u32[]{:S(2)}, u32[]{:S(2)}) %collective-permute-start.12) | collective-permute-done | bytes 131104 | tf_op jit(solution)/shard_map/ppermute | solution.py:422
  98.7 1.3 bitcast_add_fusion.4
  100.1 3.3 %collective-permute-start.15 = (f32[64,1024]{1,0:T(8,128)S(1)}, f32[64,1024]{1,0:T(8,128)S(1)}, u32[]{:S(2)}, u32[]{:S(2)}) collective-permute-start(f32[64,1024]{1,0:T(8,128)S(1)} %get-tuple-element.144), channel_id=1, source_target_pairs={{0,56},{8,0},{16,8},{24,16},{32,24},{40,32},{48,40},{56,48},{64,12... | collective-permute-start | bytes 786440 | tf_op jit(solution)/shard_map/ppermute | solution.py:423
  103.4 4.4 %collective-permute-done.14 = f32[64,1024]{1,0:T(8,128)S(1)} collective-permute-done((f32[64,1024]{1,0:T(8,128)S(1)}, f32[64,1024]{1,0:T(8,128)S(1)}, u32[]{:S(2)}, u32[]{:S(2)}) %collective-permute-start.14) | collective-permute-done | bytes 262176 | tf_op jit(solution)/shard_map/ppermute | solution.py:422
  107.8 1.3 bitcast_add_fusion.2
  109.2 1.9 %collective-permute-start.16 = (f32[64,1024]{1,0:T(8,128)S(1)}, f32[64,1024]{1,0:T(8,128)S(1)}, u32[]{:S(2)}, u32[]{:S(2)}) collective-permute-start(f32[64,1024]{1,0:T(8,128)S(1)} %get-tuple-element.149), channel_id=1, source_target_pairs={{0,8},{8,16},{16,24},{24,32},{32,40},{40,48},{48,56},{56,0},{64,72... | collective-permute-start | bytes 786440 | tf_op jit(solution)/shard_map/ppermute | solution.py:422
  111.0 1.5 %collective-permute-start.17 = (f32[64,1024]{1,0:T(8,128)S(1)}, f32[64,1024]{1,0:T(8,128)S(1)}, u32[]{:S(2)}, u32[]{:S(2)}) collective-permute-start(f32[64,1024]{1,0:T(8,128)S(1)} %get-tuple-element.150), channel_id=1, source_target_pairs={{0,56},{8,0},{16,8},{24,16},{32,24},{40,32},{48,40},{56,48},{64,12... | collective-permute-start | bytes 786440 | tf_op jit(solution)/shard_map/ppermute | solution.py:423
  112.5 4.3 %collective-permute-done.16 = f32[64,1024]{1,0:T(8,128)S(1)} collective-permute-done((f32[64,1024]{1,0:T(8,128)S(1)}, f32[64,1024]{1,0:T(8,128)S(1)}, u32[]{:S(2)}, u32[]{:S(2)}) %collective-permute-start.16) | collective-permute-done | bytes 262176 | tf_op jit(solution)/shard_map/ppermute | solution.py:422
  116.8 0.6 collective-permute-done.17
  117.4 1.3 bitcast_add_fusion
  118.8 2.9 %collective-permute-start.18 = (f32[64,1024]{1,0:T(8,128)S(1)}, f32[64,1024]{1,0:T(8,128)S(1)}, u32[]{:S(2)}, u32[]{:S(2)}) collective-permute-start(f32[64,1024]{1,0:T(8,128)S(1)} %get-tuple-element.155), channel_id=1, source_target_pairs={{0,8},{8,16},{16,24},{24,32},{32,40},{40,48},{48,56},{56,0},{64,72... | collective-permute-start | bytes 786440 | tf_op jit(solution)/shard_map/ppermute | solution.py:422
  122.2 4.2 %collective-permute-done.18 = f32[64,1024]{1,0:T(8,128)S(1)} collective-permute-done((f32[64,1024]{1,0:T(8,128)S(1)}, f32[64,1024]{1,0:T(8,128)S(1)}, u32[]{:S(2)}, u32[]{:S(2)}) %collective-permute-start.18) | collective-permute-done | bytes 262176 | tf_op jit(solution)/shard_map/ppermute | solution.py:422
  126.4 1.6 %collective-permute-done.19 = f32[64,1024]{1,0:T(8,128)S(1)} collective-permute-done((f32[64,1024]{1,0:T(8,128)S(1)}, f32[64,1024]{1,0:T(8,128)S(1)}, u32[]{:S(2)}, u32[]{:S(2)}) %collective-permute-start.19) | collective-permute-done | bytes 262176 | tf_op jit(solution)/shard_map/ppermute | solution.py:423
  128.0 1.2 fusion.11
  129.2 0.5 slice.60
  131.2 0.7 copy-done.14
  (45 shorter events, 1.3 us)
Async XLA Ops:
  6.5 51.0 %all-gather.6.cloned.1.call-start = ((), (), s32[]{:S(2)}) async-start(), calls=%async_computation.3 | async-start | bytes 2359296 | tf_op jit(solution)/shard_map/all_gather | solution.py:442
  11.4 9.4 %collective-permute-start = (f32[33,16,128]{2,1,0:T(8,128)S(1)}, f32[33,16,128]{2,1,0:T(8,128)S(1)}, u32[]{:S(2)}, u32[]{:S(2)}) collective-permute-start(f32[33,16,128]{2,1,0:T(8,128)S(1)} %get-tuple-element.124), channel_id=1, source_target_pairs={{0,64},{8,72},{16,80},{24,88},{32,96},{40,104},{48,112},{56,120},{... | collective-permute-start | bytes 811016 | tf_op jit(solution)/shard_map/ppermute | solution.py:445
  13.5 10.7 %collective-permute-start.1 = (f32[33,16,128]{2,1,0:T(8,128)S(1)}, f32[33,16,128]{2,1,0:T(8,128)S(1)}, u32[]{:S(2)}, u32[]{:S(2)}) collective-permute-start(f32[33,16,128]{2,1,0:T(8,128)S(1)} %get-tuple-element.125), channel_id=1, source_target_pairs={{0,128},{8,136},{16,144},{24,152},{32,160},{40,168},{48,176},{56,1... | collective-permute-start | bytes 811016 | tf_op jit(solution)/shard_map/ppermute | solution.py:445
  14.9 12.2 %collective-permute-start.2 = (f32[33,16,128]{2,1,0:T(8,128)S(1)}, f32[33,16,128]{2,1,0:T(8,128)S(1)}, u32[]{:S(2)}, u32[]{:S(2)}) collective-permute-start(f32[33,16,128]{2,1,0:T(8,128)S(1)} %get-tuple-element.126), channel_id=1, source_target_pairs={{0,192},{8,200},{16,208},{24,216},{32,224},{40,232},{48,240},{56,2... | collective-permute-start | bytes 811016 | tf_op jit(solution)/shard_map/ppermute | solution.py:445
  29.9 4.8 %collective-permute-start.5 = (f32[68,16,128]{2,1,0:T(8,128)S(1)}, f32[68,16,128]{2,1,0:T(8,128)S(1)}, u32[]{:S(2)}, u32[]{:S(2)}) collective-permute-start(f32[68,16,128]{2,1,0:T(8,128)S(1)} %get-tuple-element.129.refs_0_), channel_id=1, source_target_pairs={{0,1},{1,0},{2,3},{3,2},{4,5},{5,4},{6,7},{7,6},{8,9},{9,8},{10,11... | collective-permute-start | bytes 1671176 | tf_op jit(solution)/shard_map/ppermute | solution.py:448
  30.0 27.5 %collective-permute-start.4 = (f32[68,16,128]{2,1,0:T(8,128)S(1)}, f32[68,16,128]{2,1,0:T(8,128)S(1)}, u32[]{:S(2)}, u32[]{:S(2)}) collective-permute-start(f32[68,16,128]{2,1,0:T(8,128)S(1)} %get-tuple-element.129.refs_0_), channel_id=1, source_target_pairs={{0,6},{1,7},{2,0},{3,1},{4,2},{5,3},{6,4},{7,5},{8,14},{9,15},{10,... | collective-permute-start | bytes 1671176 | tf_op jit(solution)/shard_map/ppermute | solution.py:447
  33.1 26.3 %collective-permute-start.7 = (f32[68,16,128]{2,1,0:T(8,128)S(1)}, f32[68,16,128]{2,1,0:T(8,128)S(1)}, u32[]{:S(2)}, u32[]{:S(2)}) collective-permute-start(f32[68,16,128]{2,1,0:T(8,128)S(1)} %get-tuple-element.129.refs_0_), channel_id=1, source_target_pairs={{0,4},{1,5},{2,6},{3,7},{4,0},{5,1},{6,2},{7,3},{8,12},{9,13},{10,... | collective-permute-start | bytes 1671176 | tf_op jit(solution)/shard_map/ppermute | solution.py:447
  33.7 27.5 %collective-permute-start.6 = (f32[68,16,128]{2,1,0:T(8,128)S(1)}, f32[68,16,128]{2,1,0:T(8,128)S(1)}, u32[]{:S(2)}, u32[]{:S(2)}) collective-permute-start(f32[68,16,128]{2,1,0:T(8,128)S(1)} %get-tuple-element.129.refs_0_), channel_id=1, source_target_pairs={{0,2},{1,3},{2,4},{3,5},{4,6},{5,7},{6,0},{7,1},{8,10},{9,11},{10,... | collective-permute-start | bytes 1671176 | tf_op jit(solution)/shard_map/ppermute | solution.py:447
  57.5 5.5 %collective-permute-start.10 = (f32[68,16,128]{2,1,0:T(8,128)S(1)}, f32[68,16,128]{2,1,0:T(8,128)S(1)}, u32[]{:S(2)}, u32[]{:S(2)}) collective-permute-start(f32[68,16,128]{2,1,0:T(8,128)S(1)} %collective-permute-done.4.refs_6_), channel_id=1, source_target_pairs={{0,1},{1,0},{2,3},{3,2},{4,5},{5,4},{6,7},{7,6},{8,9},{9,8},{10,11... | collective-permute-start | bytes 1671176 | tf_op jit(solution)/shard_map/ppermute | solution.py:455
  61.2 2.1 %collective-permute-start.8 = (f32[68,16,128]{2,1,0:T(8,128)S(1)}, f32[68,16,128]{2,1,0:T(8,128)}, u32[]{:S(2)}, u32[]{:S(2)}) collective-permute-start(f32[68,16,128]{2,1,0:T(8,128)S(1)} %collective-permute-done.6.refs_2_), channel_id=1, source_target_pairs={{0,1},{1,0},{2,3},{3,2},{4,5},{5,4},{6,7},{7,6},{8,9},{9,8},{10,11... | collective-permute-start | bytes 1671176 | tf_op jit(solution)/shard_map/ppermute | solution.py:455
  61.3 2.9 %collective-permute-start.9 = (f32[68,16,128]{2,1,0:T(8,128)S(1)}, f32[68,16,128]{2,1,0:T(8,128)}, u32[]{:S(2)}, u32[]{:S(2)}) collective-permute-start(f32[68,16,128]{2,1,0:T(8,128)S(1)} %collective-permute-done.7.refs_4_), channel_id=1, source_target_pairs={{0,1},{1,0},{2,3},{3,2},{4,5},{5,4},{6,7},{7,6},{8,9},{9,8},{10,11... | collective-permute-start | bytes 1671176 | tf_op jit(solution)/shard_map/ppermute | solution.py:455
  61.7 15.4 %collective-permute-start.3 = (f32[2,64,1024]{2,1,0:T(8,128)}, f32[2,64,1024]{2,1,0:T(8,128)}, u32[]{:S(2)}, u32[]{:S(2)}) collective-permute-start(f32[2,64,1024]{2,1,0:T(8,128)} %bitcast.8), channel_id=1, source_target_pairs={{0,192},{8,200},{16,208},{24,216},{32,224},{40,232},{48,240},{56,2... | collective-permute-start | bytes 1572872 | tf_op jit(solution)/shard_map/ppermute | solution.py:451
  64.1 1.6 %copy-start = (f32[512,1024]{1,0:T(8,128)S(1)}, f32[512,1024]{1,0:T(8,128)}, u32[]{:S(2)}) copy-start(f32[512,1024]{1,0:T(8,128)} %all-gather.6.cloned.1.call-done) | copy-start | bytes 6291460
  65.7 11.4 %copy-start.1 = (f32[512,1024]{1,0:T(8,128)S(1)}, f32[512,1024]{1,0:T(8,128)}, u32[]{:S(2)}) copy-start(f32[512,1024]{1,0:T(8,128)} %all-gather.6.cloned.1.call-done) | copy-start | bytes 6291460
  65.7 11.4 %copy-start.11 = (f32[64,128,128]{2,1,0:T(8,128)S(1)}, f32[64,128,128]{2,1,0:T(8,128)}, u32[]{:S(2)}) copy-start(f32[64,128,128]{2,1,0:T(8,128)} %stored_hbm.3) | copy-start | bytes 12582916
  66.9 55.2 %copy-start.15 = (f32[1024]{0:T(1024)S(1)}, f32[1024]{0:T(1024)}, u32[]{:S(2)}) copy-start(f32[1024]{0:T(1024)} %param.21) | copy-start | bytes 12292
  66.9 55.2 %copy-start.16 = (f32[64]{0:T(128)S(1)}, f32[64]{0:T(128)}, u32[]{:S(2)}) copy-start(f32[64]{0:T(128)} %param.20) | copy-start | bytes 772
  66.9 22.1 %collective-permute-start.11 = (f32[2,64,1024]{2,1,0:T(8,128)S(1)}, f32[2,64,1024]{2,1,0:T(8,128)S(1)}, u32[]{:S(2)}, u32[]{:S(2)}) collective-permute-start(f32[2,64,1024]{2,1,0:T(8,128)S(1)} %outer.1), channel_id=1, source_target_pairs={{0,64},{8,72},{16,80},{24,88},{32,96},{40,104},{48,112},{56,120},{... | collective-permute-start | bytes 1572872 | tf_op jit(solution)/shard_map/ppermute | solution.py:457
  84.1 0.7 copy-start.2
  84.8 0.7 copy-start.3
  85.5 0.7 copy-start.4
  86.2 0.7 copy-start.5
  86.9 0.7 copy-start.6
  87.6 0.7 copy-start.7
  88.3 0.7 copy-start.8
  89.0 42.0 %copy-start.9 = (s32[64]{0:T(128)S(1)}, s32[64]{0:T(128)}, u32[]{:S(2)}) copy-start(s32[64]{0:T(128)} %rows.1) | copy-start | bytes 772
  89.0 42.0 %copy-start.10 = (s32[64]{0:T(128)S(1)}, s32[64]{0:T(128)}, u32[]{:S(2)}) copy-start(s32[64]{0:T(128)} %cols.1) | copy-start | bytes 772
  89.0 42.0 %copy-start.13 = (f32[64,1024]{1,0:T(8,128)S(1)}, f32[64,1024]{1,0:T(8,128)}, u32[]{:S(2)}) copy-start(f32[64,1024]{1,0:T(8,128)} %param.15) | copy-start | bytes 786436
  89.1 0.8 copy-start.12
  89.8 8.9 %collective-permute-start.12 = (f32[32,1024]{1,0:T(8,128)S(1)}, f32[32,1024]{1,0:T(8,128)S(1)}, u32[]{:S(2)}, u32[]{:S(2)}) collective-permute-start(f32[32,1024]{1,0:T(8,128)S(1)} %get-tuple-element.137), channel_id=1, source_target_pairs={{0,8},{8,16},{16,24},{24,32},{32,40},{40,48},{48,56},{56,0},{64,72... | collective-permute-start | bytes 393224 | tf_op jit(solution)/shard_map/ppermute | solution.py:422
  93.0 5.7 %collective-permute-start.13 = (f32[32,1024]{1,0:T(8,128)S(1)}, f32[32,1024]{1,0:T(8,128)S(1)}, u32[]{:S(2)}, u32[]{:S(2)}) collective-permute-start(f32[32,1024]{1,0:T(8,128)S(1)} %get-tuple-element.138), channel_id=1, source_target_pairs={{0,56},{8,0},{16,8},{24,16},{32,24},{40,32},{48,40},{56,48},{64,12... | collective-permute-start | bytes 393224 | tf_op jit(solution)/shard_map/ppermute | solution.py:423
  100.0 7.8 %collective-permute-start.14 = (f32[64,1024]{1,0:T(8,128)S(1)}, f32[64,1024]{1,0:T(8,128)S(1)}, u32[]{:S(2)}, u32[]{:S(2)}) collective-permute-start(f32[64,1024]{1,0:T(8,128)S(1)} %get-tuple-element.143), channel_id=1, source_target_pairs={{0,8},{8,16},{16,24},{24,32},{32,40},{40,48},{48,56},{56,0},{64,72... | collective-permute-start | bytes 786440 | tf_op jit(solution)/shard_map/ppermute | solution.py:422
  100.1 7.7 %collective-permute-start.15 = (f32[64,1024]{1,0:T(8,128)S(1)}, f32[64,1024]{1,0:T(8,128)S(1)}, u32[]{:S(2)}, u32[]{:S(2)}) collective-permute-start(f32[64,1024]{1,0:T(8,128)S(1)} %get-tuple-element.144), channel_id=1, source_target_pairs={{0,56},{8,0},{16,8},{24,16},{32,24},{40,32},{48,40},{56,48},{64,12... | collective-permute-start | bytes 786440 | tf_op jit(solution)/shard_map/ppermute | solution.py:423
  109.2 7.7 %collective-permute-start.16 = (f32[64,1024]{1,0:T(8,128)S(1)}, f32[64,1024]{1,0:T(8,128)S(1)}, u32[]{:S(2)}, u32[]{:S(2)}) collective-permute-start(f32[64,1024]{1,0:T(8,128)S(1)} %get-tuple-element.149), channel_id=1, source_target_pairs={{0,8},{8,16},{16,24},{24,32},{32,40},{40,48},{48,56},{56,0},{64,72... | collective-permute-start | bytes 786440 | tf_op jit(solution)/shard_map/ppermute | solution.py:422
  111.0 6.4 %collective-permute-start.17 = (f32[64,1024]{1,0:T(8,128)S(1)}, f32[64,1024]{1,0:T(8,128)S(1)}, u32[]{:S(2)}, u32[]{:S(2)}) collective-permute-start(f32[64,1024]{1,0:T(8,128)S(1)} %get-tuple-element.150), channel_id=1, source_target_pairs={{0,56},{8,0},{16,8},{24,16},{32,24},{40,32},{48,40},{56,48},{64,12... | collective-permute-start | bytes 786440 | tf_op jit(solution)/shard_map/ppermute | solution.py:423
  118.8 7.7 %collective-permute-start.18 = (f32[64,1024]{1,0:T(8,128)S(1)}, f32[64,1024]{1,0:T(8,128)S(1)}, u32[]{:S(2)}, u32[]{:S(2)}) collective-permute-start(f32[64,1024]{1,0:T(8,128)S(1)} %get-tuple-element.155), channel_id=1, source_target_pairs={{0,8},{8,16},{16,24},{24,32},{32,40},{40,48},{48,56},{56,0},{64,72... | collective-permute-start | bytes 786440 | tf_op jit(solution)/shard_map/ppermute | solution.py:422
  121.6 6.4 %collective-permute-start.19 = (f32[64,1024]{1,0:T(8,128)S(1)}, f32[64,1024]{1,0:T(8,128)S(1)}, u32[]{:S(2)}, u32[]{:S(2)}) collective-permute-start(f32[64,1024]{1,0:T(8,128)S(1)} %get-tuple-element.156), channel_id=1, source_target_pairs={{0,56},{8,0},{16,8},{24,16},{32,24},{40,32},{48,40},{56,48},{64,12... | collective-permute-start | bytes 786440 | tf_op jit(solution)/shard_map/ppermute | solution.py:423
  131.1 0.7 copy-start.14
Sparse Core Ops, SparseCore 0:
  9.3 44.2 all-gather.5

commit v5 on v3

v5 whole, which is shorter than its diff:
```python
import jax
import jax.numpy as jnp
from jax import lax
from jax.experimental import pallas as pl
from jax.experimental.pallas import tpu as pltpu
from jax.sharding import PartitionSpec as P

XS = 4
ZS = 8
YS = 4
CAP = 32
TOTAL_CAP = 68
LIST = 72
GROUP = 4
EXTRA = 16
ROUND = 16
LIMIT = 56
HERE = 64
PIECE = 16
WIDTH = 128

Z_GROUPS = [[x * ZS + z for z in range(ZS)] for x in range(XS)]


def x_shift(step):
    return [(x * ZS + z, ((x + step) % XS) * ZS + z) for x in range(XS) for z in range(ZS)]


def z_shift(step):
    return [(x * ZS + z, x * ZS + (z + step) % ZS) for x in range(XS) for z in range(ZS)]


def y_shift(step):
    return [(y * 2 + core, ((y + step) % YS) * 2 + core) for y in range(YS) for core in range(2)]


CORE_SWAP = [(y * 2 + core, y * 2 + 1 - core) for y in range(YS) for core in range(2)]


def contract(blocks, stored, row_list, col_list, live_count):
    tile_width = stored.shape[1]
    group_size = 8
    slot_total = stored.shape[0]
    rows_here = blocks.shape[0]
    groups = (live_count + group_size - 1) // group_size

    def group_step(group, totals):
        index_list = group * group_size + jnp.arange(group_size, dtype=jnp.int32)
        safe_index = jnp.minimum(index_list, slot_total - 1)
        pieces = jnp.take(stored, safe_index, axis=0)
        row_ids = jnp.take(row_list, safe_index, axis=0)
        col_ids = jnp.take(col_list, safe_index, axis=0)
        active = (index_list < live_count).astype(jnp.float32)
        inputs = jnp.take(blocks, row_ids, axis=1)
        product = jnp.einsum("pgk,gkn->pgn", inputs, pieces, precision=lax.Precision.HIGHEST)
        product = product * active[None, :, None]
        return totals.at[:, col_ids, :].add(product)

    start_totals = jnp.zeros((rows_here, blocks.shape[1], tile_width), jnp.float32)
    return lax.fori_loop(0, groups, group_step, start_totals)


def dense_ladder(amplitudes, integrals, tile_rows, tile_cols, tile_count):
    rows_here = amplitudes.shape[0]
    columns_all = amplitudes.shape[1] * lax.axis_size("tile")
    gathered = lax.all_gather(amplitudes, "tile", axis=1, tiled=True)
    blocks = gathered.reshape(rows_here, columns_all // WIDTH, WIDTH)
    partial_value = contract(blocks, integrals, tile_rows, tile_cols, tile_count[0])
    partial_value = partial_value.reshape(rows_here, columns_all)
    return lax.psum_scatter(partial_value, "tile", scatter_dimension=1, tiled=True)


def home(row, col):
    return jnp.minimum(row, col) // HERE


class Part:
    def __init__(self, ref, first, width=0):
        self.ref, self.first, self.width = ref, first, width

    def spot(self, key):
        if isinstance(key, tuple):
            return self.first + key[0] * self.width + key[1]
        return self.first + key

    def __getitem__(self, key):
        return self.ref[self.spot(key)]

    def __setitem__(self, key, value):
        self.ref[self.spot(key)] = value


OWN_WIDTH = (XS + 1) * LIST
MOVED_WIDTH = 2 * LIST


def own_parts(ref):
    return Part(ref, 0), Part(ref, 8), Part(ref, 16, OWN_WIDTH)


def moved_parts(ref):
    return Part(ref, 0), Part(ref, 8, MOVED_WIDTH)


def pad_list(table, first, size, row, col):
    for pad in range(GROUP):
        table[0, first + size + pad] = 0
        table[1, first + size + pad] = row
        table[2, first + size + pad] = col


def pack_kernel(facts, stored, *refs):
    outs, (plan, mine_of, entries, sems) = refs[:XS - 1], refs[XS - 1:]
    slots = stored.shape[0]
    rows, cols = Part(facts, 8), Part(facts, 8 + slots)
    place, sizes, table = own_parts(plan)
    for each in range(3):
        place[each] = facts[each]
    mine = place[0]
    low = mine * HERE
    fetch = pltpu.make_async_copy(stored.at[:, pl.ds(pl.multiple_of(place[1] * PIECE, PIECE), PIECE)], mine_of, sems.at[XS - 1])
    fetch.start()
    for each in range(8):
        sizes[each] = 0

    def sort_step(slot, _):
        row, col = rows[slot], cols[slot]
        target = lax.rem(home(row, col) - mine + XS, XS)
        kind = jnp.where((target == 0) & (row - low >= HERE), XS, target)
        position = sizes[kind]
        at = kind * LIST + position
        table[0, at] = slot
        table[1, at] = row
        table[2, at] = col
        sizes[kind] = position + 1
        return 0

    lax.fori_loop(0, facts[3], sort_step, 0)
    over = jnp.int32(0)
    for j in range(1, XS):
        over = jnp.maximum(over, (sizes[j] > CAP).astype(jnp.int32))
    sizes[XS + 1] = over
    fetch.wait()
    pad_list(table, 0, sizes[0], low, low + HERE + EXTRA)
    pad_list(table, XS * LIST, sizes[XS], low + HERE, low + HERE)
    copies = []
    for j in range(1, XS):
        out = outs[j - 1]
        entries[j - 1, 2, 0] = over.astype(jnp.float32)
        entries[j - 1, 3, mine] = 0.0
        for other in range(1, XS):
            entries[j - 1, 3, lax.rem(mine + other, XS)] = sizes[other].astype(jnp.float32)

        def move_step(item, _):
            at = j * LIST + item
            out[item] = mine_of[table[0, at]]
            entries[j - 1, 0, item] = table[1, at].astype(jnp.float32)
            entries[j - 1, 1, item] = table[2, at].astype(jnp.float32)
            return 0

        lax.fori_loop(0, jnp.minimum(sizes[j], CAP), move_step, 0)
        copy = pltpu.make_async_copy(entries.at[j - 1], out.at[CAP, pl.ds(0, 8)], sems.at[j - 1])
        copy.start()
        copies.append(copy)
    for copy in copies:
        copy.wait()


def pack(facts, integrals):
    slots = integrals.shape[0]
    spec = pltpu.PrefetchScalarGridSpec(
        num_scalar_prefetch=1,
        grid=(1,),
        in_specs=[pl.BlockSpec(memory_space=pl.ANY)],
        out_specs=[pl.BlockSpec((CAP + 1, PIECE, WIDTH), lambda i, *_: (0, 0, 0))] * (XS - 1)
        + [pl.BlockSpec(memory_space=pltpu.SMEM)],
        scratch_shapes=[
            pltpu.VMEM((slots, PIECE, WIDTH), jnp.float32),
            pltpu.SMEM((XS - 1, 8, WIDTH), jnp.float32),
            pltpu.SemaphoreType.DMA((XS,)),
        ],
    )
    return pl.pallas_call(
        pack_kernel,
        grid_spec=spec,
        out_shape=[jax.ShapeDtypeStruct((CAP + 1, PIECE, WIDTH), jnp.float32)] * (XS - 1)
        + [jax.ShapeDtypeStruct((16 + 3 * OWN_WIDTH,), jnp.int32)],
        compiler_params=pltpu.CompilerParams(vmem_limit_bytes=8 * 2**20),
        name="pack",
    )(facts, integrals)


def compact_kernel(plan, *refs):
    sources, (out, moved_plan, entries, sems) = refs[:XS - 1], refs[XS - 1:]
    place, sizes, _ = own_parts(plan)
    totals, table = moved_parts(moved_plan)
    mine = place[0]
    low = mine * HERE
    copies = [
        pltpu.make_async_copy(sources[j].at[CAP, pl.ds(0, 8)], entries.at[j], sems.at[j]) for j in range(XS - 1)
    ]
    for copy in copies:
        copy.start()
    for copy in copies:
        copy.wait()
    for each in range(8):
        totals[each] = 0
    over = sizes[XS + 1] > 0
    for j in range(XS - 1):
        over = over | (entries[j, 2, 0] > 0.5)
    for j in range(XS):
        there = lax.rem(mine + j, XS)
        total = jnp.int32(0) if j == 0 else sizes[j]
        for source in range(XS - 1):
            total = total + entries[source, 3, there].astype(jnp.int32)
        over = over | (total > TOTAL_CAP)
    for j in range(XS - 1):
        source = sources[j]
        size = jnp.minimum(entries[j, 3, mine].astype(jnp.int32), CAP)

        def step(item, _):
            row = entries[j, 0, item].astype(jnp.int32)
            col = entries[j, 1, item].astype(jnp.int32)
            kind = jnp.where(row - low >= HERE, 1, 0)
            position = jnp.minimum(totals[kind], TOTAL_CAP - 1)
            out[jnp.where(kind == 1, TOTAL_CAP - 1 - position, position)] = source[item]
            at = kind * LIST + position
            table[1, at] = row
            table[2, at] = col
            totals[kind] = position + 1
            return 0

        lax.fori_loop(0, size, step, 0)
    totals[2] = over.astype(jnp.int32)
    pad_list(table, 0, totals[0], low, low + HERE + EXTRA)
    pad_list(table, LIST, totals[1], low + HERE, low + HERE)


def compact(plan, sources):
    vmem = pl.BlockSpec(memory_space=pltpu.VMEM)
    smem = pl.BlockSpec(memory_space=pltpu.SMEM)
    return pl.pallas_call(
        compact_kernel,
        in_specs=[smem] + [vmem] * (XS - 1),
        out_specs=[vmem, smem],
        out_shape=[
            jax.ShapeDtypeStruct((TOTAL_CAP, PIECE, WIDTH), jnp.float32),
            jax.ShapeDtypeStruct((8 + 3 * MOVED_WIDTH,), jnp.int32),
        ],
        scratch_shapes=[pltpu.SMEM((XS - 1, 8, WIDTH), jnp.float32), pltpu.SemaphoreType.DMA((XS - 1,))],
        compiler_params=pltpu.CompilerParams(vmem_limit_bytes=8 * 2**20),
        name="compact",
    )(plan, *sources)


def split_of(value):
    high = value.astype(jnp.bfloat16)
    return high, (value - high.astype(jnp.float32)).astype(jnp.bfloat16)


def products_of(low, table, first, size, left, fetch, sums):
    blank = jnp.zeros((WIDTH, WIDTH), jnp.bfloat16)

    def step(group, _):
        products = []
        for member in range(GROUP):
            item = group * GROUP + member
            high, rest = split_of(fetch(member, item, table[0, first + item]))
            right = jnp.concatenate(
                [jnp.concatenate([high, rest], axis=1), jnp.concatenate([high, blank], axis=1)], axis=0
            )
            product = jnp.dot(left(table[1, first + item] - low), right, preferred_element_type=jnp.float32)
            products.append(product[:, :WIDTH] + product[:, WIDTH:])
        for member in range(GROUP):
            col = table[2, first + group * GROUP + member] - low
            lanes = pl.ds(pl.multiple_of(lax.rem(col, ZS) * WIDTH, WIDTH), WIDTH)
            sums[lax.div(col, ZS), :, lanes] += products[member]
        return 0

    lax.fori_loop(0, lax.div(size + GROUP - 1, GROUP), step, 0)


def split_at(source, row):
    lanes = pl.ds(pl.multiple_of(lax.rem(row, ZS) * WIDTH, WIDTH), WIDTH)
    return jnp.concatenate(split_of(source[lax.div(row, ZS), :, lanes]), axis=1)


def start_own(table, first, size, stored_hbm, stored, sems):
    def step(item, _):
        pltpu.make_async_copy(stored_hbm.at[table[0, first + item]], stored.at[item], sems.at[item]).start()
        return 0

    lax.fori_loop(0, size, step, 0)


def wait_own(size, stored_hbm, stored, sems):
    def step(item, _):
        pltpu.make_async_copy(stored_hbm.at[0], stored.at[item], sems.at[item]).wait()
        return 0

    lax.fori_loop(0, size, step, 0)


def piece_rows(place):
    my_y = lax.div(place[1], 2)
    my_core = lax.rem(place[1], 2)
    rows = []
    for shift in range(YS):
        for swapped in range(2):
            core = my_core if swapped == 0 else 1 - my_core
            rows.append(pl.multiple_of((lax.rem(my_y - shift + YS, YS) * 2 + core) * PIECE, PIECE))
    return rows


def prepare_kernel(near_hbm, split_hbm, first_hbm, near, split, sems):
    copies = [pltpu.make_async_copy(near_hbm.at[z], near.at[z], sems.at[z]) for z in range(ZS)]
    for copy in copies:
        copy.start()
    backs = []
    for z in range(ZS):
        copies[z].wait()
        if z == 1:
            firsts = pltpu.make_async_copy(near.at[pl.ds(0, 2)], first_hbm, sems.at[ZS])
            firsts.start()
        for part in range(ZS):
            value = near[z, :, part * WIDTH:(part + 1) * WIDTH]
            split[z * ZS + part] = jnp.concatenate(split_of(value), axis=1)
        back = pltpu.make_async_copy(split.at[pl.ds(z * ZS, ZS)], split_hbm.at[pl.ds(z * ZS, ZS)], sems.at[ZS + 1 + z])
        back.start()
        backs.append(back)
    firsts.wait()
    for back in backs:
        back.wait()


def prepare(near):
    _, rows_here, wide = near.shape
    return pl.pallas_call(
        prepare_kernel,
        in_specs=[pl.BlockSpec(memory_space=pl.ANY)],
        out_specs=[pl.BlockSpec(memory_space=pl.ANY)] * 2,
        out_shape=[
            jax.ShapeDtypeStruct((HERE, rows_here, 2 * WIDTH), jnp.bfloat16),
            jax.ShapeDtypeStruct((2, rows_here, wide), jnp.float32),
        ],
        scratch_shapes=[
            pltpu.VMEM(near.shape, jnp.float32),
            pltpu.VMEM((HERE, rows_here, 2 * WIDTH), jnp.bfloat16),
            pltpu.SemaphoreType.DMA((2 * ZS + 1,)),
        ],
        compiler_params=pltpu.CompilerParams(vmem_limit_bytes=LIMIT * 2**20),
        name="prepare",
    )(near)


def chunk_copies(pieces_hbm, tiles, sems, rows_of, source, target, size):
    return [
        pltpu.make_async_copy(
            pieces_hbm[k].at[pl.ds(source, size)],
            tiles.at[pl.ds(target, size), pl.ds(rows_of[k], PIECE)],
            sems.at[target // ROUND, k],
        )
        for k in range(2 * YS)
    ]


def main_kernel(plan, moved_plan, split_hbm, stored_hbm, *refs):
    place, sizes, own = own_parts(plan)
    totals, moved = moved_parts(moved_plan)
    pieces_hbm, refs = refs[:2 * YS], refs[2 * YS:]
    out_hbm, soon_hbm, later_hbm, stored, tiles, sums, split, sems, own_sems, tile_sems = refs
    low = place[0] * HERE
    rows_of = piece_rows(place)
    copies = [
        pltpu.make_async_copy(split_hbm.at[pl.ds(z * ZS, ZS)], split.at[pl.ds(z * ZS, ZS)], sems.at[z])
        for z in range(ZS)
    ]
    for copy in copies:
        copy.start()
    start_own(own, 0, sizes[0], stored_hbm, stored, own_sems)
    chunks = []
    for first in range(0, TOTAL_CAP - ROUND + 1, ROUND):
        size = ROUND if first + 2 * ROUND <= TOTAL_CAP else TOTAL_CAP - first
        chunks.append((first, size, chunk_copies(pieces_hbm, tiles, tile_sems, rows_of, first, first, size)))
    for first, size, chunk in chunks:
        for copy in chunk:
            pl.when(totals[0] > first)(copy.start)
    sums[...] = jnp.zeros_like(sums)
    left = lambda row: split[row]
    for copy in copies:
        copy.wait()
    wait_own(sizes[0], stored_hbm, stored, own_sems)
    products_of(low, own, 0, sizes[0], left, lambda member, item, index: stored[item], sums)
    for first, size, chunk in chunks:
        for copy in chunk:
            pl.when(totals[0] > first)(copy.wait)
        here = jnp.clip(totals[0] - first, 0, size)
        products_of(low, moved, first, here, left, lambda member, item, index, first=first: tiles[first + item], sums)
    soon = jnp.where(place[2] == ZS // 2 + 1, 1, 0)
    last = ZS
    backs = [
        pltpu.make_async_copy(sums.at[ZS + soon], soon_hbm, sems.at[last]),
        pltpu.make_async_copy(sums.at[ZS + 1 - soon], later_hbm, sems.at[last + 1]),
    ]
    for z in range(ZS):
        block = lax.rem(place[2] + z, ZS)
        backs.append(pltpu.make_async_copy(sums.at[block], out_hbm.at[z], sems.at[last + 2 + z]))
    for back in backs:
        back.start()
    for back in backs:
        back.wait()


def late_kernel(plan, moved_plan, sums_in, extra_hbm, stored_hbm, *refs):
    place, sizes, own = own_parts(plan)
    totals, moved = moved_parts(moved_plan)
    pieces_hbm, refs = refs[:2 * YS], refs[2 * YS:]
    sums_hbm, extra, own_tiles, moved_tiles, sums, touched, sems, own_sems, moved_sems = refs
    low = place[0] * HERE
    rows_of = piece_rows(place)
    over = totals[2]
    own_first = XS * LIST

    left = lambda row: split_at(extra, row - HERE)

    def start_round(turn):
        start_own(own, own_first + turn * ROUND, own_here(turn), stored_hbm, own_tiles, own_sems)
        base = jnp.maximum(TOTAL_CAP - ROUND * (turn + 1), 0)
        chunk = chunk_copies(pieces_hbm, moved_tiles, moved_sems, rows_of, base, 0, ROUND)
        for copy in chunk:
            pl.when(moved_here(turn) > 0)(copy.start)
        return base, chunk

    def finish_round(turn, base, chunk):
        wait_own(own_here(turn), stored_hbm, own_tiles, own_sems)
        products_of(
            low, own, own_first + turn * ROUND, own_here(turn), left, lambda member, item, index: own_tiles[item], sums
        )
        for copy in chunk:
            pl.when(moved_here(turn) > 0)(copy.wait)

        def fetch(member, item, index):
            return moved_tiles[jnp.maximum(TOTAL_CAP - 1 - turn * ROUND - item - base, 0)]

        products_of(low, moved, LIST + turn * ROUND, moved_here(turn), left, fetch, sums)

    def own_here(turn):
        return jnp.clip(sizes[XS] - turn * ROUND, 0, ROUND)

    def moved_here(turn):
        return jnp.clip(totals[1] - turn * ROUND, 0, ROUND)

    def whole_round(turn, _):
        finish_round(turn, *start_round(turn))
        return 0

    def touch(table, first, size):
        def one(item, _):
            touched[lax.div(table[2, first + item] - low, ZS)] = 1
            return 0

        lax.fori_loop(0, size, one, 0)

    def spot(z):
        return lax.rem(z - place[2] + ZS, ZS)


    @pl.when((sizes[XS] + totals[1] > 0) & (over == 0))
    def _():
        first_round = start_round(0)
        copies = [pltpu.make_async_copy(extra_hbm.at[z], extra.at[z], sems.at[ZS + z]) for z in range(2)]
        for copy in copies:
            copy.start()
        for z in range(ZS):
            touched[z] = 0
        touch(own, own_first, sizes[XS])
        touch(moved, LIST, totals[1])
        inward = [pltpu.make_async_copy(sums_in.at[spot(z)], sums.at[z], sems.at[z]) for z in range(ZS)]
        outward = [pltpu.make_async_copy(sums.at[z], sums_hbm.at[spot(z)], sems.at[z]) for z in range(ZS)]
        for z in range(ZS):
            pl.when(touched[z] > 0)(inward[z].start)
        sums[ZS] = jnp.zeros(sums.shape[1:], jnp.float32)
        for copy in copies:
            copy.wait()
        for z in range(ZS):
            pl.when(touched[z] > 0)(inward[z].wait)
        finish_round(0, *first_round)
        rounds = lax.div(jnp.maximum(sizes[XS], totals[1]) + ROUND - 1, ROUND)
        lax.fori_loop(1, rounds, whole_round, 0)
        for z in range(ZS):
            pl.when(touched[z] > 0)(outward[z].start)
        for z in range(ZS):
            pl.when(touched[z] > 0)(outward[z].wait)

    @pl.when(over > 0)
    def _():
        sums[...] = jnp.full_like(sums, jnp.nan)
        whole = pltpu.make_async_copy(sums.at[pl.ds(0, ZS)], sums_hbm, sems.at[0])
        whole.start()
        whole.wait()


def call(kernel, name, scalars, arrays, outs, scratch, aliases):
    smem = pl.BlockSpec(memory_space=pltpu.SMEM)
    anywhere = pl.BlockSpec(memory_space=pl.ANY)
    return pl.pallas_call(
        kernel,
        in_specs=[smem] * len(scalars) + [anywhere] * len(arrays),
        out_specs=[anywhere] * len(outs),
        out_shape=[jax.ShapeDtypeStruct(shape, jnp.float32) for shape in outs],
        input_output_aliases=aliases,
        scratch_shapes=scratch,
        cost_estimate=pl.CostEstimate(flops=10**6, bytes_accessed=10**4, transcendentals=0),
        compiler_params=pltpu.CompilerParams(vmem_limit_bytes=LIMIT * 2**20),
        name=name,
    )(*scalars, *arrays)


def main_sums(scalars, split, stored, pieces, wide):
    rows_here = split.shape[1]
    scratch = [
        pltpu.VMEM((LIST,) + stored.shape[1:], jnp.float32),
        pltpu.VMEM((TOTAL_CAP + GROUP, WIDTH, WIDTH), jnp.float32),
        pltpu.VMEM((ZS + 3, rows_here, wide), jnp.float32),
        pltpu.VMEM(split.shape, jnp.bfloat16),
        pltpu.SemaphoreType.DMA((2 * ZS + 2,)),
        pltpu.SemaphoreType.DMA((LIST,)),
        pltpu.SemaphoreType.DMA((TOTAL_CAP // ROUND + 1, 2 * YS)),
    ]
    outs = [(ZS, rows_here, wide)] + [(rows_here, wide)] * 2
    return call(main_kernel, "main", scalars, [split, stored, *pieces], outs, scratch, {})


def late_sums(scalars, sums, extra, stored, pieces):
    _, rows_here, wide = sums.shape
    scratch = [
        pltpu.VMEM(extra.shape, jnp.float32),
        pltpu.VMEM((ROUND + GROUP, WIDTH, WIDTH), jnp.float32),
        pltpu.VMEM((ROUND, WIDTH, WIDTH), jnp.float32),
        pltpu.VMEM((ZS + 1, rows_here, wide), jnp.float32),
        pltpu.SMEM((ZS,), jnp.int32),
        pltpu.SemaphoreType.DMA((ZS + 2,)),
        pltpu.SemaphoreType.DMA((ROUND,)),
        pltpu.SemaphoreType.DMA((1, 2 * YS)),
    ]
    return call(late_kernel, "late", scalars, [sums, extra, stored, *pieces], [sums.shape], scratch, {2: 0})[0]


def ring_sum(sums, more):
    half = ZS // 2
    middle = sums[half] + more(half)
    rows_here = middle.shape[0]
    up, down = middle[:rows_here // 2], middle[rows_here // 2:]
    for step in range(half - 1, -1, -1):
        up, down = lax.optimization_barrier((up, down))
        up = lax.ppermute(up, "tile", z_shift(1))
        down = lax.ppermute(down, "tile", z_shift(-1))
        up, down = lax.optimization_barrier((up, down))
        if step == half - 1:
            up = jnp.concatenate([up, jnp.zeros_like(up)], axis=0)
            down = jnp.concatenate([jnp.zeros_like(down), down], axis=0)
        if step > 0:
            up = up + (sums[step] + more(step))
            down = down + (sums[ZS - step] + more(ZS - step))
    return sums[0] + more(0) + up + down


def shards(
    amplitudes, driver, integrals, tile_rows, tile_cols, tile_count, pair_energy, virt_energy
):
    my_tile = lax.axis_index("tile")
    my_x = my_tile // ZS
    my_z = lax.rem(my_tile, ZS)
    place = jnp.stack([my_x, lax.axis_index("pair"), my_z, tile_count[0], my_x, my_x, my_x, my_x]).astype(jnp.int32)
    facts = jnp.concatenate([place, tile_rows, tile_cols])

    near = lax.all_gather(amplitudes, "tile", axis=0, axis_index_groups=Z_GROUPS)

    *packed, plan = pack(facts, integrals)
    arrived = [lax.ppermute(packed[step - 1], "tile", x_shift(step)) for step in range(1, XS)]
    mine, moved_plan = compact(plan, arrived)
    along_y = [mine] + [lax.ppermute(mine, "pair", y_shift(step)) for step in range(1, YS)]
    across = lax.ppermute(mine, "pair", CORE_SWAP)
    along_y[YS - 1], across = lax.optimization_barrier((along_y[YS - 1], across))
    split, first = prepare(near)
    extra = lax.ppermute(first, "tile", x_shift(-1))
    along_y[1], along_y[2], first = lax.optimization_barrier((along_y[1], along_y[2], first))
    pieces = [mine, across]
    for piece in along_y[1:]:
        pieces += [piece, lax.ppermute(piece, "pair", CORE_SWAP)]
    scalars = (plan, moved_plan)
    sums, soon, later = main_sums(scalars, split, integrals, pieces, near.shape[2])
    soon = lax.ppermute(soon, "tile", x_shift(1))
    later = lax.ppermute(later, "tile", x_shift(1))
    sums = late_sums(scalars, sums, extra, integrals, pieces)
    soon_block = jnp.where(my_z == ZS // 2 + 1, 1, 0)

    def more(step):
        block = lax.rem(my_z + step, ZS)
        value = jnp.where(block == soon_block, soon, 0.0)
        if step == ZS // 2:
            return value
        return jnp.where(block == 1 - soon_block, later, value)

    ladder = ring_sum(sums, more)
    denominator = virt_energy[None, :] - pair_energy[:, None]
    result = (driver + ladder) / denominator

    def slow():
        full = dense_ladder(amplitudes, integrals, tile_rows, tile_cols, tile_count)
        return (driver + full) / denominator

    return lax.cond(jnp.isnan(ladder[0, 0]), slow, lambda: result)


def solution(mesh):
    return jax.shard_map(
        shards,
        mesh=mesh,
        in_specs=(
            P("pair", "tile"),
            P("pair", "tile"),
            P("tile", None, None),
            P("tile"),
            P("tile"),
            P("tile"),
            P("pair"),
            P("tile"),
        ),
        out_specs=P("pair", "tile"),
        check_vma=False,
    )
```

time: 138 us -> 135 us (0.978); the launches traced: 137 us -> 135 us
  local copies, waits for them, and re-layouts: 9.17 us -> 3.37 us
  Pallas kernels: 13.7 us -> 18.5 us
  starting transfers between devices: 29.3 us -> 26.9 us
    ppermute x4, starting transfers between devices: 0.68 us -> 6.58 us  [ring_sum(): up = lax.ppermute(up, 'tile', z_shift(1))]
    ppermute x4, starting transfers between devices: 14.9 us -> 9.36 us  [ring_sum(): down = lax.ppermute(down, 'tile', z_shift(-1))]
    pallas_call x3 -> x4, Pallas kernels: 10.2 us -> 15.2 us  [the longest x2 9.68 us: call(): pl.pallas_call(kernel, in_specs=[smem] * len(scalars) + [anywhere] * len(...]
    unnamed x30 -> x32, local copies, waits for them, and re-layouts: 6.56 us -> 2.08 us
    ppermute x4, waiting for transfers between devices: 0.01 us -> 4.48 us  [ring_sum(): down = lax.ppermute(down, 'tile', z_shift(-1))]
    ppermute x2 -> x4, waiting for transfers between devices: 9.23 us -> 6.4 us  [the longest x1 3.99 us: shards(): soon = lax.ppermute(soon, 'tile', x_shift(1))]
    slice x1, local copies, waits for them, and re-layouts: 2.1 us -> 0.02 us  [ring_sum(): up, down = (middle[:rows_here // 2], middle[rows_here // 2:])]
    ppermute x3, waiting for transfers between devices: 25.7 us -> 23.6 us  [shards(): lax.ppermute(mine, 'pair', y_shift(step))]
  transfers between devices with their start and end apart: 21 -> 22, of which waited for: 10 -> 16; matrix products, arithmetic and copies ran while one was open for 2% -> 1% of each run, Pallas kernels for 10% -> 14%
where the time goes in v5:
time: 135 us
  waiting for transfers between devices  65 us (48%)
  starting transfers between devices  26.9 us (20%)
  Pallas kernels  18.5 us (14%)
  between operations  15.6 us (12%)
  other arithmetic  5.71 us (4%)
  local copies, waits for them, and re-layouts  3.37 us (2%)
    ppermute x3, waiting for transfers between devices, shards(): lax.ppermute(mine, 'pair', y_shift(step))  23.6 us
    ppermute x4, waiting for transfers between devices, ring_sum(): up = lax.ppermute(up, 'tile', z_shift(1))  15.7 us
    ppermute x3, waiting for transfers between devices, shards(): lax.ppermute(packed[step - 1], 'tile', x_shift(step))  12.3 us
    pallas_call x2, Pallas kernels, call(): pl.pallas_call(kernel, in_specs=[smem] * len(scalars) + [anywhere] * len(...  9.68 us
    ppermute x4, starting transfers between devices, ring_sum(): down = lax.ppermute(down, 'tile', z_shift(-1))  9.36 us
    ppermute x4, starting transfers between devices, ring_sum(): up = lax.ppermute(up, 'tile', z_shift(1))  6.58 us
    ppermute x3, starting transfers between devices, shards(): lax.ppermute(mine, 'pair', y_shift(step))  5.01 us
    ppermute x4, waiting for transfers between devices, ring_sum(): down = lax.ppermute(down, 'tile', z_shift(-1))  4.48 us
  transfers between devices with their start and end apart: 22, of which 16 were waited for; matrix products, arithmetic and copies ran while one was open for 1% of the time, Pallas kernels for 14%

profile of v5, /device:TPU:6, one launch (start us, length us, event | category | flops | bytes accessed | tf_op | source)
XLA Modules:
  0.0 135.1 jit_solution(7442863622762850127)
XLA Ops:
  6.5 0.7 all-gather.6.cloned.1.call-update
  7.9 0.8 concatenate.9.facts
  8.7 3.3 %pack.1 = (f32[33,16,128]{2,1,0:T(8,128)S(1)}, f32[33,16,128]{2,1,0:T(8,128)S(1)}, f32[33,16,128]{2,1,0:T(8,128)S(1)}, s32[1096]{0:T(1024)S(1)}) custom-call(s32[136]{0:T(256)S(1)} %concatenate.9.facts, f32[64,128,128]{2,1,0:T(8,128)} %stored_hbm.3), custom_call_target="tpu_custom_call" | custom-call | tf_op jit(solution)/shard_map/pack/pallas_call | solution.py:183
  12.0 2.5 %collective-permute-start = (f32[33,16,128]{2,1,0:T(8,128)S(1)}, f32[33,16,128]{2,1,0:T(8,128)S(1)}, u32[]{:S(2)}, u32[]{:S(2)}) collective-permute-start(f32[33,16,128]{2,1,0:T(8,128)S(1)} %get-tuple-element.117), channel_id=1, source_target_pairs={{0,64},{8,72},{16,80},{24,88},{32,96},{40,104},{48,112},{56,120},{... | collective-permute-start | bytes 811016 | tf_op jit(solution)/shard_map/ppermute | solution.py:580
  14.5 0.3 collective-permute-start.1
  14.7 0.7 collective-permute-start.2
  15.4 6.0 %collective-permute-done.refs_0_ = f32[33,16,128]{2,1,0:T(8,128)S(1)} collective-permute-done((f32[33,16,128]{2,1,0:T(8,128)S(1)}, f32[33,16,128]{2,1,0:T(8,128)S(1)}, u32[]{:S(2)}, u32[]{:S(2)}) %collective-permute-start) | collective-permute-done | bytes 270368 | tf_op jit(solution)/shard_map/ppermute | solution.py:580
  21.4 3.4 %collective-permute-done.1.refs_1_ = f32[33,16,128]{2,1,0:T(8,128)S(1)} collective-permute-done((f32[33,16,128]{2,1,0:T(8,128)S(1)}, f32[33,16,128]{2,1,0:T(8,128)S(1)}, u32[]{:S(2)}, u32[]{:S(2)}) %collective-permute-start.1) | collective-permute-done | bytes 270368 | tf_op jit(solution)/shard_map/ppermute | solution.py:580
  24.9 2.8 %collective-permute-done.2.refs_2_ = f32[33,16,128]{2,1,0:T(8,128)S(1)} collective-permute-done((f32[33,16,128]{2,1,0:T(8,128)S(1)}, f32[33,16,128]{2,1,0:T(8,128)S(1)}, u32[]{:S(2)}, u32[]{:S(2)}) %collective-permute-start.2) | collective-permute-done | bytes 270368 | tf_op jit(solution)/shard_map/ppermute | solution.py:580
  27.7 2.7 %compact.1 = (f32[68,16,128]{2,1,0:T(8,128)S(1)}, s32[440]{0:T(512)S(1)}) custom-call(s32[1096]{0:T(1024)S(1)} %get-tuple-element.116.plan, f32[33,16,128]{2,1,0:T(8,128)S(1)} %collective-permute-done.refs_0_, f32[33,16,128]{2,1,0:T(8,128)S(1)} %collective-permute-done.1.refs_1_, f32[33,16,128]{2,1,0:T(8,128)S(1)} %collective-permute-done.2.refs_2_), custom_call_target="tpu_custom_call" | custom-call | tf_op jit(solution)/shard_map/compact/pallas_call | solution.py:242
  30.4 0.5 copy-done.2
  31.0 3.5 %collective-permute-start.3 = (f32[68,16,128]{2,1,0:T(8,128)S(1)}, f32[68,16,128]{2,1,0:T(8,128)S(1)}, u32[]{:S(2)}, u32[]{:S(2)}) collective-permute-start(f32[68,16,128]{2,1,0:T(8,128)S(1)} %get-tuple-element.122.refs_0_), channel_id=1, source_target_pairs={{0,6},{1,7},{2,0},{3,1},{4,2},{5,3},{6,4},{7,5},{8,14},{9,15},{10,... | collective-permute-start | bytes 1671176 | tf_op jit(solution)/shard_map/ppermute | solution.py:582
  34.4 0.6 collective-permute-start.6
  35.1 0.9 collective-permute-start.5
  36.0 22.8 %collective-permute-done.3.refs_6_ = f32[68,16,128]{2,1,0:T(8,128)S(1)} collective-permute-done((f32[68,16,128]{2,1,0:T(8,128)S(1)}, f32[68,16,128]{2,1,0:T(8,128)S(1)}, u32[]{:S(2)}, u32[]{:S(2)}) %collective-permute-start.3) | collective-permute-done | bytes 557088 | tf_op jit(solution)/shard_map/ppermute | solution.py:582
  58.8 2.8 %prepare.1 = (bf16[64,64,256]{2,1,0:T(8,128)(2,1)}, f32[2,64,1024]{2,1,0:T(8,128)}) custom-call(f32[8,64,1024]{2,1,0:T(8,128)} %bitcast.77), custom_call_target="tpu_custom_call" | custom-call | tf_op jit(solution)/shard_map/prepare/pallas_call | solution.py:338
  61.6 0.8 collective-permute-done.5.refs_2_
  62.5 0.5 collective-permute-start.8
  63.0 0.4 collective-permute-start.10
  63.4 1.1 collective-permute-done.7.refs_3_
  64.4 0.8 collective-permute-done.8.refs_5_
  65.3 0.8 copy-done.11
  66.1 8.3 %main.1 = (f32[8,64,1024]{2,1,0:T(8,128)}, f32[64,1024]{1,0:T(8,128)}, f32[64,1024]{1,0:T(8,128)}) custom-call(s32[1096]{0:T(1024)} %copy-done.1, s32[440]{0:T(512)} %copy-done.2, bf16[64,64,256]{2,1,0:T(8,128)(2,1)} %get-tuple-element.121.split_hbm, f32[64,128,128]{2,1,0:T(8,128)} %stored_hbm.3, f32[68,16,128]{2,1,0:T(8,128)} %copy-done, ...), custom_call_target="tpu_custom_call" | custom-call | flops 1000000 | bytes 10000 | tf_op jit(solution)/shard_map/main/pallas_call | solution.py:506
  74.5 1.5 %collective-permute-start.11 = (f32[64,1024]{1,0:T(8,128)}, f32[64,1024]{1,0:T(8,128)S(1)}, u32[]{:S(2)}, u32[]{:S(2)}) collective-permute-start(f32[64,1024]{1,0:T(8,128)} %get-tuple-element.129), channel_id=1, source_target_pairs={{0,64},{8,72},{16,80},{24,88},{32,96},{40,104},{48,112},{56,120},{... | collective-permute-start | bytes 786440 | tf_op jit(solution)/shard_map/ppermute | solution.py:594
  76.0 2.4 %collective-permute-done.10.extra_hbm = f32[2,64,1024]{2,1,0:T(8,128)} collective-permute-done((f32[2,64,1024]{2,1,0:T(8,128)}, f32[2,64,1024]{2,1,0:T(8,128)}, u32[]{:S(2)}, u32[]{:S(2)}) %collective-permute-start.10) | collective-permute-done | bytes 524320 | tf_op jit(solution)/shard_map/ppermute | solution.py:586
  78.4 1.4 %late.1 = f32[8,64,1024]{2,1,0:T(8,128)} custom-call(s32[1096]{0:T(1024)} %copy-done.1, s32[440]{0:T(512)} %copy-done.2, f32[8,64,1024]{2,1,0:T(8,128)} %get-tuple-element.128.sums_in, f32[2,64,1024]{2,1,0:T(8,128)} %collective-permute-done.10.extra_hbm, f32[64,128,128]{2,1,0:T(8,128)} %stored_hbm.3, ...), custom_call_target="tpu_custom_call", output_to_operand_aliasing={{}: (2, {})} | custom-call | flops 1000000 | bytes 10000 | tf_op jit(solution)/shard_map/late/pallas_call | solution.py:506
  79.8 4.0 %collective-permute-done.12 = f32[64,1024]{1,0:T(8,128)S(1)} collective-permute-done((f32[64,1024]{1,0:T(8,128)}, f32[64,1024]{1,0:T(8,128)S(1)}, u32[]{:S(2)}, u32[]{:S(2)}) %collective-permute-start.12) | collective-permute-done | bytes 262176 | tf_op jit(solution)/shard_map/ppermute | solution.py:593
  83.8 1.0 fusion.22
  84.8 0.5 collective-permute-start.13
  85.4 5.3 %collective-permute-start.14 = (f32[32,1024]{1,0:T(8,128)S(1)}, f32[32,1024]{1,0:T(8,128)S(1)}, u32[]{:S(2)}, u32[]{:S(2)}) collective-permute-start(f32[32,1024]{1,0:T(8,128)S(1)} %get-tuple-element.132), channel_id=1, source_target_pairs={{0,56},{8,0},{16,8},{24,16},{32,24},{40,32},{48,40},{56,48},{64,12... | collective-permute-start | bytes 393224 | tf_op jit(solution)/shard_map/ppermute | solution.py:557
  90.7 2.9 %collective-permute-done.13 = f32[32,1024]{1,0:T(8,128)S(1)} collective-permute-done((f32[32,1024]{1,0:T(8,128)S(1)}, f32[32,1024]{1,0:T(8,128)S(1)}, u32[]{:S(2)}, u32[]{:S(2)}) %collective-permute-start.13) | collective-permute-done | bytes 131104 | tf_op jit(solution)/shard_map/ppermute | solution.py:556
  93.5 1.2 fusion.19
  94.8 3.4 %collective-permute-start.16 = (f32[64,1024]{1,0:T(8,128)S(1)}, f32[64,1024]{1,0:T(8,128)S(1)}, u32[]{:S(2)}, u32[]{:S(2)}) collective-permute-start(f32[64,1024]{1,0:T(8,128)S(1)} %get-tuple-element.136), channel_id=1, source_target_pairs={{0,56},{8,0},{16,8},{24,16},{32,24},{40,32},{48,40},{56,48},{64,12... | collective-permute-start | bytes 786440 | tf_op jit(solution)/shard_map/ppermute | solution.py:557
  98.2 4.3 %collective-permute-done.15 = f32[64,1024]{1,0:T(8,128)S(1)} collective-permute-done((f32[64,1024]{1,0:T(8,128)S(1)}, f32[64,1024]{1,0:T(8,128)S(1)}, u32[]{:S(2)}, u32[]{:S(2)}) %collective-permute-start.15) | collective-permute-done | bytes 262176 | tf_op jit(solution)/shard_map/ppermute | solution.py:556
  102.4 1.1 collective-permute-done.16
  103.5 1.2 fusion.15
  104.7 3.3 %collective-permute-start.17 = (f32[64,1024]{1,0:T(8,128)S(1)}, f32[64,1024]{1,0:T(8,128)S(1)}, u32[]{:S(2)}, u32[]{:S(2)}) collective-permute-start(f32[64,1024]{1,0:T(8,128)S(1)} %get-tuple-element.139), channel_id=1, source_target_pairs={{0,8},{8,16},{16,24},{24,32},{32,40},{40,48},{48,56},{56,0},{64,72... | collective-permute-start | bytes 786440 | tf_op jit(solution)/shard_map/ppermute | solution.py:556
  108.0 4.3 %collective-permute-done.17 = f32[64,1024]{1,0:T(8,128)S(1)} collective-permute-done((f32[64,1024]{1,0:T(8,128)S(1)}, f32[64,1024]{1,0:T(8,128)S(1)}, u32[]{:S(2)}, u32[]{:S(2)}) %collective-permute-start.17) | collective-permute-done | bytes 262176 | tf_op jit(solution)/shard_map/ppermute | solution.py:556
  112.4 2.0 %collective-permute-done.18 = f32[64,1024]{1,0:T(8,128)S(1)} collective-permute-done((f32[64,1024]{1,0:T(8,128)S(1)}, f32[64,1024]{1,0:T(8,128)S(1)}, u32[]{:S(2)}, u32[]{:S(2)}) %collective-permute-start.18) | collective-permute-done | bytes 262176 | tf_op jit(solution)/shard_map/ppermute | solution.py:557
  114.4 1.2 fusion.11
  115.6 2.7 %collective-permute-start.19 = (f32[64,1024]{1,0:T(8,128)S(1)}, f32[64,1024]{1,0:T(8,128)S(1)}, u32[]{:S(2)}, u32[]{:S(2)}) collective-permute-start(f32[64,1024]{1,0:T(8,128)S(1)} %get-tuple-element.143), channel_id=1, source_target_pairs={{0,8},{8,16},{16,24},{24,32},{32,40},{40,48},{48,56},{56,0},{64,72... | collective-permute-start | bytes 786440 | tf_op jit(solution)/shard_map/ppermute | solution.py:556
  118.2 0.6 collective-permute-start.20
  118.9 0.1 broadcast_subtract_fusion
  119.0 4.2 %collective-permute-done.19 = f32[64,1024]{1,0:T(8,128)S(1)} collective-permute-done((f32[64,1024]{1,0:T(8,128)S(1)}, f32[64,1024]{1,0:T(8,128)S(1)}, u32[]{:S(2)}, u32[]{:S(2)}) %collective-permute-start.19) | collective-permute-done | bytes 262176 | tf_op jit(solution)/shard_map/ppermute | solution.py:556
  123.2 1.4 %collective-permute-done.20 = f32[64,1024]{1,0:T(8,128)S(1)} collective-permute-done((f32[64,1024]{1,0:T(8,128)S(1)}, f32[64,1024]{1,0:T(8,128)S(1)}, u32[]{:S(2)}, u32[]{:S(2)}) %collective-permute-start.20) | collective-permute-done | bytes 262176 | tf_op jit(solution)/shard_map/ppermute | solution.py:557
  124.6 1.1 fusion.25
  125.7 0.5 slice.62
  127.6 0.7 copy-done.13
  (45 shorter events, 0.4 us)
Async XLA Ops:
  6.5 52.2 %all-gather.6.cloned.1.call-start = ((), (), s32[]{:S(2)}) async-start(), calls=%async_computation.3 | async-start | bytes 2359296 | tf_op jit(solution)/shard_map/all_gather | solution.py:577
  12.0 53.3 %copy-start.1 = (s32[1096]{0:T(1024)}, s32[1096]{0:T(1024)S(1)}, u32[]{:S(2)}) copy-start(s32[1096]{0:T(1024)S(1)} %get-tuple-element.116.plan) | copy-start | bytes 13156
  12.0 9.4 %collective-permute-start = (f32[33,16,128]{2,1,0:T(8,128)S(1)}, f32[33,16,128]{2,1,0:T(8,128)S(1)}, u32[]{:S(2)}, u32[]{:S(2)}) collective-permute-start(f32[33,16,128]{2,1,0:T(8,128)S(1)} %get-tuple-element.117), channel_id=1, source_target_pairs={{0,64},{8,72},{16,80},{24,88},{32,96},{40,104},{48,112},{56,120},{... | collective-permute-start | bytes 811016 | tf_op jit(solution)/shard_map/ppermute | solution.py:580
  14.5 10.4 %collective-permute-start.1 = (f32[33,16,128]{2,1,0:T(8,128)S(1)}, f32[33,16,128]{2,1,0:T(8,128)S(1)}, u32[]{:S(2)}, u32[]{:S(2)}) collective-permute-start(f32[33,16,128]{2,1,0:T(8,128)S(1)} %get-tuple-element.118), channel_id=1, source_target_pairs={{0,128},{8,136},{16,144},{24,152},{32,160},{40,168},{48,176},{56,1... | collective-permute-start | bytes 811016 | tf_op jit(solution)/shard_map/ppermute | solution.py:580
  14.7 12.9 %collective-permute-start.2 = (f32[33,16,128]{2,1,0:T(8,128)S(1)}, f32[33,16,128]{2,1,0:T(8,128)S(1)}, u32[]{:S(2)}, u32[]{:S(2)}) collective-permute-start(f32[33,16,128]{2,1,0:T(8,128)S(1)} %get-tuple-element.119), channel_id=1, source_target_pairs={{0,192},{8,200},{16,208},{24,216},{32,224},{40,232},{48,240},{56,2... | collective-permute-start | bytes 811016 | tf_op jit(solution)/shard_map/ppermute | solution.py:580
  30.4 0.5 copy-start.2
  31.0 34.3 %copy-start = (f32[68,16,128]{2,1,0:T(8,128)}, f32[68,16,128]{2,1,0:T(8,128)S(1)}, u32[]{:S(2)}) copy-start(f32[68,16,128]{2,1,0:T(8,128)S(1)} %get-tuple-element.122.refs_0_) | copy-start | bytes 1671172
  31.0 5.0 %collective-permute-start.4 = (f32[68,16,128]{2,1,0:T(8,128)S(1)}, f32[68,16,128]{2,1,0:T(8,128)S(1)}, u32[]{:S(2)}, u32[]{:S(2)}) collective-permute-start(f32[68,16,128]{2,1,0:T(8,128)S(1)} %get-tuple-element.122.refs_0_), channel_id=1, source_target_pairs={{0,1},{1,0},{2,3},{3,2},{4,5},{5,4},{6,7},{7,6},{8,9},{9,8},{10,11... | collective-permute-start | bytes 1671176 | tf_op jit(solution)/shard_map/ppermute | solution.py:583
  31.0 27.8 %collective-permute-start.3 = (f32[68,16,128]{2,1,0:T(8,128)S(1)}, f32[68,16,128]{2,1,0:T(8,128)S(1)}, u32[]{:S(2)}, u32[]{:S(2)}) collective-permute-start(f32[68,16,128]{2,1,0:T(8,128)S(1)} %get-tuple-element.122.refs_0_), channel_id=1, source_target_pairs={{0,6},{1,7},{2,0},{3,1},{4,2},{5,3},{6,4},{7,5},{8,14},{9,15},{10,... | collective-permute-start | bytes 1671176 | tf_op jit(solution)/shard_map/ppermute | solution.py:582
  34.4 27.2 %collective-permute-start.6 = (f32[68,16,128]{2,1,0:T(8,128)S(1)}, f32[68,16,128]{2,1,0:T(8,128)S(1)}, u32[]{:S(2)}, u32[]{:S(2)}) collective-permute-start(f32[68,16,128]{2,1,0:T(8,128)S(1)} %get-tuple-element.122.refs_0_), channel_id=1, source_target_pairs={{0,4},{1,5},{2,6},{3,7},{4,0},{5,1},{6,2},{7,3},{8,12},{9,13},{10,... | collective-permute-start | bytes 1671176 | tf_op jit(solution)/shard_map/ppermute | solution.py:582
  35.1 27.4 %collective-permute-start.5 = (f32[68,16,128]{2,1,0:T(8,128)S(1)}, f32[68,16,128]{2,1,0:T(8,128)S(1)}, u32[]{:S(2)}, u32[]{:S(2)}) collective-permute-start(f32[68,16,128]{2,1,0:T(8,128)S(1)} %get-tuple-element.122.refs_0_), channel_id=1, source_target_pairs={{0,2},{1,3},{2,4},{3,5},{4,6},{5,7},{6,0},{7,1},{8,10},{9,11},{10,... | collective-permute-start | bytes 1671176 | tf_op jit(solution)/shard_map/ppermute | solution.py:582
  36.0 29.3 %copy-start.5 = (f32[68,16,128]{2,1,0:T(8,128)}, f32[68,16,128]{2,1,0:T(8,128)S(1)}, u32[]{:S(2)}) copy-start(f32[68,16,128]{2,1,0:T(8,128)S(1)} %collective-permute-done.4.refs_1_) | copy-start | bytes 1671172
  58.8 6.5 %copy-start.6 = (f32[68,16,128]{2,1,0:T(8,128)}, f32[68,16,128]{2,1,0:T(8,128)S(1)}, u32[]{:S(2)}) copy-start(f32[68,16,128]{2,1,0:T(8,128)S(1)} %collective-permute-done.3.refs_6_) | copy-start | bytes 1671172
  58.8 4.6 %collective-permute-start.9 = (f32[68,16,128]{2,1,0:T(8,128)S(1)}, f32[68,16,128]{2,1,0:T(8,128)S(1)}, u32[]{:S(2)}, u32[]{:S(2)}) collective-permute-start(f32[68,16,128]{2,1,0:T(8,128)S(1)} %collective-permute-done.3.refs_6_), channel_id=1, source_target_pairs={{0,1},{1,0},{2,3},{3,2},{4,5},{5,4},{6,7},{7,6},{8,9},{9,8},{10,11... | collective-permute-start | bytes 1671176 | tf_op jit(solution)/shard_map/ppermute | solution.py:590
  61.6 3.6 %copy-start.7 = (f32[68,16,128]{2,1,0:T(8,128)}, f32[68,16,128]{2,1,0:T(8,128)S(1)}, u32[]{:S(2)}) copy-start(f32[68,16,128]{2,1,0:T(8,128)S(1)} %collective-permute-done.6.refs_4_) | copy-start | bytes 1671172
  62.5 2.8 %copy-start.8 = (f32[68,16,128]{2,1,0:T(8,128)}, f32[68,16,128]{2,1,0:T(8,128)S(1)}, u32[]{:S(2)}) copy-start(f32[68,16,128]{2,1,0:T(8,128)S(1)} %collective-permute-done.5.refs_2_) | copy-start | bytes 1671172
  62.5 2.0 %collective-permute-start.7 = (f32[68,16,128]{2,1,0:T(8,128)S(1)}, f32[68,16,128]{2,1,0:T(8,128)S(1)}, u32[]{:S(2)}, u32[]{:S(2)}) collective-permute-start(f32[68,16,128]{2,1,0:T(8,128)S(1)} %collective-permute-done.5.refs_2_), channel_id=1, source_target_pairs={{0,1},{1,0},{2,3},{3,2},{4,5},{5,4},{6,7},{7,6},{8,9},{9,8},{10,11... | collective-permute-start | bytes 1671176 | tf_op jit(solution)/shard_map/ppermute | solution.py:590
  62.5 2.7 %collective-permute-start.8 = (f32[68,16,128]{2,1,0:T(8,128)S(1)}, f32[68,16,128]{2,1,0:T(8,128)S(1)}, u32[]{:S(2)}, u32[]{:S(2)}) collective-permute-start(f32[68,16,128]{2,1,0:T(8,128)S(1)} %collective-permute-done.6.refs_4_), channel_id=1, source_target_pairs={{0,1},{1,0},{2,3},{3,2},{4,5},{5,4},{6,7},{7,6},{8,9},{9,8},{10,11... | collective-permute-start | bytes 1671176 | tf_op jit(solution)/shard_map/ppermute | solution.py:590
  63.0 15.4 %collective-permute-start.10 = (f32[2,64,1024]{2,1,0:T(8,128)}, f32[2,64,1024]{2,1,0:T(8,128)}, u32[]{:S(2)}, u32[]{:S(2)}) collective-permute-start(f32[2,64,1024]{2,1,0:T(8,128)} %get-tuple-element.124), channel_id=1, source_target_pairs={{0,192},{8,200},{16,208},{24,216},{32,224},{40,232},{48,240},{56,2... | collective-permute-start | bytes 1572872 | tf_op jit(solution)/shard_map/ppermute | solution.py:586
  63.4 1.9 %copy-start.9 = (f32[68,16,128]{2,1,0:T(8,128)}, f32[68,16,128]{2,1,0:T(8,128)S(1)}, u32[]{:S(2)}) copy-start(f32[68,16,128]{2,1,0:T(8,128)S(1)} %collective-permute-done.9.refs_7_) | copy-start | bytes 1671172
  64.4 0.9 copy-start.10
  65.2 0.9 copy-start.11
  74.4 9.4 %collective-permute-start.12 = (f32[64,1024]{1,0:T(8,128)}, f32[64,1024]{1,0:T(8,128)S(1)}, u32[]{:S(2)}, u32[]{:S(2)}) collective-permute-start(f32[64,1024]{1,0:T(8,128)} %get-tuple-element.130), channel_id=1, source_target_pairs={{0,64},{8,72},{16,80},{24,88},{32,96},{40,104},{48,112},{56,120},{... | collective-permute-start | bytes 786440 | tf_op jit(solution)/shard_map/ppermute | solution.py:593
  74.5 19.1 %collective-permute-start.11 = (f32[64,1024]{1,0:T(8,128)}, f32[64,1024]{1,0:T(8,128)S(1)}, u32[]{:S(2)}, u32[]{:S(2)}) collective-permute-start(f32[64,1024]{1,0:T(8,128)} %get-tuple-element.129), channel_id=1, source_target_pairs={{0,64},{8,72},{16,80},{24,88},{32,96},{40,104},{48,112},{56,120},{... | collective-permute-start | bytes 786440 | tf_op jit(solution)/shard_map/ppermute | solution.py:594
  78.4 40.5 %copy-start.14 = (f32[1024]{0:T(1024)S(1)}, f32[1024]{0:T(1024)}, u32[]{:S(2)}) copy-start(f32[1024]{0:T(1024)} %param.21) | copy-start | bytes 12292
  78.4 40.5 %copy-start.15 = (f32[64]{0:T(128)S(1)}, f32[64]{0:T(128)}, u32[]{:S(2)}) copy-start(f32[64]{0:T(128)} %param.20) | copy-start | bytes 772
  78.4 49.1 %copy-start.3 = (s32[64]{0:T(128)S(1)}, s32[64]{0:T(128)}, u32[]{:S(2)}) copy-start(s32[64]{0:T(128)} %param.17) | copy-start | bytes 772
  78.4 49.1 %copy-start.4 = (s32[64]{0:T(128)S(1)}, s32[64]{0:T(128)}, u32[]{:S(2)}) copy-start(s32[64]{0:T(128)} %param.18) | copy-start | bytes 772
  78.4 49.1 %copy-start.12 = (f32[64,1024]{1,0:T(8,128)S(1)}, f32[64,1024]{1,0:T(8,128)}, u32[]{:S(2)}) copy-start(f32[64,1024]{1,0:T(8,128)} %param.15) | copy-start | bytes 786436
  84.8 8.7 %collective-permute-start.13 = (f32[32,1024]{1,0:T(8,128)S(1)}, f32[32,1024]{1,0:T(8,128)S(1)}, u32[]{:S(2)}, u32[]{:S(2)}) collective-permute-start(f32[32,1024]{1,0:T(8,128)S(1)} %get-tuple-element.131), channel_id=1, source_target_pairs={{0,8},{8,16},{16,24},{24,32},{32,40},{40,48},{48,56},{56,0},{64,72... | collective-permute-start | bytes 393224 | tf_op jit(solution)/shard_map/ppermute | solution.py:556
  85.4 8.2 %collective-permute-start.14 = (f32[32,1024]{1,0:T(8,128)S(1)}, f32[32,1024]{1,0:T(8,128)S(1)}, u32[]{:S(2)}, u32[]{:S(2)}) collective-permute-start(f32[32,1024]{1,0:T(8,128)S(1)} %get-tuple-element.132), channel_id=1, source_target_pairs={{0,56},{8,0},{16,8},{24,16},{32,24},{40,32},{48,40},{56,48},{64,12... | collective-permute-start | bytes 393224 | tf_op jit(solution)/shard_map/ppermute | solution.py:557
  94.7 7.7 %collective-permute-start.15 = (f32[64,1024]{1,0:T(8,128)S(1)}, f32[64,1024]{1,0:T(8,128)S(1)}, u32[]{:S(2)}, u32[]{:S(2)}) collective-permute-start(f32[64,1024]{1,0:T(8,128)S(1)} %get-tuple-element.135), channel_id=1, source_target_pairs={{0,8},{8,16},{16,24},{24,32},{32,40},{40,48},{48,56},{56,0},{64,72... | collective-permute-start | bytes 786440 | tf_op jit(solution)/shard_map/ppermute | solution.py:556
  94.8 8.7 %collective-permute-start.16 = (f32[64,1024]{1,0:T(8,128)S(1)}, f32[64,1024]{1,0:T(8,128)S(1)}, u32[]{:S(2)}, u32[]{:S(2)}) collective-permute-start(f32[64,1024]{1,0:T(8,128)S(1)} %get-tuple-element.136), channel_id=1, source_target_pairs={{0,56},{8,0},{16,8},{24,16},{32,24},{40,32},{48,40},{56,48},{64,12... | collective-permute-start | bytes 786440 | tf_op jit(solution)/shard_map/ppermute | solution.py:557
  104.7 7.7 %collective-permute-start.17 = (f32[64,1024]{1,0:T(8,128)S(1)}, f32[64,1024]{1,0:T(8,128)S(1)}, u32[]{:S(2)}, u32[]{:S(2)}) collective-permute-start(f32[64,1024]{1,0:T(8,128)S(1)} %get-tuple-element.139), channel_id=1, source_target_pairs={{0,8},{8,16},{16,24},{24,32},{32,40},{40,48},{48,56},{56,0},{64,72... | collective-permute-start | bytes 786440 | tf_op jit(solution)/shard_map/ppermute | solution.py:556
  108.0 6.4 %collective-permute-start.18 = (f32[64,1024]{1,0:T(8,128)S(1)}, f32[64,1024]{1,0:T(8,128)S(1)}, u32[]{:S(2)}, u32[]{:S(2)}) collective-permute-start(f32[64,1024]{1,0:T(8,128)S(1)} %get-tuple-element.140), channel_id=1, source_target_pairs={{0,56},{8,0},{16,8},{24,16},{32,24},{40,32},{48,40},{56,48},{64,12... | collective-permute-start | bytes 786440 | tf_op jit(solution)/shard_map/ppermute | solution.py:557
  115.6 7.7 %collective-permute-start.19 = (f32[64,1024]{1,0:T(8,128)S(1)}, f32[64,1024]{1,0:T(8,128)S(1)}, u32[]{:S(2)}, u32[]{:S(2)}) collective-permute-start(f32[64,1024]{1,0:T(8,128)S(1)} %get-tuple-element.143), channel_id=1, source_target_pairs={{0,8},{8,16},{16,24},{24,32},{32,40},{40,48},{48,56},{56,0},{64,72... | collective-permute-start | bytes 786440 | tf_op jit(solution)/shard_map/ppermute | solution.py:556
  118.2 6.4 %collective-permute-start.20 = (f32[64,1024]{1,0:T(8,128)S(1)}, f32[64,1024]{1,0:T(8,128)S(1)}, u32[]{:S(2)}, u32[]{:S(2)}) collective-permute-start(f32[64,1024]{1,0:T(8,128)S(1)} %get-tuple-element.144), channel_id=1, source_target_pairs={{0,56},{8,0},{16,8},{24,16},{32,24},{40,32},{48,40},{56,48},{64,12... | collective-permute-start | bytes 786440 | tf_op jit(solution)/shard_map/ppermute | solution.py:557
  127.6 0.7 copy-start.13
Sparse Core Ops, SparseCore 0:
  9.3 44.2 all-gather.5

commit v6 on v5

--- a/solution.py
+++ b/solution.py
@@ -11,10 +11,10 @@
 CAP = 32
 TOTAL_CAP = 68
 LIST = 72
-GROUP = 4
+GROUP = 8
 EXTRA = 16
 ROUND = 16
-LIMIT = 56
+LIMIT = 53
 HERE = 64
 PIECE = 16
 WIDTH = 128
@@ -71,7 +71,7 @@
 
 
 def home(row, col):
-    return jnp.minimum(row, col) // HERE
+    return jnp.minimum(row, col) >> 6
 
 
 class Part:
@@ -95,7 +95,7 @@
 
 
 def own_parts(ref):
-    return Part(ref, 0), Part(ref, 8), Part(ref, 16, OWN_WIDTH)
+    return Part(ref, 0), Part(ref, 8), Part(ref, 24, OWN_WIDTH)
 
 
 def moved_parts(ref):
@@ -109,13 +109,11 @@
         table[2, first + size + pad] = col
 
 
-def pack_kernel(facts, stored, *refs):
+def pack_kernel(here, rows, cols, count, stored, *refs):
     outs, (plan, mine_of, entries, sems) = refs[:XS - 1], refs[XS - 1:]
-    slots = stored.shape[0]
-    rows, cols = Part(facts, 8), Part(facts, 8 + slots)
     place, sizes, table = own_parts(plan)
     for each in range(3):
-        place[each] = facts[each]
+        place[each] = here[each]
     mine = place[0]
     low = mine * HERE
     fetch = pltpu.make_async_copy(stored.at[:, pl.ds(pl.multiple_of(place[1] * PIECE, PIECE), PIECE)], mine_of, sems.at[XS - 1])
@@ -125,7 +123,7 @@
 
     def sort_step(slot, _):
         row, col = rows[slot], cols[slot]
-        target = lax.rem(home(row, col) - mine + XS, XS)
+        target = (home(row, col) - mine) & (XS - 1)
         kind = jnp.where((target == 0) & (row - low >= HERE), XS, target)
         position = sizes[kind]
         at = kind * LIST + position
@@ -135,7 +133,7 @@
         sizes[kind] = position + 1
         return 0
 
-    lax.fori_loop(0, facts[3], sort_step, 0)
+    lax.fori_loop(0, count[0], sort_step, 0)
     over = jnp.int32(0)
     for j in range(1, XS):
         over = jnp.maximum(over, (sizes[j] > CAP).astype(jnp.int32))
@@ -149,7 +147,7 @@
         entries[j - 1, 2, 0] = over.astype(jnp.float32)
         entries[j - 1, 3, mine] = 0.0
         for other in range(1, XS):
-            entries[j - 1, 3, lax.rem(mine + other, XS)] = sizes[other].astype(jnp.float32)
+            entries[j - 1, 3, (mine + other) & (XS - 1)] = sizes[other].astype(jnp.float32)
 
         def move_step(item, _):
             at = j * LIST + item
@@ -166,28 +164,24 @@
         copy.wait()
 
 
-def pack(facts, integrals):
+def pack(place, rows, cols, count, integrals):
     slots = integrals.shape[0]
-    spec = pltpu.PrefetchScalarGridSpec(
-        num_scalar_prefetch=1,
-        grid=(1,),
-        in_specs=[pl.BlockSpec(memory_space=pl.ANY)],
-        out_specs=[pl.BlockSpec((CAP + 1, PIECE, WIDTH), lambda i, *_: (0, 0, 0))] * (XS - 1)
-        + [pl.BlockSpec(memory_space=pltpu.SMEM)],
+    vmem = pl.BlockSpec(memory_space=pltpu.VMEM)
+    smem = pl.BlockSpec(memory_space=pltpu.SMEM)
+    return pl.pallas_call(
+        pack_kernel,
+        in_specs=[smem] * 4 + [pl.BlockSpec(memory_space=pl.ANY)],
+        out_specs=[vmem] * (XS - 1) + [smem],
+        out_shape=[jax.ShapeDtypeStruct((CAP + 1, PIECE, WIDTH), jnp.float32)] * (XS - 1)
+        + [jax.ShapeDtypeStruct((24 + 3 * OWN_WIDTH,), jnp.int32)],
         scratch_shapes=[
             pltpu.VMEM((slots, PIECE, WIDTH), jnp.float32),
             pltpu.SMEM((XS - 1, 8, WIDTH), jnp.float32),
             pltpu.SemaphoreType.DMA((XS,)),
         ],
-    )
-    return pl.pallas_call(
-        pack_kernel,
-        grid_spec=spec,
-        out_shape=[jax.ShapeDtypeStruct((CAP + 1, PIECE, WIDTH), jnp.float32)] * (XS - 1)
-        + [jax.ShapeDtypeStruct((16 + 3 * OWN_WIDTH,), jnp.int32)],
         compiler_params=pltpu.CompilerParams(vmem_limit_bytes=8 * 2**20),
         name="pack",
-    )(facts, integrals)
+    )(place, rows, cols, count, integrals)
 
 
 def compact_kernel(plan, *refs):
@@ -209,7 +203,7 @@
     for j in range(XS - 1):
         over = over | (entries[j, 2, 0] > 0.5)
     for j in range(XS):
-        there = lax.rem(mine + j, XS)
+        there = (mine + j) & (XS - 1)
         total = jnp.int32(0) if j == 0 else sizes[j]
         for source in range(XS - 1):
             total = total + entries[source, 3, there].astype(jnp.int32)
@@ -273,16 +267,16 @@
             products.append(product[:, :WIDTH] + product[:, WIDTH:])
         for member in range(GROUP):
             col = table[2, first + group * GROUP + member] - low
-            lanes = pl.ds(pl.multiple_of(lax.rem(col, ZS) * WIDTH, WIDTH), WIDTH)
-            sums[lax.div(col, ZS), :, lanes] += products[member]
+            lanes = pl.ds(pl.multiple_of((col & (ZS - 1)) * WIDTH, WIDTH), WIDTH)
+            sums[(col >> 3), :, lanes] += products[member]
         return 0
 
-    lax.fori_loop(0, lax.div(size + GROUP - 1, GROUP), step, 0)
+    lax.fori_loop(0, (size + GROUP - 1) >> 3, step, 0)
 
 
 def split_at(source, row):
-    lanes = pl.ds(pl.multiple_of(lax.rem(row, ZS) * WIDTH, WIDTH), WIDTH)
-    return jnp.concatenate(split_of(source[lax.div(row, ZS), :, lanes]), axis=1)
+    lanes = pl.ds(pl.multiple_of((row & (ZS - 1)) * WIDTH, WIDTH), WIDTH)
+    return jnp.concatenate(split_of(source[(row >> 3), :, lanes]), axis=1)
 
 
 def start_own(table, first, size, stored_hbm, stored, sems):
@@ -302,13 +296,13 @@
 
 
 def piece_rows(place):
-    my_y = lax.div(place[1], 2)
-    my_core = lax.rem(place[1], 2)
+    my_y = place[1] >> 1
+    my_core = place[1] & 1
     rows = []
     for shift in range(YS):
         for swapped in range(2):
             core = my_core if swapped == 0 else 1 - my_core
-            rows.append(pl.multiple_of((lax.rem(my_y - shift + YS, YS) * 2 + core) * PIECE, PIECE))
+            rows.append(pl.multiple_of((((my_y - shift) & (YS - 1)) * 2 + core) * PIECE, PIECE))
     return rows
 
 
@@ -403,7 +397,7 @@
         pltpu.make_async_copy(sums.at[ZS + 1 - soon], later_hbm, sems.at[last + 1]),
     ]
     for z in range(ZS):
-        block = lax.rem(place[2] + z, ZS)
+        block = (place[2] + z) & (ZS - 1)
         backs.append(pltpu.make_async_copy(sums.at[block], out_hbm.at[z], sems.at[last + 2 + z]))
     for back in backs:
         back.start()
@@ -418,7 +412,6 @@
     sums_hbm, extra, own_tiles, moved_tiles, sums, touched, sems, own_sems, moved_sems = refs
     low = place[0] * HERE
     rows_of = piece_rows(place)
-    over = totals[2]
     own_first = XS * LIST
 
     left = lambda row: split_at(extra, row - HERE)
@@ -456,16 +449,16 @@
 
     def touch(table, first, size):
         def one(item, _):
-            touched[lax.div(table[2, first + item] - low, ZS)] = 1
+            touched[(table[2, first + item] - low) >> 3] = 1
             return 0
 
         lax.fori_loop(0, size, one, 0)
 
     def spot(z):
-        return lax.rem(z - place[2] + ZS, ZS)
-
-
-    @pl.when((sizes[XS] + totals[1] > 0) & (over == 0))
+        return (z - place[2]) & (ZS - 1)
+
+
+    @pl.when(sizes[XS] + totals[1] > 0)
     def _():
         first_round = start_round(0)
         copies = [pltpu.make_async_copy(extra_hbm.at[z], extra.at[z], sems.at[ZS + z]) for z in range(2)]
@@ -485,19 +478,12 @@
         for z in range(ZS):
             pl.when(touched[z] > 0)(inward[z].wait)
         finish_round(0, *first_round)
-        rounds = lax.div(jnp.maximum(sizes[XS], totals[1]) + ROUND - 1, ROUND)
+        rounds = (jnp.maximum(sizes[XS], totals[1]) + ROUND - 1) >> 4
         lax.fori_loop(1, rounds, whole_round, 0)
         for z in range(ZS):
             pl.when(touched[z] > 0)(outward[z].start)
         for z in range(ZS):
             pl.when(touched[z] > 0)(outward[z].wait)
-
-    @pl.when(over > 0)
-    def _():
-        sums[...] = jnp.full_like(sums, jnp.nan)
-        whole = pltpu.make_async_copy(sums.at[pl.ds(0, ZS)], sums_hbm, sems.at[0])
-        whole.start()
-        whole.wait()
 
 
 def call(kernel, name, scalars, arrays, outs, scratch, aliases):
@@ -571,20 +557,21 @@
     my_tile = lax.axis_index("tile")
     my_x = my_tile // ZS
     my_z = lax.rem(my_tile, ZS)
-    place = jnp.stack([my_x, lax.axis_index("pair"), my_z, tile_count[0], my_x, my_x, my_x, my_x]).astype(jnp.int32)
-    facts = jnp.concatenate([place, tile_rows, tile_cols])
+    place = jnp.stack([my_x, lax.axis_index("pair"), my_z]).astype(jnp.int32)
 
     near = lax.all_gather(amplitudes, "tile", axis=0, axis_index_groups=Z_GROUPS)
 
-    *packed, plan = pack(facts, integrals)
+    *packed, plan = pack(place, tile_rows, tile_cols, tile_count, integrals)
     arrived = [lax.ppermute(packed[step - 1], "tile", x_shift(step)) for step in range(1, XS)]
     mine, moved_plan = compact(plan, arrived)
     along_y = [mine] + [lax.ppermute(mine, "pair", y_shift(step)) for step in range(1, YS)]
     across = lax.ppermute(mine, "pair", CORE_SWAP)
-    along_y[YS - 1], across = lax.optimization_barrier((along_y[YS - 1], across))
+    marks = moved_plan[2:3].astype(jnp.float32)
+    for step in (1, 2, 4):
+        marks = jnp.maximum(marks, lax.ppermute(marks, "tile", z_shift(step)))
     split, first = prepare(near)
     extra = lax.ppermute(first, "tile", x_shift(-1))
-    along_y[1], along_y[2], first = lax.optimization_barrier((along_y[1], along_y[2], first))
+    along_y[1], along_y[2], first, marks = lax.optimization_barrier((along_y[1], along_y[2], first, marks))
     pieces = [mine, across]
     for piece in along_y[1:]:
         pieces += [piece, lax.ppermute(piece, "pair", CORE_SWAP)]
@@ -610,7 +597,7 @@
         full = dense_ladder(amplitudes, integrals, tile_rows, tile_cols, tile_count)
         return (driver + full) / denominator
 
-    return lax.cond(jnp.isnan(ladder[0, 0]), slow, lambda: result)
+    return lax.cond(marks[0] > 0.5, slow, lambda: result)
 
 
 def solution(mesh):

time: 135 us -> 129 us (0.956)
  waiting for transfers between devices: 65 us -> 50.7 us
  starting transfers between devices: 26.9 us -> 36.3 us
    ppermute x3, waiting for transfers between devices: 23.6 us -> 0.01 us  [shards(): lax.ppermute(mine, 'pair', y_shift(step))]
    ppermute x0 -> x3, waiting for transfers between devices: none -> 11.2 us  [shards(): marks = jnp.maximum(marks, lax.ppermute(marks, 'tile', z_shift(step)))]
    ppermute x0 -> x3, starting transfers between devices: none -> 10 us  [shards(): marks = jnp.maximum(marks, lax.ppermute(marks, 'tile', z_shift(step)))]
    ppermute x4, waiting for transfers between devices: 4.48 us -> 1.82 us  [ring_sum(): down = lax.ppermute(down, 'tile', z_shift(-1))]
  transfers between devices with their start and end apart: 22 -> 25, of which waited for: 16 -> 16; matrix products, arithmetic and copies ran while one was open for 1% -> 1% of each run, Pallas kernels for 14% -> 14%
where the time goes in v6:
time: 129 us
  waiting for transfers between devices  50.7 us (39%)
  starting transfers between devices  36.3 us (28%)
  Pallas kernels  17.7 us (14%)
  between operations  16.5 us (13%)
  other arithmetic  5.74 us (4%)
  local copies, waits for them, and re-layouts  2.12 us (2%)
    ppermute x4, waiting for transfers between devices, ring_sum(): up = lax.ppermute(up, 'tile', z_shift(1))  15.6 us
    ppermute x3, waiting for transfers between devices, shards(): lax.ppermute(packed[step - 1], 'tile', x_shift(step))  12.5 us
    ppermute x3, waiting for transfers between devices, shards(): marks = jnp.maximum(marks, lax.ppermute(marks, 'tile', z_shift(step)))  11.2 us
    ppermute x4, starting transfers between devices, ring_sum(): down = lax.ppermute(down, 'tile', z_shift(-1))  10.6 us
    ppermute x3, starting transfers between devices, shards(): marks = jnp.maximum(marks, lax.ppermute(marks, 'tile', z_shift(step)))  10 us
    pallas_call x2, Pallas kernels, call(): pl.pallas_call(kernel, in_specs=[smem] * len(scalars) + [anywhere] * len(...  8.87 us
    ppermute x4, starting transfers between devices, ring_sum(): up = lax.ppermute(up, 'tile', z_shift(1))  5.44 us
    ppermute x3, starting transfers between devices, shards(): lax.ppermute(mine, 'pair', y_shift(step))  4.75 us
  transfers between devices with their start and end apart: 25, of which 16 were waited for; matrix products, arithmetic and copies ran while one was open for 1% of the time, Pallas kernels for 14%

profile of v6, /device:TPU:6, one launch (start us, length us, event | category | flops | bytes accessed | tf_op | source)
XLA Modules:
  0.0 129.1 jit_solution(15828778646805154817)
XLA Ops:
  6.5 0.7 all-gather.6.cloned.1.call-update
  8.0 3.4 %pack.1 = (f32[33,16,128]{2,1,0:T(8,128)S(1)}, f32[33,16,128]{2,1,0:T(8,128)S(1)}, f32[33,16,128]{2,1,0:T(8,128)S(1)}, s32[1104]{0:T(1024)S(1)}) custom-call(s32[3]{0:T(128)S(1)} %pad_add_fusion.here, s32[64]{0:T(128)} %rows.1, s32[64]{0:T(128)} %cols.1, s32[1]{0:T(128)S(6)} %copy.32.count, f32[64,128,128]{2,1,0:T(8,128)} %stored_hbm.3), custom_call_target="tpu_custom_call" | custom-call | tf_op jit(solution)/shard_map/pack/pallas_call | solution.py:171
  11.4 2.3 %collective-permute-start = (f32[33,16,128]{2,1,0:T(8,128)S(1)}, f32[33,16,128]{2,1,0:T(8,128)S(1)}, u32[]{:S(2)}, u32[]{:S(2)}) collective-permute-start(f32[33,16,128]{2,1,0:T(8,128)S(1)} %get-tuple-element.152), channel_id=1, source_target_pairs={{0,64},{8,72},{16,80},{24,88},{32,96},{40,104},{48,112},{56,120},{... | collective-permute-start | bytes 811016 | tf_op jit(solution)/shard_map/ppermute | solution.py:565
  13.7 0.8 collective-permute-start.1
  14.6 6.2 %collective-permute-done.refs_0_ = f32[33,16,128]{2,1,0:T(8,128)S(1)} collective-permute-done((f32[33,16,128]{2,1,0:T(8,128)S(1)}, f32[33,16,128]{2,1,0:T(8,128)S(1)}, u32[]{:S(2)}, u32[]{:S(2)}) %collective-permute-start) | collective-permute-done | bytes 270368 | tf_op jit(solution)/shard_map/ppermute | solution.py:565
  20.8 3.4 %collective-permute-done.1.refs_1_ = f32[33,16,128]{2,1,0:T(8,128)S(1)} collective-permute-done((f32[33,16,128]{2,1,0:T(8,128)S(1)}, f32[33,16,128]{2,1,0:T(8,128)S(1)}, u32[]{:S(2)}, u32[]{:S(2)}) %collective-permute-start.1) | collective-permute-done | bytes 270368 | tf_op jit(solution)/shard_map/ppermute | solution.py:565
  24.2 2.9 %collective-permute-done.2.refs_2_ = f32[33,16,128]{2,1,0:T(8,128)S(1)} collective-permute-done((f32[33,16,128]{2,1,0:T(8,128)S(1)}, f32[33,16,128]{2,1,0:T(8,128)S(1)}, u32[]{:S(2)}, u32[]{:S(2)}) %collective-permute-start.2) | collective-permute-done | bytes 270368 | tf_op jit(solution)/shard_map/ppermute | solution.py:565
  27.1 2.9 %compact.1 = (f32[68,16,128]{2,1,0:T(8,128)S(1)}, s32[440]{0:T(512)S(1)}) custom-call(s32[1104]{0:T(1024)S(1)} %get-tuple-element.151.plan, f32[33,16,128]{2,1,0:T(8,128)S(1)} %collective-permute-done.refs_0_, f32[33,16,128]{2,1,0:T(8,128)S(1)} %collective-permute-done.1.refs_1_, f32[33,16,128]{2,1,0:T(8,128)S(1)} %collective-permute-done.2.refs_2_), custom_call_target="tpu_custom_call" | custom-call | tf_op jit(solution)/shard_map/compact/pallas_call | solution.py:236
  30.0 3.2 %collective-permute-start.11 = (f32[68,16,128]{2,1,0:T(8,128)S(1)}, f32[68,16,128]{2,1,0:T(8,128)S(1)}, u32[]{:S(2)}, u32[]{:S(2)}) collective-permute-start(f32[68,16,128]{2,1,0:T(8,128)S(1)} %get-tuple-element.155.refs_0_), channel_id=1, source_target_pairs={{0,6},{1,7},{2,0},{3,1},{4,2},{5,3},{6,4},{7,5},{8,14},{9,15},{10,... | collective-permute-start | bytes 1671176 | tf_op jit(solution)/shard_map/ppermute | solution.py:567
  33.1 0.6 collective-permute-start.4
  33.8 1.0 collective-permute-start.3
  34.8 0.6 slice.34
  35.9 3.2 %collective-permute-start.5 = (f32[1]{0:T(128)}, f32[1]{0:T(128)}, u32[]{:S(2)}, u32[]{:S(2)}) collective-permute-start(f32[1]{0:T(128)} %convert_element_type.16), channel_id=1, source_target_pairs={{0,8},{8,16},{16,24},{24,32},{32,40},{40,48},{48,56},{56,0},{64,72... | collective-permute-start | bytes 20 | tf_op jit(solution)/shard_map/ppermute | solution.py:571
  39.1 4.5 %collective-permute-done.5 = f32[1]{0:T(128)} collective-permute-done((f32[1]{0:T(128)}, f32[1]{0:T(128)}, u32[]{:S(2)}, u32[]{:S(2)}) %collective-permute-start.5) | collective-permute-done | bytes 36 | tf_op jit(solution)/shard_map/ppermute | solution.py:571
  44.1 1.4 %collective-permute-start.6 = (f32[1]{0:T(128)}, f32[1]{0:T(128)}, u32[]{:S(2)}, u32[]{:S(2)}) collective-permute-start(f32[1]{0:T(128)} %max.9), channel_id=1, source_target_pairs={{0,16},{8,24},{16,32},{24,40},{32,48},{40,56},{48,0},{56,8},{64,80... | collective-permute-start | bytes 20 | tf_op jit(solution)/shard_map/ppermute | solution.py:571
  45.5 4.5 %collective-permute-done.6 = f32[1]{0:T(128)} collective-permute-done((f32[1]{0:T(128)}, f32[1]{0:T(128)}, u32[]{:S(2)}, u32[]{:S(2)}) %collective-permute-start.6) | collective-permute-done | bytes 36 | tf_op jit(solution)/shard_map/ppermute | solution.py:571
  50.5 5.4 %collective-permute-start.7 = (f32[1]{0:T(128)}, f32[1]{0:T(128)}, u32[]{:S(2)}, u32[]{:S(2)}) collective-permute-start(f32[1]{0:T(128)} %max.10), channel_id=1, source_target_pairs={{0,32},{8,40},{16,48},{24,56},{32,0},{40,8},{48,16},{56,24},{64,96... | collective-permute-start | bytes 20 | tf_op jit(solution)/shard_map/ppermute | solution.py:571
  56.0 2.2 %collective-permute-done.7 = f32[1]{0:T(128)} collective-permute-done((f32[1]{0:T(128)}, f32[1]{0:T(128)}, u32[]{:S(2)}, u32[]{:S(2)}) %collective-permute-start.7) | collective-permute-done | bytes 36 | tf_op jit(solution)/shard_map/ppermute | solution.py:571
  58.9 2.6 %prepare.1 = (bf16[64,64,256]{2,1,0:T(8,128)(2,1)}, f32[2,64,1024]{2,1,0:T(8,128)S(1)}) custom-call(f32[8,64,1024]{2,1,0:T(8,128)} %bitcast.79), custom_call_target="tpu_custom_call" | custom-call | tf_op jit(solution)/shard_map/prepare/pallas_call | solution.py:332
  61.5 0.5 collective-permute-start.9
  62.4 1.4 %collective-permute-done.9.refs_3_ = f32[68,16,128]{2,1,0:T(8,128)S(1)} collective-permute-done((f32[68,16,128]{2,1,0:T(8,128)}, f32[68,16,128]{2,1,0:T(8,128)S(1)}, u32[]{:S(2)}, u32[]{:S(2)}) %collective-permute-start.9) | collective-permute-done | bytes 557088 | tf_op jit(solution)/shard_map/ppermute | solution.py:577
  63.7 0.6 collective-permute-done.10.refs_5_
  64.5 0.6 copy-done.6
  65.1 7.9 %main.1 = (f32[8,64,1024]{2,1,0:T(8,128)}, f32[64,1024]{1,0:T(8,128)S(1)}, f32[64,1024]{1,0:T(8,128)S(1)}) custom-call(s32[1104]{0:T(1024)S(1)} %get-tuple-element.151.plan, s32[440]{0:T(512)S(1)} %get-tuple-element.157.moved_plan, bf16[64,64,256]{2,1,0:T(8,128)(2,1)} %get-tuple-element.159.split_hbm, f32[64,128,128]{2,1,0:T(8,128)} %stored_hbm.3, ...), custom_call_target="tpu_custom_call" | custom-call | flops 1000000 | bytes 10000 | tf_op jit(solution)/shard_map/main/pallas_call | solution.py:492
  73.2 1.2 collective-permute-start.15
  74.4 3.1 %collective-permute-done.13.extra_hbm = f32[2,64,1024]{2,1,0:T(8,128)S(1)} collective-permute-done((f32[2,64,1024]{2,1,0:T(8,128)S(1)}, f32[2,64,1024]{2,1,0:T(8,128)S(1)}, u32[]{:S(2)}, u32[]{:S(2)}) %collective-permute-start.13) | collective-permute-done | bytes 524320 | tf_op jit(solution)/shard_map/ppermute | solution.py:573
  77.6 1.0 late.1
  78.5 3.7 %collective-permute-done.14 = f32[64,1024]{1,0:T(8,128)S(1)} collective-permute-done((f32[64,1024]{1,0:T(8,128)S(1)}, f32[64,1024]{1,0:T(8,128)S(1)}, u32[]{:S(2)}, u32[]{:S(2)}) %collective-permute-start.14) | collective-permute-done | bytes 262176 | tf_op jit(solution)/shard_map/ppermute | solution.py:580
  82.3 1.0 fusion.26
  83.3 0.9 collective-permute-start.16
  84.2 4.9 %collective-permute-start.17 = (f32[32,1024]{1,0:T(8,128)S(1)}, f32[32,1024]{1,0:T(8,128)S(1)}, u32[]{:S(2)}, u32[]{:S(2)}) collective-permute-start(f32[32,1024]{1,0:T(8,128)S(1)} %get-tuple-element.166), channel_id=1, source_target_pairs={{0,56},{8,0},{16,8},{24,16},{32,24},{40,32},{48,40},{56,48},{64,12... | collective-permute-start | bytes 393224 | tf_op jit(solution)/shard_map/ppermute | solution.py:543
  89.0 2.9 %collective-permute-done.16 = f32[32,1024]{1,0:T(8,128)S(1)} collective-permute-done((f32[32,1024]{1,0:T(8,128)S(1)}, f32[32,1024]{1,0:T(8,128)S(1)}, u32[]{:S(2)}, u32[]{:S(2)}) %collective-permute-start.16) | collective-permute-done | bytes 131104 | tf_op jit(solution)/shard_map/ppermute | solution.py:542
  91.9 1.1 fusion.23
  93.1 3.4 %collective-permute-start.19 = (f32[64,1024]{1,0:T(8,128)S(1)}, f32[64,1024]{1,0:T(8,128)S(1)}, u32[]{:S(2)}, u32[]{:S(2)}) collective-permute-start(f32[64,1024]{1,0:T(8,128)S(1)} %get-tuple-element.170), channel_id=1, source_target_pairs={{0,56},{8,0},{16,8},{24,16},{32,24},{40,32},{48,40},{56,48},{64,12... | collective-permute-start | bytes 786440 | tf_op jit(solution)/shard_map/ppermute | solution.py:543
  96.5 4.3 %collective-permute-done.18 = f32[64,1024]{1,0:T(8,128)S(1)} collective-permute-done((f32[64,1024]{1,0:T(8,128)S(1)}, f32[64,1024]{1,0:T(8,128)S(1)}, u32[]{:S(2)}, u32[]{:S(2)}) %collective-permute-start.18) | collective-permute-done | bytes 262176 | tf_op jit(solution)/shard_map/ppermute | solution.py:542
  100.8 1.2 fusion.19
  101.9 1.8 %collective-permute-start.20 = (f32[64,1024]{1,0:T(8,128)S(1)}, f32[64,1024]{1,0:T(8,128)S(1)}, u32[]{:S(2)}, u32[]{:S(2)}) collective-permute-start(f32[64,1024]{1,0:T(8,128)S(1)} %get-tuple-element.173), channel_id=1, source_target_pairs={{0,8},{8,16},{16,24},{24,32},{32,40},{40,48},{48,56},{56,0},{64,72... | collective-permute-start | bytes 786440 | tf_op jit(solution)/shard_map/ppermute | solution.py:542
  103.8 1.7 %collective-permute-start.21 = (f32[64,1024]{1,0:T(8,128)S(1)}, f32[64,1024]{1,0:T(8,128)S(1)}, u32[]{:S(2)}, u32[]{:S(2)}) collective-permute-start(f32[64,1024]{1,0:T(8,128)S(1)} %get-tuple-element.174), channel_id=1, source_target_pairs={{0,56},{8,0},{16,8},{24,16},{32,24},{40,32},{48,40},{56,48},{64,12... | collective-permute-start | bytes 786440 | tf_op jit(solution)/shard_map/ppermute | solution.py:543
  105.4 4.3 %collective-permute-done.20 = f32[64,1024]{1,0:T(8,128)S(1)} collective-permute-done((f32[64,1024]{1,0:T(8,128)S(1)}, f32[64,1024]{1,0:T(8,128)S(1)}, u32[]{:S(2)}, u32[]{:S(2)}) %collective-permute-start.20) | collective-permute-done | bytes 262176 | tf_op jit(solution)/shard_map/ppermute | solution.py:542
  109.7 0.4 collective-permute-done.21
  110.1 1.2 fusion.15
  111.3 2.7 %collective-permute-start.22 = (f32[64,1024]{1,0:T(8,128)S(1)}, f32[64,1024]{1,0:T(8,128)S(1)}, u32[]{:S(2)}, u32[]{:S(2)}) collective-permute-start(f32[64,1024]{1,0:T(8,128)S(1)} %get-tuple-element.177), channel_id=1, source_target_pairs={{0,8},{8,16},{16,24},{24,32},{32,40},{40,48},{48,56},{56,0},{64,72... | collective-permute-start | bytes 786440 | tf_op jit(solution)/shard_map/ppermute | solution.py:542
  114.0 0.6 collective-permute-start.23
  114.7 4.2 %collective-permute-done.22 = f32[64,1024]{1,0:T(8,128)S(1)} collective-permute-done((f32[64,1024]{1,0:T(8,128)S(1)}, f32[64,1024]{1,0:T(8,128)S(1)}, u32[]{:S(2)}, u32[]{:S(2)}) %collective-permute-start.22) | collective-permute-done | bytes 262176 | tf_op jit(solution)/shard_map/ppermute | solution.py:542
  119.0 1.4 %collective-permute-done.23 = f32[64,1024]{1,0:T(8,128)S(1)} collective-permute-done((f32[64,1024]{1,0:T(8,128)S(1)}, f32[64,1024]{1,0:T(8,128)S(1)}, u32[]{:S(2)}, u32[]{:S(2)}) %collective-permute-start.23) | collective-permute-done | bytes 262176 | tf_op jit(solution)/shard_map/ppermute | solution.py:543
  120.4 1.2 conditional.1
  120.4 1.1 fusion.3
  121.6 0.7 copy-done.8
  (41 shorter events, 1.3 us)
Async XLA Ops:
  6.5 52.3 %all-gather.6.cloned.1.call-start = ((), (), s32[]{:S(2)}) async-start(), calls=%async_computation.3 | async-start | bytes 2359296 | tf_op jit(solution)/shard_map/all_gather | solution.py:562
  11.4 9.4 %collective-permute-start = (f32[33,16,128]{2,1,0:T(8,128)S(1)}, f32[33,16,128]{2,1,0:T(8,128)S(1)}, u32[]{:S(2)}, u32[]{:S(2)}) collective-permute-start(f32[33,16,128]{2,1,0:T(8,128)S(1)} %get-tuple-element.152), channel_id=1, source_target_pairs={{0,64},{8,72},{16,80},{24,88},{32,96},{40,104},{48,112},{56,120},{... | collective-permute-start | bytes 811016 | tf_op jit(solution)/shard_map/ppermute | solution.py:565
  13.7 10.6 %collective-permute-start.1 = (f32[33,16,128]{2,1,0:T(8,128)S(1)}, f32[33,16,128]{2,1,0:T(8,128)S(1)}, u32[]{:S(2)}, u32[]{:S(2)}) collective-permute-start(f32[33,16,128]{2,1,0:T(8,128)S(1)} %get-tuple-element.153), channel_id=1, source_target_pairs={{0,128},{8,136},{16,144},{24,152},{32,160},{40,168},{48,176},{56,1... | collective-permute-start | bytes 811016 | tf_op jit(solution)/shard_map/ppermute | solution.py:565
  14.4 12.7 %collective-permute-start.2 = (f32[33,16,128]{2,1,0:T(8,128)S(1)}, f32[33,16,128]{2,1,0:T(8,128)S(1)}, u32[]{:S(2)}, u32[]{:S(2)}) collective-permute-start(f32[33,16,128]{2,1,0:T(8,128)S(1)} %get-tuple-element.154), channel_id=1, source_target_pairs={{0,192},{8,200},{16,208},{24,216},{32,224},{40,232},{48,240},{56,2... | collective-permute-start | bytes 811016 | tf_op jit(solution)/shard_map/ppermute | solution.py:565
  30.0 34.4 %copy-start = (f32[68,16,128]{2,1,0:T(8,128)}, f32[68,16,128]{2,1,0:T(8,128)S(1)}, u32[]{:S(2)}) copy-start(f32[68,16,128]{2,1,0:T(8,128)S(1)} %get-tuple-element.155.refs_0_) | copy-start | bytes 1671172
  30.0 28.7 %collective-permute-start.11 = (f32[68,16,128]{2,1,0:T(8,128)S(1)}, f32[68,16,128]{2,1,0:T(8,128)S(1)}, u32[]{:S(2)}, u32[]{:S(2)}) collective-permute-start(f32[68,16,128]{2,1,0:T(8,128)S(1)} %get-tuple-element.155.refs_0_), channel_id=1, source_target_pairs={{0,6},{1,7},{2,0},{3,1},{4,2},{5,3},{6,4},{7,5},{8,14},{9,15},{10,... | collective-permute-start | bytes 1671176 | tf_op jit(solution)/shard_map/ppermute | solution.py:567
  33.1 28.3 %collective-permute-start.4 = (f32[68,16,128]{2,1,0:T(8,128)S(1)}, f32[68,16,128]{2,1,0:T(8,128)S(1)}, u32[]{:S(2)}, u32[]{:S(2)}) collective-permute-start(f32[68,16,128]{2,1,0:T(8,128)S(1)} %get-tuple-element.155.refs_0_), channel_id=1, source_target_pairs={{0,4},{1,5},{2,6},{3,7},{4,0},{5,1},{6,2},{7,3},{8,12},{9,13},{10,... | collective-permute-start | bytes 1671176 | tf_op jit(solution)/shard_map/ppermute | solution.py:567
  33.8 27.7 %collective-permute-start.3 = (f32[68,16,128]{2,1,0:T(8,128)S(1)}, f32[68,16,128]{2,1,0:T(8,128)}, u32[]{:S(2)}, u32[]{:S(2)}) collective-permute-start(f32[68,16,128]{2,1,0:T(8,128)S(1)} %get-tuple-element.155.refs_0_), channel_id=1, source_target_pairs={{0,2},{1,3},{2,4},{3,5},{4,6},{5,7},{6,0},{7,1},{8,10},{9,11},{10,... | collective-permute-start | bytes 1671176 | tf_op jit(solution)/shard_map/ppermute | solution.py:567
  34.8 27.6 %collective-permute-start.8 = (f32[68,16,128]{2,1,0:T(8,128)S(1)}, f32[68,16,128]{2,1,0:T(8,128)}, u32[]{:S(2)}, u32[]{:S(2)}) collective-permute-start(f32[68,16,128]{2,1,0:T(8,128)S(1)} %get-tuple-element.155.refs_0_), channel_id=1, source_target_pairs={{0,1},{1,0},{2,3},{3,2},{4,5},{5,4},{6,7},{7,6},{8,9},{9,8},{10,11... | collective-permute-start | bytes 1671176 | tf_op jit(solution)/shard_map/ppermute | solution.py:568
  35.9 7.7 %collective-permute-start.5 = (f32[1]{0:T(128)}, f32[1]{0:T(128)}, u32[]{:S(2)}, u32[]{:S(2)}) collective-permute-start(f32[1]{0:T(128)} %convert_element_type.16), channel_id=1, source_target_pairs={{0,8},{8,16},{16,24},{24,32},{32,40},{40,48},{48,56},{56,0},{64,72... | collective-permute-start | bytes 20 | tf_op jit(solution)/shard_map/ppermute | solution.py:571
  44.1 5.8 %collective-permute-start.6 = (f32[1]{0:T(128)}, f32[1]{0:T(128)}, u32[]{:S(2)}, u32[]{:S(2)}) collective-permute-start(f32[1]{0:T(128)} %max.9), channel_id=1, source_target_pairs={{0,16},{8,24},{16,32},{24,40},{32,48},{40,56},{48,0},{56,8},{64,80... | collective-permute-start | bytes 20 | tf_op jit(solution)/shard_map/ppermute | solution.py:571
  50.5 7.6 %collective-permute-start.7 = (f32[1]{0:T(128)}, f32[1]{0:T(128)}, u32[]{:S(2)}, u32[]{:S(2)}) collective-permute-start(f32[1]{0:T(128)} %max.10), channel_id=1, source_target_pairs={{0,32},{8,40},{16,48},{24,56},{32,0},{40,8},{48,16},{56,24},{64,96... | collective-permute-start | bytes 20 | tf_op jit(solution)/shard_map/ppermute | solution.py:571
  58.7 5.6 %copy-start.3 = (f32[68,16,128]{2,1,0:T(8,128)}, f32[68,16,128]{2,1,0:T(8,128)S(1)}, u32[]{:S(2)}) copy-start(f32[68,16,128]{2,1,0:T(8,128)S(1)} %collective-permute-done.11.refs_6_) | copy-start | bytes 1671172
  58.7 3.6 %collective-permute-start.12 = (f32[68,16,128]{2,1,0:T(8,128)S(1)}, f32[68,16,128]{2,1,0:T(8,128)}, u32[]{:S(2)}, u32[]{:S(2)}) collective-permute-start(f32[68,16,128]{2,1,0:T(8,128)S(1)} %collective-permute-done.11.refs_6_), channel_id=1, source_target_pairs={{0,1},{1,0},{2,3},{3,2},{4,5},{5,4},{6,7},{7,6},{8,9},{9,8},{10,11... | collective-permute-start | bytes 1671176 | tf_op jit(solution)/shard_map/ppermute | solution.py:577
  61.4 2.9 %copy-start.4 = (f32[68,16,128]{2,1,0:T(8,128)}, f32[68,16,128]{2,1,0:T(8,128)S(1)}, u32[]{:S(2)}) copy-start(f32[68,16,128]{2,1,0:T(8,128)S(1)} %collective-permute-done.4.refs_4_) | copy-start | bytes 1671172
  61.5 2.3 %collective-permute-start.9 = (f32[68,16,128]{2,1,0:T(8,128)}, f32[68,16,128]{2,1,0:T(8,128)S(1)}, u32[]{:S(2)}, u32[]{:S(2)}) collective-permute-start(f32[68,16,128]{2,1,0:T(8,128)} %collective-permute-done.3.refs_2_), channel_id=1, source_target_pairs={{0,1},{1,0},{2,3},{3,2},{4,5},{5,4},{6,7},{7,6},{8,9},{9,8},{10,11... | collective-permute-start | bytes 1671176 | tf_op jit(solution)/shard_map/ppermute | solution.py:577
  61.9 2.4 %collective-permute-start.10 = (f32[68,16,128]{2,1,0:T(8,128)S(1)}, f32[68,16,128]{2,1,0:T(8,128)S(1)}, u32[]{:S(2)}, u32[]{:S(2)}) collective-permute-start(f32[68,16,128]{2,1,0:T(8,128)S(1)} %collective-permute-done.4.refs_4_), channel_id=1, source_target_pairs={{0,1},{1,0},{2,3},{3,2},{4,5},{5,4},{6,7},{7,6},{8,9},{9,8},{10,11... | collective-permute-start | bytes 1671176 | tf_op jit(solution)/shard_map/ppermute | solution.py:577
  62.1 15.5 %collective-permute-start.13 = (f32[2,64,1024]{2,1,0:T(8,128)S(1)}, f32[2,64,1024]{2,1,0:T(8,128)S(1)}, u32[]{:S(2)}, u32[]{:S(2)}) collective-permute-start(f32[2,64,1024]{2,1,0:T(8,128)S(1)} %get-tuple-element.156), channel_id=1, source_target_pairs={{0,192},{8,200},{16,208},{24,216},{32,224},{40,232},{48,240},{56,2... | collective-permute-start | bytes 1572872 | tf_op jit(solution)/shard_map/ppermute | solution.py:573
  63.7 0.8 copy-start.5
  64.3 0.8 copy-start.6
  73.0 9.2 %collective-permute-start.14 = (f32[64,1024]{1,0:T(8,128)S(1)}, f32[64,1024]{1,0:T(8,128)S(1)}, u32[]{:S(2)}, u32[]{:S(2)}) collective-permute-start(f32[64,1024]{1,0:T(8,128)S(1)} %get-tuple-element.163), channel_id=1, source_target_pairs={{0,64},{8,72},{16,80},{24,88},{32,96},{40,104},{48,112},{56,120},{... | collective-permute-start | bytes 786440 | tf_op jit(solution)/shard_map/ppermute | solution.py:580
  73.2 18.7 %collective-permute-start.15 = (f32[64,1024]{1,0:T(8,128)S(1)}, f32[64,1024]{1,0:T(8,128)S(1)}, u32[]{:S(2)}, u32[]{:S(2)}) collective-permute-start(f32[64,1024]{1,0:T(8,128)S(1)} %get-tuple-element.164), channel_id=1, source_target_pairs={{0,64},{8,72},{16,80},{24,88},{32,96},{40,104},{48,112},{56,120},{... | collective-permute-start | bytes 786440 | tf_op jit(solution)/shard_map/ppermute | solution.py:581
  77.5 37.1 %copy-start.9 = (f32[1024]{0:T(1024)S(1)}, f32[1024]{0:T(1024)}, u32[]{:S(2)}) copy-start(f32[1024]{0:T(1024)} %param.21) | copy-start | bytes 12292
  77.5 37.1 %copy-start.10 = (f32[64]{0:T(128)S(1)}, f32[64]{0:T(128)}, u32[]{:S(2)}) copy-start(f32[64]{0:T(128)} %param.20) | copy-start | bytes 772
  77.5 42.8 %copy-start.1 = (s32[64]{0:T(128)S(1)}, s32[64]{0:T(128)}, u32[]{:S(2)}) copy-start(s32[64]{0:T(128)} %rows.1) | copy-start | bytes 772
  77.5 42.8 %copy-start.2 = (s32[64]{0:T(128)S(1)}, s32[64]{0:T(128)}, u32[]{:S(2)}) copy-start(s32[64]{0:T(128)} %cols.1) | copy-start | bytes 772
  77.5 42.8 %copy-start.7 = (f32[64,1024]{1,0:T(8,128)S(1)}, f32[64,1024]{1,0:T(8,128)}, u32[]{:S(2)}) copy-start(f32[64,1024]{1,0:T(8,128)} %param.15) | copy-start | bytes 786436
  83.3 8.6 %collective-permute-start.16 = (f32[32,1024]{1,0:T(8,128)S(1)}, f32[32,1024]{1,0:T(8,128)S(1)}, u32[]{:S(2)}, u32[]{:S(2)}) collective-permute-start(f32[32,1024]{1,0:T(8,128)S(1)} %get-tuple-element.165), channel_id=1, source_target_pairs={{0,8},{8,16},{16,24},{24,32},{32,40},{40,48},{48,56},{56,0},{64,72... | collective-permute-start | bytes 393224 | tf_op jit(solution)/shard_map/ppermute | solution.py:542
  84.2 7.7 %collective-permute-start.17 = (f32[32,1024]{1,0:T(8,128)S(1)}, f32[32,1024]{1,0:T(8,128)S(1)}, u32[]{:S(2)}, u32[]{:S(2)}) collective-permute-start(f32[32,1024]{1,0:T(8,128)S(1)} %get-tuple-element.166), channel_id=1, source_target_pairs={{0,56},{8,0},{16,8},{24,16},{32,24},{40,32},{48,40},{56,48},{64,12... | collective-permute-start | bytes 393224 | tf_op jit(solution)/shard_map/ppermute | solution.py:543
  93.0 7.7 %collective-permute-start.18 = (f32[64,1024]{1,0:T(8,128)S(1)}, f32[64,1024]{1,0:T(8,128)S(1)}, u32[]{:S(2)}, u32[]{:S(2)}) collective-permute-start(f32[64,1024]{1,0:T(8,128)S(1)} %get-tuple-element.169), channel_id=1, source_target_pairs={{0,8},{8,16},{16,24},{24,32},{32,40},{40,48},{48,56},{56,0},{64,72... | collective-permute-start | bytes 786440 | tf_op jit(solution)/shard_map/ppermute | solution.py:542
  93.1 7.7 %collective-permute-start.19 = (f32[64,1024]{1,0:T(8,128)S(1)}, f32[64,1024]{1,0:T(8,128)S(1)}, u32[]{:S(2)}, u32[]{:S(2)}) collective-permute-start(f32[64,1024]{1,0:T(8,128)S(1)} %get-tuple-element.170), channel_id=1, source_target_pairs={{0,56},{8,0},{16,8},{24,16},{32,24},{40,32},{48,40},{56,48},{64,12... | collective-permute-start | bytes 786440 | tf_op jit(solution)/shard_map/ppermute | solution.py:543
  101.9 7.7 %collective-permute-start.20 = (f32[64,1024]{1,0:T(8,128)S(1)}, f32[64,1024]{1,0:T(8,128)S(1)}, u32[]{:S(2)}, u32[]{:S(2)}) collective-permute-start(f32[64,1024]{1,0:T(8,128)S(1)} %get-tuple-element.173), channel_id=1, source_target_pairs={{0,8},{8,16},{16,24},{24,32},{32,40},{40,48},{48,56},{56,0},{64,72... | collective-permute-start | bytes 786440 | tf_op jit(solution)/shard_map/ppermute | solution.py:542
  103.8 6.4 %collective-permute-start.21 = (f32[64,1024]{1,0:T(8,128)S(1)}, f32[64,1024]{1,0:T(8,128)S(1)}, u32[]{:S(2)}, u32[]{:S(2)}) collective-permute-start(f32[64,1024]{1,0:T(8,128)S(1)} %get-tuple-element.174), channel_id=1, source_target_pairs={{0,56},{8,0},{16,8},{24,16},{32,24},{40,32},{48,40},{56,48},{64,12... | collective-permute-start | bytes 786440 | tf_op jit(solution)/shard_map/ppermute | solution.py:543
  111.3 7.7 %collective-permute-start.22 = (f32[64,1024]{1,0:T(8,128)S(1)}, f32[64,1024]{1,0:T(8,128)S(1)}, u32[]{:S(2)}, u32[]{:S(2)}) collective-permute-start(f32[64,1024]{1,0:T(8,128)S(1)} %get-tuple-element.177), channel_id=1, source_target_pairs={{0,8},{8,16},{16,24},{24,32},{32,40},{40,48},{48,56},{56,0},{64,72... | collective-permute-start | bytes 786440 | tf_op jit(solution)/shard_map/ppermute | solution.py:542
  114.0 6.4 %collective-permute-start.23 = (f32[64,1024]{1,0:T(8,128)S(1)}, f32[64,1024]{1,0:T(8,128)S(1)}, u32[]{:S(2)}, u32[]{:S(2)}) collective-permute-start(f32[64,1024]{1,0:T(8,128)S(1)} %get-tuple-element.178), channel_id=1, source_target_pairs={{0,56},{8,0},{16,8},{24,16},{32,24},{40,32},{48,40},{56,48},{64,12... | collective-permute-start | bytes 786440 | tf_op jit(solution)/shard_map/ppermute | solution.py:543
  121.6 0.7 copy-start.8
Sparse Core Ops, SparseCore 0:
  9.3 44.2 all-gather.5

commit v7 on v6

--- a/solution.py
+++ b/solution.py
@@ -9,7 +9,7 @@
 ZS = 8
 YS = 4
 CAP = 32
-TOTAL_CAP = 68
+TOTAL_CAP = 64
 LIST = 72
 GROUP = 8
 EXTRA = 16
@@ -185,7 +185,7 @@
 
 
 def compact_kernel(plan, *refs):
-    sources, (out, moved_plan, entries, sems) = refs[:XS - 1], refs[XS - 1:]
+    sources, (out, moved_plan, mark, entries, sems) = refs[:XS - 1], refs[XS - 1:]
     place, sizes, _ = own_parts(plan)
     totals, table = moved_parts(moved_plan)
     mine = place[0]
@@ -225,7 +225,7 @@
             return 0
 
         lax.fori_loop(0, size, step, 0)
-    totals[2] = over.astype(jnp.int32)
+    mark[...] = jnp.broadcast_to(over.astype(jnp.float32), mark.shape)
     pad_list(table, 0, totals[0], low, low + HERE + EXTRA)
     pad_list(table, LIST, totals[1], low + HERE, low + HERE)
 
@@ -236,10 +236,11 @@
     return pl.pallas_call(
         compact_kernel,
         in_specs=[smem] + [vmem] * (XS - 1),
-        out_specs=[vmem, smem],
+        out_specs=[vmem, smem, vmem],
         out_shape=[
             jax.ShapeDtypeStruct((TOTAL_CAP, PIECE, WIDTH), jnp.float32),
             jax.ShapeDtypeStruct((8 + 3 * MOVED_WIDTH,), jnp.int32),
+            jax.ShapeDtypeStruct((8, WIDTH), jnp.float32),
         ],
         scratch_shapes=[pltpu.SMEM((XS - 1, 8, WIDTH), jnp.float32), pltpu.SemaphoreType.DMA((XS - 1,))],
         compiler_params=pltpu.CompilerParams(vmem_limit_bytes=8 * 2**20),
@@ -562,16 +563,15 @@
     near = lax.all_gather(amplitudes, "tile", axis=0, axis_index_groups=Z_GROUPS)
 
     *packed, plan = pack(place, tile_rows, tile_cols, tile_count, integrals)
-    arrived = [lax.ppermute(packed[step - 1], "tile", x_shift(step)) for step in range(1, XS)]
-    mine, moved_plan = compact(plan, arrived)
+    arrived = [lax.ppermute(packed[step - 1], "tile", x_shift(step)) for step in (2, 1, 3)]
+    mine, moved_plan, marks = compact(plan, arrived)
     along_y = [mine] + [lax.ppermute(mine, "pair", y_shift(step)) for step in range(1, YS)]
     across = lax.ppermute(mine, "pair", CORE_SWAP)
-    marks = moved_plan[2:3].astype(jnp.float32)
     for step in (1, 2, 4):
         marks = jnp.maximum(marks, lax.ppermute(marks, "tile", z_shift(step)))
     split, first = prepare(near)
     extra = lax.ppermute(first, "tile", x_shift(-1))
-    along_y[1], along_y[2], first, marks = lax.optimization_barrier((along_y[1], along_y[2], first, marks))
+    along_y[1], along_y[2], marks = lax.optimization_barrier((along_y[1], along_y[2], marks))
     pieces = [mine, across]
     for piece in along_y[1:]:
         pieces += [piece, lax.ppermute(piece, "pair", CORE_SWAP)]
@@ -597,7 +597,7 @@
         full = dense_ladder(amplitudes, integrals, tile_rows, tile_cols, tile_count)
         return (driver + full) / denominator
 
-    return lax.cond(marks[0] > 0.5, slow, lambda: result)
+    return lax.cond(marks[0, 0] > 0.5, slow, lambda: result)
 
 
 def solution(mesh):

time: 129 us -> 128 us (level)
  the two profiles are of different devices: /device:TPU:6 before, /device:TPU:24 now
where the time goes in v7:
time: 128 us
  waiting for transfers between devices  52.8 us (41%)
  starting transfers between devices  38.2 us (30%)
  between operations  14.9 us (12%)
  Pallas kernels  14.6 us (11%)
  other arithmetic  5.76 us (4%)
  local copies, waits for them, and re-layouts  1.34 us (1%)
    ppermute x3, waiting for transfers between devices, shards(): marks = jnp.maximum(marks, lax.ppermute(marks, 'tile', z_shift(step)))  14.7 us
    ppermute x4, waiting for transfers between devices, ring_sum(): up = lax.ppermute(up, 'tile', z_shift(1))  14.4 us
    ppermute x3, waiting for transfers between devices, shards(): lax.ppermute(packed[step - 1], 'tile', x_shift(step))  9.38 us
    ppermute x4, starting transfers between devices, ring_sum(): down = lax.ppermute(down, 'tile', z_shift(-1))  8.85 us
    ppermute x4, starting transfers between devices, ring_sum(): up = lax.ppermute(up, 'tile', z_shift(1))  7.94 us
    pallas_call x2, Pallas kernels, call(): pl.pallas_call(kernel, in_specs=[smem] * len(scalars) + [anywhere] * len(...  6.64 us
    ppermute x3, starting transfers between devices, shards(): lax.ppermute(packed[step - 1], 'tile', x_shift(step))  6.34 us
    ppermute x3, starting transfers between devices, shards(): marks = jnp.maximum(marks, lax.ppermute(marks, 'tile', z_shift(step)))  6.3 us
  transfers between devices with their start and end apart: 25, of which 15 were waited for; matrix products, arithmetic and copies ran while one was open for 1% of the time, Pallas kernels for 11%

profile of v7, /device:TPU:24, one launch (start us, length us, event | category | flops | bytes accessed | tf_op | source)
XLA Modules:
  0.0 127.6 jit_solution(10955245544751614299)
XLA Ops:
  6.5 0.7 all-gather.6.cloned.1.call-update
  8.0 3.2 %pack.1 = (f32[33,16,128]{2,1,0:T(8,128)S(1)}, f32[33,16,128]{2,1,0:T(8,128)S(1)}, f32[33,16,128]{2,1,0:T(8,128)S(1)}, s32[1104]{0:T(1024)S(1)}) custom-call(s32[3]{0:T(128)S(1)} %pad_add_fusion.here, s32[64]{0:T(128)} %rows.1, s32[64]{0:T(128)} %cols.1, s32[1]{0:T(128)S(6)} %copy.32.count, f32[64,128,128]{2,1,0:T(8,128)} %stored_hbm.3), custom_call_target="tpu_custom_call" | custom-call | tf_op jit(solution)/shard_map/pack/pallas_call | solution.py:171
  11.2 3.1 %collective-permute-start = (f32[33,16,128]{2,1,0:T(8,128)S(1)}, f32[33,16,128]{2,1,0:T(8,128)S(1)}, u32[]{:S(2)}, u32[]{:S(2)}) collective-permute-start(f32[33,16,128]{2,1,0:T(8,128)S(1)} %get-tuple-element.153), channel_id=1, source_target_pairs={{0,128},{8,136},{16,144},{24,152},{32,160},{40,168},{48,176},{56,1... | collective-permute-start | bytes 811016 | tf_op jit(solution)/shard_map/ppermute | solution.py:566
  14.3 0.6 collective-permute-start.1
  14.9 2.6 %collective-permute-start.2 = (f32[33,16,128]{2,1,0:T(8,128)S(1)}, f32[33,16,128]{2,1,0:T(8,128)S(1)}, u32[]{:S(2)}, u32[]{:S(2)}) collective-permute-start(f32[33,16,128]{2,1,0:T(8,128)S(1)} %get-tuple-element.155), channel_id=1, source_target_pairs={{0,192},{8,200},{16,208},{24,216},{32,224},{40,232},{48,240},{56,2... | collective-permute-start | bytes 811016 | tf_op jit(solution)/shard_map/ppermute | solution.py:566
  17.6 4.7 %collective-permute-done.refs_0_ = f32[33,16,128]{2,1,0:T(8,128)S(1)} collective-permute-done((f32[33,16,128]{2,1,0:T(8,128)S(1)}, f32[33,16,128]{2,1,0:T(8,128)S(1)}, u32[]{:S(2)}, u32[]{:S(2)}) %collective-permute-start) | collective-permute-done | bytes 270368 | tf_op jit(solution)/shard_map/ppermute | solution.py:566
  22.2 4.6 %collective-permute-done.1.refs_1_ = f32[33,16,128]{2,1,0:T(8,128)S(1)} collective-permute-done((f32[33,16,128]{2,1,0:T(8,128)S(1)}, f32[33,16,128]{2,1,0:T(8,128)S(1)}, u32[]{:S(2)}, u32[]{:S(2)}) %collective-permute-start.1) | collective-permute-done | bytes 270368 | tf_op jit(solution)/shard_map/ppermute | solution.py:566
  26.8 0.1 collective-permute-done.2.refs_2_
  27.0 2.2 %compact.1 = (f32[64,16,128]{2,1,0:T(8,128)S(1)}, s32[440]{0:T(512)S(1)}, f32[8,128]{1,0:T(8,128)S(1)}) custom-call(s32[1104]{0:T(1024)S(1)} %get-tuple-element.152.plan, f32[33,16,128]{2,1,0:T(8,128)S(1)} %collective-permute-done.refs_0_, f32[33,16,128]{2,1,0:T(8,128)S(1)} %collective-permute-done.1.refs_1_, f32[33,16,128]{2,1,0:T(8,128)S(1)} %collective-permute-done.2.refs_2_), custom_call_target="tpu_custom_call" | custom-call | tf_op jit(solution)/shard_map/compact/pallas_call | solution.py:236
  29.2 1.3 %collective-permute-start.4 = (f32[64,16,128]{2,1,0:T(8,128)S(1)}, f32[64,16,128]{2,1,0:T(8,128)S(1)}, u32[]{:S(2)}, u32[]{:S(2)}) collective-permute-start(f32[64,16,128]{2,1,0:T(8,128)S(1)} %get-tuple-element.156.refs_0_), channel_id=1, source_target_pairs={{0,4},{1,5},{2,6},{3,7},{4,0},{5,1},{6,2},{7,3},{8,12},{9,13},{10,... | collective-permute-start | bytes 1572872 | tf_op jit(solution)/shard_map/ppermute | solution.py:568
  30.5 2.2 %collective-permute-start.3 = (f32[64,16,128]{2,1,0:T(8,128)S(1)}, f32[64,16,128]{2,1,0:T(8,128)S(1)}, u32[]{:S(2)}, u32[]{:S(2)}) collective-permute-start(f32[64,16,128]{2,1,0:T(8,128)S(1)} %get-tuple-element.156.refs_0_), channel_id=1, source_target_pairs={{0,2},{1,3},{2,4},{3,5},{4,6},{5,7},{6,0},{7,1},{8,10},{9,11},{10,... | collective-permute-start | bytes 1572872 | tf_op jit(solution)/shard_map/ppermute | solution.py:568
  32.7 1.9 %collective-permute-start.5 = (f32[8,128]{1,0:T(8,128)S(1)}, f32[8,128]{1,0:T(8,128)S(1)}, u32[]{:S(2)}, u32[]{:S(2)}) collective-permute-start(f32[8,128]{1,0:T(8,128)S(1)} %get-tuple-element.157), channel_id=1, source_target_pairs={{0,8},{8,16},{16,24},{24,32},{32,40},{40,48},{48,56},{56,0},{64,72... | collective-permute-start | bytes 12296 | tf_op jit(solution)/shard_map/ppermute | solution.py:571
  34.6 5.8 %collective-permute-done.5 = f32[8,128]{1,0:T(8,128)S(1)} collective-permute-done((f32[8,128]{1,0:T(8,128)S(1)}, f32[8,128]{1,0:T(8,128)S(1)}, u32[]{:S(2)}, u32[]{:S(2)}) %collective-permute-start.5) | collective-permute-done | bytes 4128 | tf_op jit(solution)/shard_map/ppermute | solution.py:571
  40.5 5.7 %collective-permute-done.6 = f32[8,128]{1,0:T(8,128)S(1)} collective-permute-done((f32[8,128]{1,0:T(8,128)S(1)}, f32[8,128]{1,0:T(8,128)S(1)}, u32[]{:S(2)}, u32[]{:S(2)}) %collective-permute-start.6) | collective-permute-done | bytes 4128 | tf_op jit(solution)/shard_map/ppermute | solution.py:571
  46.2 4.4 %collective-permute-start.7 = (f32[8,128]{1,0:T(8,128)S(1)}, f32[8,128]{1,0:T(8,128)S(1)}, u32[]{:S(2)}, u32[]{:S(2)}) collective-permute-start(f32[8,128]{1,0:T(8,128)S(1)} %max.10), channel_id=1, source_target_pairs={{0,32},{8,40},{16,48},{24,56},{32,0},{40,8},{48,16},{56,24},{64,96... | collective-permute-start | bytes 12296 | tf_op jit(solution)/shard_map/ppermute | solution.py:571
  50.6 3.1 %collective-permute-done.7 = f32[8,128]{1,0:T(8,128)S(1)} collective-permute-done((f32[8,128]{1,0:T(8,128)S(1)}, f32[8,128]{1,0:T(8,128)S(1)}, u32[]{:S(2)}, u32[]{:S(2)}) %collective-permute-start.7) | collective-permute-done | bytes 4128 | tf_op jit(solution)/shard_map/ppermute | solution.py:571
  53.7 0.1 collective-permute-start.9
  53.8 2.0 %collective-permute-done.11.refs_6_ = f32[64,16,128]{2,1,0:T(8,128)} collective-permute-done((f32[64,16,128]{2,1,0:T(8,128)S(1)}, f32[64,16,128]{2,1,0:T(8,128)}, u32[]{:S(2)}, u32[]{:S(2)}) %collective-permute-start.11) | collective-permute-done | bytes 524320 | tf_op jit(solution)/shard_map/ppermute | solution.py:568
  55.9 0.5 collective-permute-start.10
  56.4 2.5 %prepare.1 = (bf16[64,64,256]{2,1,0:T(8,128)(2,1)}, f32[2,64,1024]{2,1,0:T(8,128)S(1)}) custom-call(f32[8,64,1024]{2,1,0:T(8,128)} %bitcast.79), custom_call_target="tpu_custom_call" | custom-call | tf_op jit(solution)/shard_map/prepare/pallas_call | solution.py:333
  58.9 3.1 %collective-permute-start.13 = (f32[2,64,1024]{2,1,0:T(8,128)S(1)}, f32[2,64,1024]{2,1,0:T(8,128)S(1)}, u32[]{:S(2)}, u32[]{:S(2)}) collective-permute-start(f32[2,64,1024]{2,1,0:T(8,128)S(1)} %get-tuple-element.164), channel_id=1, source_target_pairs={{0,192},{8,200},{16,208},{24,216},{32,224},{40,232},{48,240},{56,2... | collective-permute-start | bytes 1572872 | tf_op jit(solution)/shard_map/ppermute | solution.py:573
  62.0 5.7 %main.1 = (f32[8,64,1024]{2,1,0:T(8,128)}, f32[64,1024]{1,0:T(8,128)S(1)}, f32[64,1024]{1,0:T(8,128)S(1)}) custom-call(s32[1104]{0:T(1024)S(1)} %get-tuple-element.152.plan, s32[440]{0:T(512)S(1)} %get-tuple-element.159.moved_plan, bf16[64,64,256]{2,1,0:T(8,128)(2,1)} %get-tuple-element.160.split_hbm, f32[64,128,128]{2,1,0:T(8,128)} %stored_hbm.3, ...), custom_call_target="tpu_custom_call" | custom-call | flops 1000000 | bytes 10000 | tf_op jit(solution)/shard_map/main/pallas_call | solution.py:493
  67.8 1.5 %collective-permute-start.15 = (f32[64,1024]{1,0:T(8,128)S(1)}, f32[64,1024]{1,0:T(8,128)S(1)}, u32[]{:S(2)}, u32[]{:S(2)}) collective-permute-start(f32[64,1024]{1,0:T(8,128)S(1)} %get-tuple-element.166), channel_id=1, source_target_pairs={{0,64},{8,72},{16,80},{24,88},{32,96},{40,104},{48,112},{56,120},{... | collective-permute-start | bytes 786440 | tf_op jit(solution)/shard_map/ppermute | solution.py:581
  69.3 4.0 %collective-permute-done.13.extra_hbm = f32[2,64,1024]{2,1,0:T(8,128)S(1)} collective-permute-done((f32[2,64,1024]{2,1,0:T(8,128)S(1)}, f32[2,64,1024]{2,1,0:T(8,128)S(1)}, u32[]{:S(2)}, u32[]{:S(2)}) %collective-permute-start.13) | collective-permute-done | bytes 524320 | tf_op jit(solution)/shard_map/ppermute | solution.py:573
  73.3 1.0 late.1
  74.3 3.9 %collective-permute-done.14 = f32[64,1024]{1,0:T(8,128)S(1)} collective-permute-done((f32[64,1024]{1,0:T(8,128)S(1)}, f32[64,1024]{1,0:T(8,128)S(1)}, u32[]{:S(2)}, u32[]{:S(2)}) %collective-permute-start.14) | collective-permute-done | bytes 262176 | tf_op jit(solution)/shard_map/ppermute | solution.py:580
  78.2 1.0 fusion.26
  79.2 2.3 %collective-permute-start.16 = (f32[32,1024]{1,0:T(8,128)S(1)}, f32[32,1024]{1,0:T(8,128)S(1)}, u32[]{:S(2)}, u32[]{:S(2)}) collective-permute-start(f32[32,1024]{1,0:T(8,128)S(1)} %get-tuple-element.167), channel_id=1, source_target_pairs={{0,8},{8,16},{16,24},{24,32},{32,40},{40,48},{48,56},{56,0},{64,72... | collective-permute-start | bytes 393224 | tf_op jit(solution)/shard_map/ppermute | solution.py:543
  81.5 4.2 %collective-permute-start.17 = (f32[32,1024]{1,0:T(8,128)S(1)}, f32[32,1024]{1,0:T(8,128)S(1)}, u32[]{:S(2)}, u32[]{:S(2)}) collective-permute-start(f32[32,1024]{1,0:T(8,128)S(1)} %get-tuple-element.168), channel_id=1, source_target_pairs={{0,56},{8,0},{16,8},{24,16},{32,24},{40,32},{48,40},{56,48},{64,12... | collective-permute-start | bytes 393224 | tf_op jit(solution)/shard_map/ppermute | solution.py:544
  85.7 2.9 %collective-permute-done.16 = f32[32,1024]{1,0:T(8,128)S(1)} collective-permute-done((f32[32,1024]{1,0:T(8,128)S(1)}, f32[32,1024]{1,0:T(8,128)S(1)}, u32[]{:S(2)}, u32[]{:S(2)}) %collective-permute-start.16) | collective-permute-done | bytes 131104 | tf_op jit(solution)/shard_map/ppermute | solution.py:543
  88.6 1.1 fusion.23
  89.7 0.1 collective-permute-start.18
  89.8 3.4 %collective-permute-start.19 = (f32[64,1024]{1,0:T(8,128)S(1)}, f32[64,1024]{1,0:T(8,128)S(1)}, u32[]{:S(2)}, u32[]{:S(2)}) collective-permute-start(f32[64,1024]{1,0:T(8,128)S(1)} %get-tuple-element.172), channel_id=1, source_target_pairs={{0,56},{8,0},{16,8},{24,16},{32,24},{40,32},{48,40},{56,48},{64,12... | collective-permute-start | bytes 786440 | tf_op jit(solution)/shard_map/ppermute | solution.py:544
  93.2 4.3 %collective-permute-done.18 = f32[64,1024]{1,0:T(8,128)S(1)} collective-permute-done((f32[64,1024]{1,0:T(8,128)S(1)}, f32[64,1024]{1,0:T(8,128)S(1)}, u32[]{:S(2)}, u32[]{:S(2)}) %collective-permute-start.18) | collective-permute-done | bytes 262176 | tf_op jit(solution)/shard_map/ppermute | solution.py:543
  97.4 1.2 fusion.19
  98.6 2.9 %collective-permute-start.20 = (f32[64,1024]{1,0:T(8,128)S(1)}, f32[64,1024]{1,0:T(8,128)S(1)}, u32[]{:S(2)}, u32[]{:S(2)}) collective-permute-start(f32[64,1024]{1,0:T(8,128)S(1)} %get-tuple-element.175), channel_id=1, source_target_pairs={{0,8},{8,16},{16,24},{24,32},{32,40},{40,48},{48,56},{56,0},{64,72... | collective-permute-start | bytes 786440 | tf_op jit(solution)/shard_map/ppermute | solution.py:543
  101.5 0.6 collective-permute-start.21
  102.1 4.3 %collective-permute-done.20 = f32[64,1024]{1,0:T(8,128)S(1)} collective-permute-done((f32[64,1024]{1,0:T(8,128)S(1)}, f32[64,1024]{1,0:T(8,128)S(1)}, u32[]{:S(2)}, u32[]{:S(2)}) %collective-permute-start.20) | collective-permute-done | bytes 262176 | tf_op jit(solution)/shard_map/ppermute | solution.py:543
  106.4 2.3 %collective-permute-done.21 = f32[64,1024]{1,0:T(8,128)S(1)} collective-permute-done((f32[64,1024]{1,0:T(8,128)S(1)}, f32[64,1024]{1,0:T(8,128)S(1)}, u32[]{:S(2)}, u32[]{:S(2)}) %collective-permute-start.21) | collective-permute-done | bytes 262176 | tf_op jit(solution)/shard_map/ppermute | solution.py:544
  108.7 1.2 fusion.15
  109.8 2.6 %collective-permute-start.22 = (f32[64,1024]{1,0:T(8,128)S(1)}, f32[64,1024]{1,0:T(8,128)S(1)}, u32[]{:S(2)}, u32[]{:S(2)}) collective-permute-start(f32[64,1024]{1,0:T(8,128)S(1)} %get-tuple-element.179), channel_id=1, source_target_pairs={{0,8},{8,16},{16,24},{24,32},{32,40},{40,48},{48,56},{56,0},{64,72... | collective-permute-start | bytes 786440 | tf_op jit(solution)/shard_map/ppermute | solution.py:543
  112.5 0.7 collective-permute-start.23
  113.2 0.6 slice.34
  114.4 3.0 %collective-permute-done.22 = f32[64,1024]{1,0:T(8,128)S(1)} collective-permute-done((f32[64,1024]{1,0:T(8,128)S(1)}, f32[64,1024]{1,0:T(8,128)S(1)}, u32[]{:S(2)}, u32[]{:S(2)}) %collective-permute-start.22) | collective-permute-done | bytes 262176 | tf_op jit(solution)/shard_map/ppermute | solution.py:543
  117.5 1.3 %collective-permute-done.23 = f32[64,1024]{1,0:T(8,128)S(1)} collective-permute-done((f32[64,1024]{1,0:T(8,128)S(1)}, f32[64,1024]{1,0:T(8,128)S(1)}, u32[]{:S(2)}, u32[]{:S(2)}) %collective-permute-start.23) | collective-permute-done | bytes 262176 | tf_op jit(solution)/shard_map/ppermute | solution.py:544
  118.9 1.2 conditional.1
  118.9 1.1 fusion.3
  120.1 0.7 copy-done.6
  (40 shorter events, 0.4 us)
Async XLA Ops:
  6.5 49.8 %all-gather.6.cloned.1.call-start = ((), (), s32[]{:S(2)}) async-start(), calls=%async_computation.3 | async-start | bytes 2359296 | tf_op jit(solution)/shard_map/all_gather | solution.py:563
  11.2 11.0 %collective-permute-start = (f32[33,16,128]{2,1,0:T(8,128)S(1)}, f32[33,16,128]{2,1,0:T(8,128)S(1)}, u32[]{:S(2)}, u32[]{:S(2)}) collective-permute-start(f32[33,16,128]{2,1,0:T(8,128)S(1)} %get-tuple-element.153), channel_id=1, source_target_pairs={{0,128},{8,136},{16,144},{24,152},{32,160},{40,168},{48,176},{56,1... | collective-permute-start | bytes 811016 | tf_op jit(solution)/shard_map/ppermute | solution.py:566
  14.3 12.5 %collective-permute-start.1 = (f32[33,16,128]{2,1,0:T(8,128)S(1)}, f32[33,16,128]{2,1,0:T(8,128)S(1)}, u32[]{:S(2)}, u32[]{:S(2)}) collective-permute-start(f32[33,16,128]{2,1,0:T(8,128)S(1)} %get-tuple-element.154), channel_id=1, source_target_pairs={{0,64},{8,72},{16,80},{24,88},{32,96},{40,104},{48,112},{56,120},{... | collective-permute-start | bytes 811016 | tf_op jit(solution)/shard_map/ppermute | solution.py:566
  14.9 12.0 %collective-permute-start.2 = (f32[33,16,128]{2,1,0:T(8,128)S(1)}, f32[33,16,128]{2,1,0:T(8,128)S(1)}, u32[]{:S(2)}, u32[]{:S(2)}) collective-permute-start(f32[33,16,128]{2,1,0:T(8,128)S(1)} %get-tuple-element.155), channel_id=1, source_target_pairs={{0,192},{8,200},{16,208},{24,216},{32,224},{40,232},{48,240},{56,2... | collective-permute-start | bytes 811016 | tf_op jit(solution)/shard_map/ppermute | solution.py:566
  29.2 32.8 %copy-start = (f32[64,16,128]{2,1,0:T(8,128)}, f32[64,16,128]{2,1,0:T(8,128)S(1)}, u32[]{:S(2)}) copy-start(f32[64,16,128]{2,1,0:T(8,128)S(1)} %get-tuple-element.156.refs_0_) | copy-start | bytes 1572868
  29.2 24.5 %collective-permute-start.4 = (f32[64,16,128]{2,1,0:T(8,128)S(1)}, f32[64,16,128]{2,1,0:T(8,128)S(1)}, u32[]{:S(2)}, u32[]{:S(2)}) collective-permute-start(f32[64,16,128]{2,1,0:T(8,128)S(1)} %get-tuple-element.156.refs_0_), channel_id=1, source_target_pairs={{0,4},{1,5},{2,6},{3,7},{4,0},{5,1},{6,2},{7,3},{8,12},{9,13},{10,... | collective-permute-start | bytes 1572872 | tf_op jit(solution)/shard_map/ppermute | solution.py:568
  30.5 23.2 %collective-permute-start.3 = (f32[64,16,128]{2,1,0:T(8,128)S(1)}, f32[64,16,128]{2,1,0:T(8,128)S(1)}, u32[]{:S(2)}, u32[]{:S(2)}) collective-permute-start(f32[64,16,128]{2,1,0:T(8,128)S(1)} %get-tuple-element.156.refs_0_), channel_id=1, source_target_pairs={{0,2},{1,3},{2,4},{3,5},{4,6},{5,7},{6,0},{7,1},{8,10},{9,11},{10,... | collective-permute-start | bytes 1572872 | tf_op jit(solution)/shard_map/ppermute | solution.py:568
  32.7 23.2 %collective-permute-start.11 = (f32[64,16,128]{2,1,0:T(8,128)S(1)}, f32[64,16,128]{2,1,0:T(8,128)}, u32[]{:S(2)}, u32[]{:S(2)}) collective-permute-start(f32[64,16,128]{2,1,0:T(8,128)S(1)} %get-tuple-element.156.refs_0_), channel_id=1, source_target_pairs={{0,6},{1,7},{2,0},{3,1},{4,2},{5,3},{6,4},{7,5},{8,14},{9,15},{10,... | collective-permute-start | bytes 1572872 | tf_op jit(solution)/shard_map/ppermute | solution.py:568
  32.7 7.8 %collective-permute-start.5 = (f32[8,128]{1,0:T(8,128)S(1)}, f32[8,128]{1,0:T(8,128)S(1)}, u32[]{:S(2)}, u32[]{:S(2)}) collective-permute-start(f32[8,128]{1,0:T(8,128)S(1)} %get-tuple-element.157), channel_id=1, source_target_pairs={{0,8},{8,16},{16,24},{24,32},{32,40},{40,48},{48,56},{56,0},{64,72... | collective-permute-start | bytes 12296 | tf_op jit(solution)/shard_map/ppermute | solution.py:571
  40.5 5.7 %collective-permute-start.6 = (f32[8,128]{1,0:T(8,128)S(1)}, f32[8,128]{1,0:T(8,128)S(1)}, u32[]{:S(2)}, u32[]{:S(2)}) collective-permute-start(f32[8,128]{1,0:T(8,128)S(1)} %max.9), channel_id=1, source_target_pairs={{0,16},{8,24},{16,32},{24,40},{32,48},{40,56},{48,0},{56,8},{64,80... | collective-permute-start | bytes 12296 | tf_op jit(solution)/shard_map/ppermute | solution.py:571
  46.2 7.5 %collective-permute-start.7 = (f32[8,128]{1,0:T(8,128)S(1)}, f32[8,128]{1,0:T(8,128)S(1)}, u32[]{:S(2)}, u32[]{:S(2)}) collective-permute-start(f32[8,128]{1,0:T(8,128)S(1)} %max.10), channel_id=1, source_target_pairs={{0,32},{8,40},{16,48},{24,56},{32,0},{40,8},{48,16},{56,24},{64,96... | collective-permute-start | bytes 12296 | tf_op jit(solution)/shard_map/ppermute | solution.py:571
  50.6 11.4 %collective-permute-start.8 = (f32[64,16,128]{2,1,0:T(8,128)S(1)}, f32[64,16,128]{2,1,0:T(8,128)}, u32[]{:S(2)}, u32[]{:S(2)}) collective-permute-start(f32[64,16,128]{2,1,0:T(8,128)S(1)} %get-tuple-element.156.refs_0_), channel_id=1, source_target_pairs={{0,1},{1,0},{2,3},{3,2},{4,5},{5,4},{6,7},{7,6},{8,9},{9,8},{10,11... | collective-permute-start | bytes 1572872 | tf_op jit(solution)/shard_map/ppermute | solution.py:569
  53.7 8.2 %copy-start.3 = (f32[64,16,128]{2,1,0:T(8,128)}, f32[64,16,128]{2,1,0:T(8,128)S(1)}, u32[]{:S(2)}) copy-start(f32[64,16,128]{2,1,0:T(8,128)S(1)} %collective-permute-done.4.refs_4_) | copy-start | bytes 1572868
  53.7 8.2 %copy-start.4 = (f32[64,16,128]{2,1,0:T(8,128)}, f32[64,16,128]{2,1,0:T(8,128)S(1)}, u32[]{:S(2)}) copy-start(f32[64,16,128]{2,1,0:T(8,128)S(1)} %collective-permute-done.3.refs_2_) | copy-start | bytes 1572868
  53.7 8.2 %collective-permute-start.9 = (f32[64,16,128]{2,1,0:T(8,128)S(1)}, f32[64,16,128]{2,1,0:T(8,128)}, u32[]{:S(2)}, u32[]{:S(2)}) collective-permute-start(f32[64,16,128]{2,1,0:T(8,128)S(1)} %collective-permute-done.3.refs_2_), channel_id=1, source_target_pairs={{0,1},{1,0},{2,3},{3,2},{4,5},{5,4},{6,7},{7,6},{8,9},{9,8},{10,11... | collective-permute-start | bytes 1572872 | tf_op jit(solution)/shard_map/ppermute | solution.py:577
  55.8 6.1 %collective-permute-start.12 = (f32[64,16,128]{2,1,0:T(8,128)}, f32[64,16,128]{2,1,0:T(8,128)}, u32[]{:S(2)}, u32[]{:S(2)}) collective-permute-start(f32[64,16,128]{2,1,0:T(8,128)} %collective-permute-done.11.refs_6_), channel_id=1, source_target_pairs={{0,1},{1,0},{2,3},{3,2},{4,5},{5,4},{6,7},{7,6},{8,9},{9,8},{10,11... | collective-permute-start | bytes 1572872 | tf_op jit(solution)/shard_map/ppermute | solution.py:577
  55.9 6.1 %collective-permute-start.10 = (f32[64,16,128]{2,1,0:T(8,128)S(1)}, f32[64,16,128]{2,1,0:T(8,128)}, u32[]{:S(2)}, u32[]{:S(2)}) collective-permute-start(f32[64,16,128]{2,1,0:T(8,128)S(1)} %collective-permute-done.4.refs_4_), channel_id=1, source_target_pairs={{0,1},{1,0},{2,3},{3,2},{4,5},{5,4},{6,7},{7,6},{8,9},{9,8},{10,11... | collective-permute-start | bytes 1572872 | tf_op jit(solution)/shard_map/ppermute | solution.py:577
  58.9 14.4 %collective-permute-start.13 = (f32[2,64,1024]{2,1,0:T(8,128)S(1)}, f32[2,64,1024]{2,1,0:T(8,128)S(1)}, u32[]{:S(2)}, u32[]{:S(2)}) collective-permute-start(f32[2,64,1024]{2,1,0:T(8,128)S(1)} %get-tuple-element.164), channel_id=1, source_target_pairs={{0,192},{8,200},{16,208},{24,216},{32,224},{40,232},{48,240},{56,2... | collective-permute-start | bytes 1572872 | tf_op jit(solution)/shard_map/ppermute | solution.py:573
  67.7 10.5 %collective-permute-start.14 = (f32[64,1024]{1,0:T(8,128)S(1)}, f32[64,1024]{1,0:T(8,128)S(1)}, u32[]{:S(2)}, u32[]{:S(2)}) collective-permute-start(f32[64,1024]{1,0:T(8,128)S(1)} %get-tuple-element.165), channel_id=1, source_target_pairs={{0,64},{8,72},{16,80},{24,88},{32,96},{40,104},{48,112},{56,120},{... | collective-permute-start | bytes 786440 | tf_op jit(solution)/shard_map/ppermute | solution.py:580
  67.8 20.8 %collective-permute-start.15 = (f32[64,1024]{1,0:T(8,128)S(1)}, f32[64,1024]{1,0:T(8,128)S(1)}, u32[]{:S(2)}, u32[]{:S(2)}) collective-permute-start(f32[64,1024]{1,0:T(8,128)S(1)} %get-tuple-element.166), channel_id=1, source_target_pairs={{0,64},{8,72},{16,80},{24,88},{32,96},{40,104},{48,112},{56,120},{... | collective-permute-start | bytes 786440 | tf_op jit(solution)/shard_map/ppermute | solution.py:581
  73.3 39.9 %copy-start.7 = (f32[1024]{0:T(1024)S(1)}, f32[1024]{0:T(1024)}, u32[]{:S(2)}) copy-start(f32[1024]{0:T(1024)} %param.21) | copy-start | bytes 12292
  73.3 39.9 %copy-start.8 = (f32[64]{0:T(128)S(1)}, f32[64]{0:T(128)}, u32[]{:S(2)}) copy-start(f32[64]{0:T(128)} %param.20) | copy-start | bytes 772
  73.3 45.6 %copy-start.1 = (s32[64]{0:T(128)S(1)}, s32[64]{0:T(128)}, u32[]{:S(2)}) copy-start(s32[64]{0:T(128)} %rows.1) | copy-start | bytes 772
  73.3 45.6 %copy-start.2 = (s32[64]{0:T(128)S(1)}, s32[64]{0:T(128)}, u32[]{:S(2)}) copy-start(s32[64]{0:T(128)} %cols.1) | copy-start | bytes 772
  73.3 45.6 %copy-start.5 = (f32[64,1024]{1,0:T(8,128)S(1)}, f32[64,1024]{1,0:T(8,128)}, u32[]{:S(2)}) copy-start(f32[64,1024]{1,0:T(8,128)} %param.15) | copy-start | bytes 786436
  79.2 9.4 %collective-permute-start.16 = (f32[32,1024]{1,0:T(8,128)S(1)}, f32[32,1024]{1,0:T(8,128)S(1)}, u32[]{:S(2)}, u32[]{:S(2)}) collective-permute-start(f32[32,1024]{1,0:T(8,128)S(1)} %get-tuple-element.167), channel_id=1, source_target_pairs={{0,8},{8,16},{16,24},{24,32},{32,40},{40,48},{48,56},{56,0},{64,72... | collective-permute-start | bytes 393224 | tf_op jit(solution)/shard_map/ppermute | solution.py:543
  81.5 7.1 %collective-permute-start.17 = (f32[32,1024]{1,0:T(8,128)S(1)}, f32[32,1024]{1,0:T(8,128)S(1)}, u32[]{:S(2)}, u32[]{:S(2)}) collective-permute-start(f32[32,1024]{1,0:T(8,128)S(1)} %get-tuple-element.168), channel_id=1, source_target_pairs={{0,56},{8,0},{16,8},{24,16},{32,24},{40,32},{48,40},{56,48},{64,12... | collective-permute-start | bytes 393224 | tf_op jit(solution)/shard_map/ppermute | solution.py:544
  89.7 7.7 %collective-permute-start.18 = (f32[64,1024]{1,0:T(8,128)S(1)}, f32[64,1024]{1,0:T(8,128)S(1)}, u32[]{:S(2)}, u32[]{:S(2)}) collective-permute-start(f32[64,1024]{1,0:T(8,128)S(1)} %get-tuple-element.171), channel_id=1, source_target_pairs={{0,8},{8,16},{16,24},{24,32},{32,40},{40,48},{48,56},{56,0},{64,72... | collective-permute-start | bytes 786440 | tf_op jit(solution)/shard_map/ppermute | solution.py:543
  89.8 7.7 %collective-permute-start.19 = (f32[64,1024]{1,0:T(8,128)S(1)}, f32[64,1024]{1,0:T(8,128)S(1)}, u32[]{:S(2)}, u32[]{:S(2)}) collective-permute-start(f32[64,1024]{1,0:T(8,128)S(1)} %get-tuple-element.172), channel_id=1, source_target_pairs={{0,56},{8,0},{16,8},{24,16},{32,24},{40,32},{48,40},{56,48},{64,12... | collective-permute-start | bytes 786440 | tf_op jit(solution)/shard_map/ppermute | solution.py:544
  98.6 7.7 %collective-permute-start.20 = (f32[64,1024]{1,0:T(8,128)S(1)}, f32[64,1024]{1,0:T(8,128)S(1)}, u32[]{:S(2)}, u32[]{:S(2)}) collective-permute-start(f32[64,1024]{1,0:T(8,128)S(1)} %get-tuple-element.175), channel_id=1, source_target_pairs={{0,8},{8,16},{16,24},{24,32},{32,40},{40,48},{48,56},{56,0},{64,72... | collective-permute-start | bytes 786440 | tf_op jit(solution)/shard_map/ppermute | solution.py:543
  101.5 7.1 %collective-permute-start.21 = (f32[64,1024]{1,0:T(8,128)S(1)}, f32[64,1024]{1,0:T(8,128)S(1)}, u32[]{:S(2)}, u32[]{:S(2)}) collective-permute-start(f32[64,1024]{1,0:T(8,128)S(1)} %get-tuple-element.176), channel_id=1, source_target_pairs={{0,56},{8,0},{16,8},{24,16},{32,24},{40,32},{48,40},{56,48},{64,12... | collective-permute-start | bytes 786440 | tf_op jit(solution)/shard_map/ppermute | solution.py:544
  109.8 7.7 %collective-permute-start.22 = (f32[64,1024]{1,0:T(8,128)S(1)}, f32[64,1024]{1,0:T(8,128)S(1)}, u32[]{:S(2)}, u32[]{:S(2)}) collective-permute-start(f32[64,1024]{1,0:T(8,128)S(1)} %get-tuple-element.179), channel_id=1, source_target_pairs={{0,8},{8,16},{16,24},{24,32},{32,40},{40,48},{48,56},{56,0},{64,72... | collective-permute-start | bytes 786440 | tf_op jit(solution)/shard_map/ppermute | solution.py:543
  112.5 6.4 %collective-permute-start.23 = (f32[64,1024]{1,0:T(8,128)S(1)}, f32[64,1024]{1,0:T(8,128)S(1)}, u32[]{:S(2)}, u32[]{:S(2)}) collective-permute-start(f32[64,1024]{1,0:T(8,128)S(1)} %get-tuple-element.180), channel_id=1, source_target_pairs={{0,56},{8,0},{16,8},{24,16},{32,24},{40,32},{48,40},{56,48},{64,12... | collective-permute-start | bytes 786440 | tf_op jit(solution)/shard_map/ppermute | solution.py:544
  120.1 0.7 copy-start.6
Sparse Core Ops, SparseCore 0:
  9.3 44.1 all-gather.5
